TPU v7x, 128 devices: a whole 4x4x4 slice. The times are simulated.
128 devices in a mesh: zt: 8 (over z_lo, x), xy: 16 (over z_hi, y, core).
Axes of the slice: x: 4, y: 4, z: 4 (z_hi: 2, z_lo: 2; z = z_hi * 2 + z_lo), core: 2. Of those that a mesh axis runs over, the one named last changes fastest.
Arguments:
- restricted: bfloat16 [8, 16, 64, 8, 256], P('zt', 'xy'), may hold values from -6 to 6
- stencil: bfloat16 [8, 16, 9, 64, 64, 256], P('zt', 'xy'), may hold values from -2 to 12, as said below
Outputs:
- smoothed: float32 [8, 16, 64, 8, 256], P('zt', 'xy')
Inputs may be any that keep to these rules, and one draw needn't show every extreme that they name: `stencil`: entries of row i of every block at a site share a positive scale of that site and row; the self block's diagonal entries are at least 0.5.
All inputs are finite; a program needn't handle non-finite values.
Results may differ from a plain program's by a relative error of at most 0.0049.
Values may be sent and summed in bfloat16 or wider, within the bound.
No kernel may reach another device: no remote copies, remote signals or barrier semaphores. Data moves between devices by JAX's collectives and lax.ppermute only.
A program may use at most 128 MiB of HBM per device.

v0:
```python
import jax
import jax.numpy as jnp
from jax import lax
from jax.sharding import PartitionSpec as P

LX = 16
LY = 16
SWEEPS = 4


def with_halo(cells, sides, width):
    for axis, dim in sides:
        count = lax.axis_size(axis)
        head = lax.slice_in_dim(cells, 0, width, axis=dim)
        tail = lax.slice_in_dim(cells, cells.shape[dim] - width, cells.shape[dim], axis=dim)
        cells = jnp.concatenate(
            [
                lax.ppermute(tail, axis, [(i, (i + 1) % count) for i in range(count)]),
                cells,
                lax.ppermute(head, axis, [((i + 1) % count, i) for i in range(count)]),
            ],
            axis=dim,
        )
    return cells


def partner(shard, axis, apart):
    return lax.ppermute(shard, axis, [(i, i ^ 1 << apart) for i in range(lax.axis_size(axis))])


def apply_local(rounded, site_blocks):
    padded = with_halo(rounded[None, None], (("zt", 0), ("xy", 1)), 1)
    plane_above = padded[1, 2]
    plane_below = padded[1, 0]
    time_after = padded[2, 1]
    time_before = padded[0, 1]
    components, vectors = (rounded.shape[0], rounded.shape[1])
    planar = rounded.reshape(components, vectors, LY, LX)
    flat_shape = (components, vectors, LY * LX)
    neighbours = jnp.stack(
        [
            rounded,
            jnp.roll(planar, -1, 3).reshape(flat_shape),
            jnp.roll(planar, 1, 3).reshape(flat_shape),
            jnp.roll(planar, -1, 2).reshape(flat_shape),
            jnp.roll(planar, 1, 2).reshape(flat_shape),
            plane_above,
            plane_below,
            time_after,
            time_before,
        ],
        axis=0,
    )
    site_vectors = neighbours.transpose(3, 2, 0, 1).reshape(LY * LX, vectors, 9 * components)
    product = lax.dot_general(
        site_blocks, site_vectors, (((2,), (2,)), ((0,), (0,))), preferred_element_type=jnp.float32
    )
    return product.transpose(1, 2, 0)


def shards(restricted, stencil):
    xy_count = lax.axis_size("xy")
    column_parts = xy_count // 4
    half_planes = xy_count // 2
    row_width = LX // column_parts
    row_count = LY // 4
    components, vectors = (restricted.shape[2], restricted.shape[3])
    parity = lax.axis_index("zt") % 2
    pieces = restricted[0, 0].reshape(components, vectors, 2, half_planes, row_count, row_width)
    kept_slice = lax.dynamic_index_in_dim(pieces, parity, 2, keepdims=False)
    outgoing = lax.dynamic_index_in_dim(pieces, 1 - parity, 2, keepdims=False)
    incoming = partner(outgoing, "zt", 0)
    lower_half = jnp.where(parity == 0, kept_slice, incoming)
    upper_half = jnp.where(parity == 0, incoming, kept_slice)
    whole_column = jnp.concatenate([lower_half, upper_half], axis=2)[:, :, :, None]
    spread = lax.all_to_all(whole_column, "xy", split_axis=2, concat_axis=3, tiled=True)
    spread = spread.reshape(components, vectors, 4, column_parts, row_count, row_width)
    spread = spread.transpose(0, 1, 2, 4, 3, 5).reshape(components, vectors, LY * LX)
    source = spread.astype(jnp.float32)
    blocks = stencil[0, 0]
    diagonal = jnp.diagonal(blocks[0], axis1=0, axis2=1).T.astype(jnp.float32)[:, None, :]
    site_blocks = blocks.transpose(3, 1, 0, 2).reshape(LY * LX, components, 9 * components)
    iterate = source / diagonal
    for sweep_index in range(SWEEPS - 1):
        rounded = iterate.astype(jnp.bfloat16)
        iterate = iterate + (source - apply_local(rounded, site_blocks)) / diagonal
    regrouped = iterate.reshape(components, vectors, 4, row_count, column_parts, row_width)
    regrouped = regrouped.transpose(0, 1, 2, 4, 3, 5).reshape(
        components, vectors, 1, xy_count, row_count, row_width
    )
    returned = lax.all_to_all(regrouped, "xy", split_axis=3, concat_axis=2, tiled=True)[:, :, :, 0]
    own_half = lax.dynamic_slice_in_dim(returned, parity * half_planes, half_planes, 2)
    other_half = lax.dynamic_slice_in_dim(returned, (1 - parity) * half_planes, half_planes, 2)
    partner_half = partner(other_half.astype(jnp.bfloat16), "zt", 0).astype(other_half.dtype)
    first_slice = jnp.where(parity == 0, own_half, partner_half)
    second_slice = jnp.where(parity == 0, partner_half, own_half)
    result = jnp.stack([first_slice, second_slice], axis=2)
    result = result.reshape(components, vectors, 2 * half_planes * row_count * row_width)
    return result[None, None]


def solution(mesh):
    placed = (P("zt", "xy", None, None, None), P("zt", "xy", None, None, None, None))
    return jax.shard_map(
        shards,
        mesh=mesh,
        in_specs=placed,
        out_specs=P("zt", "xy", None, None, None),
        check_vma=False,
    )
```

profile of v0, /device:TPU:1, one launch (start us, length us, event | category | flops | bytes accessed | tf_op | source)
XLA Modules:
  0.0 275.5 jit_solution(3621511214817711953)
XLA Ops:
  3.6 17.0 %copy.87 = bf16[1,1,9,64,64,256]{5,4,2,3,1,0:T(8,128)(2,1)} copy(bf16[1,1,9,64,64,256]{5,4,3,2,1,0:T(8,128)(2,1)} %param.3) | data formatting | bytes 37748736 | tf_op args[1]
  21.8 8.8 %all-to-all-start = ((bf16[16,2,4096]{2,1,0:T(2,128)(2,1)}), bf16[16,2,4096]{2,1,0:T(2,128)(2,1)S(1)}, u32[]{:S(2)}, u32[]{:S(2)}) async-start(bf16[16,2,4096]{2,1,0:T(2,128)(2,1)} %reshape.121), calls=%async_computation | async-start | bytes 524288 | tf_op jit(solution)/shard_map/all_to_all | solution.py:76
  33.3 27.8 %copy.89 = bf16[256,64,576]{2,1,0:T(8,128)(2,1)} copy(bf16[256,64,576]{0,2,1:T(8,128)(2,1)} %bitcast.139) | data formatting | bytes 37748736 | tf_op jit(solution)/shard_map/reshape | solution.py:82
  62.5 3.3 %collective-permute-start.2 = (bf16[1,1,64,8,256]{2,3,4,1,0:T(8,128)(2,1)S(1)}, bf16[1,1,64,8,256]{2,3,4,1,0:T(8,128)(2,1)S(1)}, u32[]{:S(2)}, u32[]{:S(2)}) collective-permute-start(bf16[1,1,64,8,256]{2,3,4,1,0:T(8,128)(2,1)S(1)} %divide_convert_fusion), channel_id=1, source_target_pairs={{16,0},{32,16},{48,32},{64,48},{80,64},{96,80},{112,96},{0,112},{1... | collective-permute-start | bytes 786440 | tf_op jit(solution)/shard_map/ppermute | solution.py:20
  69.8 8.0 %collective-permute-done.1 = bf16[1,1,64,8,256]{2,3,4,1,0:T(8,128)(2,1)S(1)} collective-permute-done((bf16[1,1,64,8,256]{2,3,4,1,0:T(8,128)(2,1)S(1)}, bf16[1,1,64,8,256]{2,3,4,1,0:T(8,128)(2,1)S(1)}, u32[]{:S(2)}, u32[]{:S(2)}) %collective-permute-start.1) | collective-permute-done | bytes 262176 | tf_op jit(solution)/shard_map/ppermute | solution.py:18
  89.0 4.2 %collective-permute-done.3 = bf16[3,1,64,8,256]{4,3,2,1,0:T(8,128)(2,1)S(1)} collective-permute-done((bf16[3,1,64,8,256]{4,3,2,1,0:T(8,128)(2,1)}, bf16[3,1,64,8,256]{4,3,2,1,0:T(8,128)(2,1)S(1)}, u32[]{:S(2)}, u32[]{:S(2)}) %collective-permute-start.3) | collective-permute-done | bytes 786464 | tf_op jit(solution)/shard_map/ppermute | solution.py:20
  98.5 5.6 %copy.86 = bf16[256,8,9,64]{0,3,2,1:T(8,128)(2,1)S(1)} copy(bf16[256,8,9,64]{3,1,0,2:T(8,128)(2,1)} %bitcast.167) | data formatting | bytes 4718592 | tf_op jit(solution)/shard_map/transpose | solution.py:54
  104.1 3.5 %copy.88 = bf16[256,8,576]{2,1,0:T(8,128)(2,1)} copy(bf16[256,8,576]{0,2,1:T(8,128)(2,1)S(1)} %bitcast.160) | data formatting | bytes 4718592 | tf_op jit(solution)/shard_map/reshape | solution.py:54
  107.5 12.3 %bitcast_dynamic-update-slice_fusion.9 = (bf16[9,64,8,256]{1,2,3,0:T(8,128)(2,1)}, bf16[64,8,256]{0,1,2:T(8,128)(2,1)S(1)}, f32[64,8,256]{0,1,2:T(8,128)}) fusion(f32[64,8,256]{0,1,2:T(8,128)} %bitcast_divide_fusion, f32[64,256]{0,1:T(8,128)S(1)} %copy.65, f32[64,8,256]{0,1,2:T(8,128)S(1)} %bitcast.143, bf16[256,8,576]{2,1,0:T(8,128)(2,1)} %copy.88, ...), kind=kOutput, calls=%fused_computation.50 | convolution fusion | flops 151519232 | bytes 24182784 | tf_op jit(solution)/shard_map/dot_general | solution.py:55
  119.9 3.7 %collective-permute-start.6 = (bf16[1,1,64,8,256]{2,3,4,1,0:T(8,128)(2,1)S(1)}, bf16[1,1,64,8,256]{2,3,4,1,0:T(8,128)(2,1)S(1)}, u32[]{:S(2)}, u32[]{:S(2)}) collective-permute-start(bf16[1,1,64,8,256]{2,3,4,1,0:T(8,128)(2,1)S(1)} %bitcast.147), channel_id=1, source_target_pairs={{16,0},{32,16},{48,32},{64,48},{80,64},{96,80},{112,96},{0,112},{1... | collective-permute-start | bytes 786440 | tf_op jit(solution)/shard_map/ppermute | solution.py:20
  125.9 4.1 %collective-permute-done.5 = bf16[1,1,64,8,256]{2,3,4,1,0:T(8,128)(2,1)S(1)} collective-permute-done((bf16[1,1,64,8,256]{2,3,4,1,0:T(8,128)(2,1)S(1)}, bf16[1,1,64,8,256]{2,3,4,1,0:T(8,128)(2,1)S(1)}, u32[]{:S(2)}, u32[]{:S(2)}) %collective-permute-start.5) | collective-permute-done | bytes 262176 | tf_op jit(solution)/shard_map/ppermute | solution.py:18
  133.8 8.7 %collective-permute-start.7 = (bf16[3,1,64,8,256]{4,3,2,1,0:T(8,128)(2,1)}, bf16[3,1,64,8,256]{4,3,2,1,0:T(8,128)(2,1)S(1)}, u32[]{:S(2)}, u32[]{:S(2)}) collective-permute-start(bf16[3,1,64,8,256]{4,3,2,1,0:T(8,128)(2,1)} %copy.90), channel_id=1, source_target_pairs={{1,0},{2,1},{3,2},{4,3},{5,4},{6,5},{7,6},{8,7},{9,8},{10,9},{11,1... | collective-permute-start | bytes 2359304 | tf_op jit(solution)/shard_map/ppermute | solution.py:20
  157.6 5.6 %copy.94 = bf16[256,8,9,64]{0,3,2,1:T(8,128)(2,1)S(1)} copy(bf16[256,8,9,64]{3,1,0,2:T(8,128)(2,1)} %bitcast.165) | data formatting | bytes 4718592 | tf_op jit(solution)/shard_map/transpose | solution.py:54
  163.2 3.5 %copy.95 = bf16[256,8,576]{2,1,0:T(8,128)(2,1)} copy(bf16[256,8,576]{0,2,1:T(8,128)(2,1)S(1)} %bitcast.161) | data formatting | bytes 4718592 | tf_op jit(solution)/shard_map/reshape | solution.py:54
  166.6 12.3 %bitcast_dynamic-update-slice_fusion.4 = (bf16[9,64,8,256]{1,2,3,0:T(8,128)(2,1)}, bf16[64,8,256]{0,1,2:T(8,128)(2,1)S(1)}, f32[64,8,256]{0,1,2:T(8,128)}) fusion(f32[64,8,256]{0,1,2:T(8,128)} %get-tuple-element.37, f32[64,256]{0,1:T(8,128)S(1)} %copy.65, f32[64,8,256]{0,1,2:T(8,128)S(1)} %bitcast.144, bf16[256,8,576]{2,1,0:T(8,128)(2,1)} %copy.95, ...), kind=kOutput, calls=%fused_computation.45 | convolution fusion | flops 151519232 | bytes 24182784 | tf_op jit(solution)/shard_map/dot_general | solution.py:55
  184.3 3.9 %collective-permute-done.10 = bf16[1,1,64,8,256]{2,3,4,1,0:T(8,128)(2,1)S(1)} collective-permute-done((bf16[1,1,64,8,256]{2,3,4,1,0:T(8,128)(2,1)S(1)}, bf16[1,1,64,8,256]{2,3,4,1,0:T(8,128)(2,1)S(1)}, u32[]{:S(2)}, u32[]{:S(2)}) %collective-permute-start.10) | collective-permute-done | bytes 262176 | tf_op jit(solution)/shard_map/ppermute | solution.py:20
  188.2 4.0 %collective-permute-done.9 = bf16[1,1,64,8,256]{2,3,4,1,0:T(8,128)(2,1)S(1)} collective-permute-done((bf16[1,1,64,8,256]{2,3,4,1,0:T(8,128)(2,1)S(1)}, bf16[1,1,64,8,256]{2,3,4,1,0:T(8,128)(2,1)S(1)}, u32[]{:S(2)}, u32[]{:S(2)}) %collective-permute-start.9) | collective-permute-done | bytes 262176 | tf_op jit(solution)/shard_map/ppermute | solution.py:18
  195.2 9.4 %collective-permute-start.11 = (bf16[3,1,64,8,256]{4,3,2,1,0:T(8,128)(2,1)}, bf16[3,1,64,8,256]{4,3,2,1,0:T(8,128)(2,1)S(1)}, u32[]{:S(2)}, u32[]{:S(2)}) collective-permute-start(bf16[3,1,64,8,256]{4,3,2,1,0:T(8,128)(2,1)} %copy.97), channel_id=1, source_target_pairs={{1,0},{2,1},{3,2},{4,3},{5,4},{6,5},{7,6},{8,7},{9,8},{10,9},{11,1... | collective-permute-start | bytes 2359304 | tf_op jit(solution)/shard_map/ppermute | solution.py:20
  219.7 5.6 %copy.101 = bf16[256,8,9,64]{0,3,2,1:T(8,128)(2,1)S(1)} copy(bf16[256,8,9,64]{3,1,0,2:T(8,128)(2,1)} %bitcast.166) | data formatting | bytes 4718592 | tf_op jit(solution)/shard_map/transpose | solution.py:54
  225.3 3.5 %copy.102 = bf16[256,8,576]{2,1,0:T(8,128)(2,1)} copy(bf16[256,8,576]{0,2,1:T(8,128)(2,1)S(1)} %bitcast.162) | data formatting | bytes 4718592 | tf_op jit(solution)/shard_map/reshape | solution.py:54
  228.8 11.3 %fusion.8 = f32[64,8,256]{0,1,2:T(8,128)S(1)} fusion(f32[64,8,256]{0,1,2:T(8,128)} %get-tuple-element.38, f32[64,8,256]{0,1,2:T(8,128)S(1)} %bitcast.145, bf16[256,8,576]{2,1,0:T(8,128)(2,1)} %copy.102, bf16[256,64,576]{2,1,0:T(8,128)(2,1)} %copy.89, f32[64,256]{0,1:T(8,128)S(1)} %copy.65), kind=kOutput, calls=%fused_computation.16 | convolution fusion | flops 151388160 | bytes 22872064 | tf_op jit(solution)/shard_map/dot_general | solution.py:55
  241.7 11.1 %all-to-all-start.1 = ((f32[16,1,8192]{2,1,0:T(1,128)}), f32[16,1,8192]{2,1,0:T(1,128)S(1)}, u32[]{:S(2)}, u32[]{:S(2)}) async-start(f32[16,1,8192]{2,1,0:T(1,128)} %reshape.123), calls=%async_computation.1 | async-start | bytes 1048576 | tf_op jit(solution)/shard_map/all_to_all | solution.py:91
  252.8 11.5 %all-to-all-done.1 = f32[16,1,8192]{2,1,0:T(1,128)S(1)} async-done(((f32[16,1,8192]{2,1,0:T(1,128)}), f32[16,1,8192]{2,1,0:T(1,128)S(1)}, u32[]{:S(2)}, u32[]{:S(2)}) %all-to-all-start.1) | async-done | bytes 524320 | tf_op jit(solution)/shard_map/all_to_all | solution.py:91
  267.3 6.7 %collective-permute-done.13 = bf16[64,8,8,4,4]{0,1,4,3,2:T(8,128)(2,1)S(1)} collective-permute-done((bf16[64,8,8,4,4]{0,1,4,3,2:T(8,128)(2,1)S(1)}, bf16[64,8,8,4,4]{0,1,4,3,2:T(8,128)(2,1)S(1)}, u32[]{:S(2)}, u32[]{:S(2)}) %collective-permute-start.13) | collective-permute-done | bytes 131104 | tf_op jit(solution)/shard_map/ppermute | solution.py:28
  (125 shorter events, 79.9 us)
Async XLA Ops:
  1.5 19.1 %collective-permute-start = (bf16[64,8,8,4,4]{0,1,4,3,2:T(8,128)(2,1)S(1)}, bf16[64,8,8,4,4]{0,1,4,3,2:T(8,128)(2,1)S(1)}, u32[]{:S(2)}, u32[]{:S(2)}) collective-permute-start(bf16[64,8,8,4,4]{0,1,4,3,2:T(8,128)(2,1)S(1)} %dynamic-slice_bitcast_fusion), channel_id=1, source_target_pairs={{0,16},{16,0},{32,48},{48,32},{64,80},{80,64},{96,112},{112,96},{1... | collective-permute-start | bytes 393224 | tf_op jit(solution)/shard_map/ppermute | solution.py:28
  21.8 39.3 %all-to-all-start = ((bf16[16,2,4096]{2,1,0:T(2,128)(2,1)}), bf16[16,2,4096]{2,1,0:T(2,128)(2,1)S(1)}, u32[]{:S(2)}, u32[]{:S(2)}) async-start(bf16[16,2,4096]{2,1,0:T(2,128)(2,1)} %reshape.121), calls=%async_computation | async-start | bytes 524288 | tf_op jit(solution)/shard_map/all_to_all | solution.py:76
  62.2 15.7 %collective-permute-start.1 = (bf16[1,1,64,8,256]{2,3,4,1,0:T(8,128)(2,1)S(1)}, bf16[1,1,64,8,256]{2,3,4,1,0:T(8,128)(2,1)S(1)}, u32[]{:S(2)}, u32[]{:S(2)}) collective-permute-start(bf16[1,1,64,8,256]{2,3,4,1,0:T(8,128)(2,1)S(1)} %divide_convert_fusion), channel_id=1, source_target_pairs={{0,16},{16,32},{32,48},{48,64},{64,80},{80,96},{96,112},{112,0},{1... | collective-permute-start | bytes 786440 | tf_op jit(solution)/shard_map/ppermute | solution.py:18
  62.5 15.3 %collective-permute-start.2 = (bf16[1,1,64,8,256]{2,3,4,1,0:T(8,128)(2,1)S(1)}, bf16[1,1,64,8,256]{2,3,4,1,0:T(8,128)(2,1)S(1)}, u32[]{:S(2)}, u32[]{:S(2)}) collective-permute-start(bf16[1,1,64,8,256]{2,3,4,1,0:T(8,128)(2,1)S(1)} %divide_convert_fusion), channel_id=1, source_target_pairs={{16,0},{32,16},{48,32},{64,48},{80,64},{96,80},{112,96},{0,112},{1... | collective-permute-start | bytes 786440 | tf_op jit(solution)/shard_map/ppermute | solution.py:20
  77.9 0.8 copy-start.6
  80.9 12.4 %collective-permute-start.3 = (bf16[3,1,64,8,256]{4,3,2,1,0:T(8,128)(2,1)}, bf16[3,1,64,8,256]{4,3,2,1,0:T(8,128)(2,1)S(1)}, u32[]{:S(2)}, u32[]{:S(2)}) collective-permute-start(bf16[3,1,64,8,256]{4,3,2,1,0:T(8,128)(2,1)} %copy.76), channel_id=1, source_target_pairs={{1,0},{2,1},{3,2},{4,3},{5,4},{6,5},{7,6},{8,7},{9,8},{10,9},{11,1... | collective-permute-start | bytes 2359304 | tf_op jit(solution)/shard_map/ppermute | solution.py:20
  81.7 12.0 %collective-permute-start.4 = (bf16[3,1,64,8,256]{4,3,2,1,0:T(8,128)(2,1)}, bf16[3,1,64,8,256]{4,3,2,1,0:T(8,128)(2,1)}, u32[]{:S(2)}, u32[]{:S(2)}) collective-permute-start(bf16[3,1,64,8,256]{4,3,2,1,0:T(8,128)(2,1)} %copy.76), channel_id=1, source_target_pairs={{0,1},{1,2},{2,3},{3,4},{4,5},{5,6},{6,7},{7,8},{8,9},{9,10},{10,1... | collective-permute-start | bytes 2359304 | tf_op jit(solution)/shard_map/ppermute | solution.py:18
  86.2 10.6 %copy-start.7 = (bf16[1,1,64,8,256]{2,3,4,1,0:T(8,128)(2,1)S(1)}, bf16[1,1,64,8,256]{2,3,4,1,0:T(8,128)(2,1)}, u32[]{:S(2)}) copy-start(bf16[1,1,64,8,256]{2,3,4,1,0:T(8,128)(2,1)} %copy-done.6) | copy-start | bytes 786436
  119.9 10.1 %collective-permute-start.5 = (bf16[1,1,64,8,256]{2,3,4,1,0:T(8,128)(2,1)S(1)}, bf16[1,1,64,8,256]{2,3,4,1,0:T(8,128)(2,1)S(1)}, u32[]{:S(2)}, u32[]{:S(2)}) collective-permute-start(bf16[1,1,64,8,256]{2,3,4,1,0:T(8,128)(2,1)S(1)} %bitcast.146), channel_id=1, source_target_pairs={{0,16},{16,32},{32,48},{48,64},{64,80},{80,96},{96,112},{112,0},{1... | collective-permute-start | bytes 786440 | tf_op jit(solution)/shard_map/ppermute | solution.py:18
  119.9 10.1 %collective-permute-start.6 = (bf16[1,1,64,8,256]{2,3,4,1,0:T(8,128)(2,1)S(1)}, bf16[1,1,64,8,256]{2,3,4,1,0:T(8,128)(2,1)S(1)}, u32[]{:S(2)}, u32[]{:S(2)}) collective-permute-start(bf16[1,1,64,8,256]{2,3,4,1,0:T(8,128)(2,1)S(1)} %bitcast.147), channel_id=1, source_target_pairs={{16,0},{32,16},{48,32},{64,48},{80,64},{96,80},{112,96},{0,112},{1... | collective-permute-start | bytes 786440 | tf_op jit(solution)/shard_map/ppermute | solution.py:20
  130.0 0.8 copy-start
  130.8 0.8 copy-start.5
  133.8 17.2 %collective-permute-start.7 = (bf16[3,1,64,8,256]{4,3,2,1,0:T(8,128)(2,1)}, bf16[3,1,64,8,256]{4,3,2,1,0:T(8,128)(2,1)S(1)}, u32[]{:S(2)}, u32[]{:S(2)}) collective-permute-start(bf16[3,1,64,8,256]{4,3,2,1,0:T(8,128)(2,1)} %copy.90), channel_id=1, source_target_pairs={{1,0},{2,1},{3,2},{4,3},{5,4},{6,5},{7,6},{8,7},{9,8},{10,9},{11,1... | collective-permute-start | bytes 2359304 | tf_op jit(solution)/shard_map/ppermute | solution.py:20
  142.5 9.3 %collective-permute-start.8 = (bf16[3,1,64,8,256]{4,3,2,1,0:T(8,128)(2,1)}, bf16[3,1,64,8,256]{4,3,2,1,0:T(8,128)(2,1)}, u32[]{:S(2)}, u32[]{:S(2)}) collective-permute-start(bf16[3,1,64,8,256]{4,3,2,1,0:T(8,128)(2,1)} %copy.90), channel_id=1, source_target_pairs={{0,1},{1,2},{2,3},{3,4},{4,5},{5,6},{6,7},{7,8},{8,9},{9,10},{10,1... | collective-permute-start | bytes 2359304 | tf_op jit(solution)/shard_map/ppermute | solution.py:18
  146.8 10.0 %copy-start.1 = (bf16[1,1,64,8,256]{2,3,4,1,0:T(8,128)(2,1)S(1)}, bf16[1,1,64,8,256]{2,3,4,1,0:T(8,128)(2,1)}, u32[]{:S(2)}) copy-start(bf16[1,1,64,8,256]{2,3,4,1,0:T(8,128)(2,1)} %copy-done) | copy-start | bytes 786436
  179.0 9.2 %collective-permute-start.10 = (bf16[1,1,64,8,256]{2,3,4,1,0:T(8,128)(2,1)S(1)}, bf16[1,1,64,8,256]{2,3,4,1,0:T(8,128)(2,1)S(1)}, u32[]{:S(2)}, u32[]{:S(2)}) collective-permute-start(bf16[1,1,64,8,256]{2,3,4,1,0:T(8,128)(2,1)S(1)} %bitcast.153), channel_id=1, source_target_pairs={{16,0},{32,16},{48,32},{64,48},{80,64},{96,80},{112,96},{0,112},{1... | collective-permute-start | bytes 786440 | tf_op jit(solution)/shard_map/ppermute | solution.py:20
  182.1 10.1 %collective-permute-start.9 = (bf16[1,1,64,8,256]{2,3,4,1,0:T(8,128)(2,1)S(1)}, bf16[1,1,64,8,256]{2,3,4,1,0:T(8,128)(2,1)S(1)}, u32[]{:S(2)}, u32[]{:S(2)}) collective-permute-start(bf16[1,1,64,8,256]{2,3,4,1,0:T(8,128)(2,1)S(1)} %bitcast.154), channel_id=1, source_target_pairs={{0,16},{16,32},{32,48},{48,64},{64,80},{80,96},{96,112},{112,0},{1... | collective-permute-start | bytes 786440 | tf_op jit(solution)/shard_map/ppermute | solution.py:18
  188.2 4.0 %copy-start.2 = (bf16[1,1,64,8,256]{2,3,4,1,0:T(8,128)(2,1)}, bf16[1,1,64,8,256]{2,3,4,1,0:T(8,128)(2,1)S(1)}, u32[]{:S(2)}) copy-start(bf16[1,1,64,8,256]{2,3,4,1,0:T(8,128)(2,1)S(1)} %collective-permute-done.10) | copy-start | bytes 786436
  192.2 0.8 copy-start.3
  195.2 17.1 %collective-permute-start.11 = (bf16[3,1,64,8,256]{4,3,2,1,0:T(8,128)(2,1)}, bf16[3,1,64,8,256]{4,3,2,1,0:T(8,128)(2,1)S(1)}, u32[]{:S(2)}, u32[]{:S(2)}) collective-permute-start(bf16[3,1,64,8,256]{4,3,2,1,0:T(8,128)(2,1)} %copy.97), channel_id=1, source_target_pairs={{1,0},{2,1},{3,2},{4,3},{5,4},{6,5},{7,6},{8,7},{9,8},{10,9},{11,1... | collective-permute-start | bytes 2359304 | tf_op jit(solution)/shard_map/ppermute | solution.py:20
  204.6 9.3 %collective-permute-start.12 = (bf16[3,1,64,8,256]{4,3,2,1,0:T(8,128)(2,1)}, bf16[3,1,64,8,256]{4,3,2,1,0:T(8,128)(2,1)}, u32[]{:S(2)}, u32[]{:S(2)}) collective-permute-start(bf16[3,1,64,8,256]{4,3,2,1,0:T(8,128)(2,1)} %copy.97), channel_id=1, source_target_pairs={{0,1},{1,2},{2,3},{3,4},{4,5},{5,6},{6,7},{7,8},{8,9},{9,10},{10,1... | collective-permute-start | bytes 2359304 | tf_op jit(solution)/shard_map/ppermute | solution.py:18
  208.9 10.0 %copy-start.4 = (bf16[1,1,64,8,256]{2,3,4,1,0:T(8,128)(2,1)S(1)}, bf16[1,1,64,8,256]{2,3,4,1,0:T(8,128)(2,1)}, u32[]{:S(2)}) copy-start(bf16[1,1,64,8,256]{2,3,4,1,0:T(8,128)(2,1)} %copy-done.3) | copy-start | bytes 786436
  241.7 22.6 %all-to-all-start.1 = ((f32[16,1,8192]{2,1,0:T(1,128)}), f32[16,1,8192]{2,1,0:T(1,128)S(1)}, u32[]{:S(2)}, u32[]{:S(2)}) async-start(f32[16,1,8192]{2,1,0:T(1,128)} %reshape.123), calls=%async_computation.1 | async-start | bytes 1048576 | tf_op jit(solution)/shard_map/all_to_all | solution.py:91
  267.2 6.8 %collective-permute-start.13 = (bf16[64,8,8,4,4]{0,1,4,3,2:T(8,128)(2,1)S(1)}, bf16[64,8,8,4,4]{0,1,4,3,2:T(8,128)(2,1)S(1)}, u32[]{:S(2)}, u32[]{:S(2)}) collective-permute-start(bf16[64,8,8,4,4]{0,1,4,3,2:T(8,128)(2,1)S(1)} %fusion.12), channel_id=1, source_target_pairs={{0,16},{16,0},{32,48},{48,32},{64,80},{80,64},{96,112},{112,96},{1... | collective-permute-start | bytes 393224 | tf_op jit(solution)/shard_map/ppermute | solution.py:28
where the time goes:
time: 278 us; the launch traced here: 276 us
  local copies, waits for them, and re-layouts  124 us (45%)
  starting transfers between devices  52.8 us (19%)
  waiting for transfers between devices  46.5 us (17%)
  matrix products  36 us (13%)
  other arithmetic  15.5 us (6%)
    unnamed x49, local copies, waits for them, and re-layouts  48.2 us
    dot_general x3, matrix products, apply_local(): lax.dot_general(site_blocks, site_vectors, (((2,), (2,)), ((0,), (0,))),...  36 us
    ppermute x6, starting transfers between devices, with_halo(): lax.ppermute(head, axis, [((i + 1) % count, i) for i in range(count)])  29.1 us
    reshape x1, local copies, waits for them, and re-layouts, shards(): blocks.transpose(3, 1, 0, 2).reshape(LY * LX, components, 9 * components)  27.8 us
    ppermute x6, waiting for transfers between devices, with_halo(): lax.ppermute(tail, axis, [(i, (i + 1) % count) for i in range(count)])  17.5 us
    transpose x3, local copies, waits for them, and re-layouts, apply_local(): neighbours.transpose(3, 2, 0, 1).reshape(LY * LX, vectors, 9 * components)  16.7 us
    all_to_all x1, waiting for transfers between devices, shards(): lax.all_to_all(regrouped, 'xy', split_axis=3, concat_axis=2, tiled=True)  11.5 us
    all_to_all x1, starting transfers between devices, shards(): lax.all_to_all(regrouped, 'xy', split_axis=3, concat_axis=2, tiled=True)  11.1 us
  transfers between devices with their start and end apart: 16, of which 11 were waited for; matrix products, arithmetic and copies ran while one was open for 28% of the time, Pallas kernels for 0%

commit v1 on v0

v1 whole, which is shorter than its diff:
```python
import functools

import jax
import jax.numpy as jnp
from jax import lax
from jax.experimental import pallas as pl
from jax.experimental.pallas import tpu as pltpu
from jax.sharding import PartitionSpec as P

LX = 16
LY = 16
SWEEPS = 4
ROWS = 16
PAIR = 2
GROUP = 4
LANES = 128
F32 = jnp.float32
BF16 = jnp.bfloat16


def total(terms):
    while len(terms) > 1:
        terms = [sum(terms[i : i + 2][1:], terms[i]) for i in range(0, len(terms), 2)]
    return terms[0]


def multiply(blocks, vectors, partial_ref, write):
    _, count, _, _ = partial_ref.shape
    sixteens = 4

    @pl.loop(0, ROWS // PAIR)
    def _(pair):
        for first in range(0, count, GROUP):
            sums = {}
            for block, vector in zip(blocks, vectors):
                rows = [[block(pair * PAIR + o, i) for i in range(sixteens)] for o in range(PAIR)]
                for r in range(first, first + GROUP):
                    column = [vector(r, i) for i in range(sixteens)]
                    for o in range(PAIR):
                        term = total([a * v for a, v in zip(rows[o], column)])
                        term = (term[:8] + term[8:]).astype(F32)
                        sums[o, r] = sums[o, r] + term if (o, r) in sums else term
            for (o, r), value in sums.items():
                place = pl.ds(pl.multiple_of((pair * PAIR + o) * 8, 8), 8)
                partial_ref[0, r, place, :] = value[:, :LANES]
                partial_ref[1, r, place, :] = value[:, LANES:]

    for r in range(count):
        for half in range(2):
            parts = []
            for eight in range(ROWS // 8):
                parts.append(
                    total([partial_ref[half, r, pl.ds(eight * 64 + j, 8, stride=8), :] for j in range(8)])
                )
            write(r, half, jnp.concatenate(parts, axis=0))


def prepare_kernel(block_ref, off_ref, inverse_ref):
    rows, components, sites = block_ref.shape[1:]
    first = pl.program_id(0) * rows
    own = lax.broadcasted_iota(jnp.int32, (components, sites), 0)
    for o in range(rows):
        block = block_ref[0, o].astype(F32)
        here = own == first + o
        off_ref[o] = jnp.where(here, 0.0, block).astype(BF16)
        diagonal = jnp.sum(jnp.where(here, block, 0.0), axis=0, keepdims=True)
        inverse_ref[o : o + 1, :] = 1.0 / diagonal


def prepare(stencil):
    components, sites = stencil.shape[2:]
    return pl.pallas_call(
        prepare_kernel,
        grid=(components // ROWS,),
        in_specs=[pl.BlockSpec((1, ROWS, components, sites), lambda g: (0, g, 0, 0))],
        out_specs=[
            pl.BlockSpec((ROWS, components, sites), lambda g: (g, 0, 0)),
            pl.BlockSpec((ROWS, sites), lambda g: (g, 0)),
        ],
        out_shape=[
            jax.ShapeDtypeStruct((components, components, sites), BF16),
            jax.ShapeDtypeStruct((components, sites), F32),
        ],
        cost_estimate=pl.CostEstimate(flops=10**7, bytes_accessed=4 * 2**20, transcendentals=0),
        name="prepare",
    )(stencil)


def start_kernel(source_ref, inverse_ref, iterate_ref, rounded_ref):
    inverse = inverse_ref[...]
    for r in range(source_ref.shape[0]):
        iterate = source_ref[r].astype(F32) * inverse
        iterate_ref[r] = iterate
        rounded_ref[r] = iterate.astype(BF16)


def start(source, inverse):
    return pl.pallas_call(
        start_kernel,
        out_shape=[jax.ShapeDtypeStruct(source.shape, F32), jax.ShapeDtypeStruct(source.shape, BF16)],
        name="start",
    )(source, inverse)


def local_kernel(off_ref, hops_ref, source_ref, iterate_ref, rounded_ref, inverse_ref, base_ref, near_ref, partial_ref):
    count, components, sites = rounded_ref.shape

    @pl.when(pl.program_id(0) == 0)
    def _():
        lane = lax.broadcasted_iota(jnp.int32, (components, sites), 1) % LX
        for r in range(count):
            value = rounded_ref[r].astype(F32)
            after = jnp.where(
                lane == LX - 1, pltpu.roll(value, LX - 1, 1), pltpu.roll(value, sites - 1, 1)
            )
            before = jnp.where(lane == 0, pltpu.roll(value, sites - LX + 1, 1), pltpu.roll(value, 1, 1))
            near_ref[0, r] = after.astype(BF16)
            near_ref[1, r] = before.astype(BF16)
            near_ref[2, r] = pltpu.roll(value, sites - LX, 1).astype(BF16)
            near_ref[3, r] = pltpu.roll(value, LX, 1).astype(BF16)

    def sixteen(i):
        return slice(16 * i, 16 * i + 16)

    blocks = [lambda o, i: off_ref[o, sixteen(i), :]]
    vectors = [lambda r, i: rounded_ref[r, sixteen(i), :]]
    for k in range(4):
        blocks.append(lambda o, i, k=k: hops_ref[k, o, sixteen(i), :])
        vectors.append(lambda r, i, k=k: near_ref[k, r, sixteen(i), :])

    here = pl.ds(pl.multiple_of(pl.program_id(0) * ROWS, ROWS), ROWS)

    def write(r, half, sums):
        lanes = slice(half * LANES, half * LANES + LANES)
        left = source_ref[r, :, lanes].astype(F32) - sums
        kept = iterate_ref[r, :, lanes] - rounded_ref[r, here, lanes].astype(F32)
        base_ref[r, :, lanes] = kept + left * inverse_ref[:, lanes]

    multiply(blocks, vectors, partial_ref, write)


def local(off, stencil, source, iterate, rounded, inverse):
    count, components, sites = rounded.shape
    part = pl.BlockSpec((count, ROWS, sites), lambda g: (0, g, 0))
    return pl.pallas_call(
        local_kernel,
        grid=(components // ROWS,),
        in_specs=[
            pl.BlockSpec((ROWS, components, sites), lambda g: (g, 0, 0)),
            pl.BlockSpec((pl.Element(4), pl.Element(ROWS), pl.Element(components), pl.Element(sites)),
                         lambda g: (1, g * ROWS, 0, 0)),
            part,
            part,
            pl.BlockSpec((count, components, sites), lambda g: (0, 0, 0)),
            pl.BlockSpec((ROWS, sites), lambda g: (g, 0)),
        ],
        out_specs=part,
        out_shape=jax.ShapeDtypeStruct(rounded.shape, F32),
        scratch_shapes=[
            pltpu.VMEM((4, count, components, sites), BF16),
            pltpu.VMEM((2, count, ROWS * 8, LANES), F32),
        ],
        compiler_params=pltpu.CompilerParams(vmem_limit_bytes=40 * 2**20),
        cost_estimate=pl.CostEstimate(flops=10**9, bytes_accessed=12 * 2**20, transcendentals=0),
        name="local",
    )(off, stencil, source, iterate, rounded, inverse)


def remote_kernel(last, hops_ref, above_ref, below_ref, after_ref, earlier_ref, base_ref, inverse_ref, *rest):
    if last:
        rounded_ref, partial_ref = rest
    else:
        iterate_ref, rounded_ref, partial_ref = rest

    def sixteen(i):
        return slice(16 * i, 16 * i + 16)

    blocks, vectors = [], []
    for k, ref in enumerate((above_ref, below_ref, after_ref, earlier_ref)):
        blocks.append(lambda o, i, k=k: hops_ref[k, o, sixteen(i), :])
        vectors.append(lambda r, i, ref=ref: ref[r, sixteen(i), :])

    def write(r, half, sums):
        lanes = slice(half * LANES, half * LANES + LANES)
        iterate = base_ref[r, :, lanes] - sums * inverse_ref[:, lanes]
        if not last:
            iterate_ref[r, :, lanes] = iterate
        rounded_ref[r, :, lanes] = iterate.astype(BF16)

    multiply(blocks, vectors, partial_ref, write)


def remote(stencil, halos, base, inverse, last):
    count, components, sites = base.shape
    part = pl.BlockSpec((count, ROWS, sites), lambda g: (0, g, 0))
    whole = pl.BlockSpec((count, components, sites), lambda g: (0, 0, 0))
    types = [BF16] if last else [F32, BF16]
    return pl.pallas_call(
        functools.partial(remote_kernel, last),
        grid=(components // ROWS,),
        in_specs=[
            pl.BlockSpec((pl.Element(4), pl.Element(ROWS), pl.Element(components), pl.Element(sites)),
                         lambda g: (5, g * ROWS, 0, 0)),
            whole, whole, whole, whole,
            part,
            pl.BlockSpec((ROWS, sites), lambda g: (g, 0)),
        ],
        out_specs=[part for _ in types],
        out_shape=[jax.ShapeDtypeStruct(base.shape, t) for t in types],
        scratch_shapes=[pltpu.VMEM((2, count, ROWS * 8, LANES), F32)],
        compiler_params=pltpu.CompilerParams(vmem_limit_bytes=40 * 2**20),
        cost_estimate=pl.CostEstimate(flops=10**9, bytes_accessed=12 * 2**20, transcendentals=0),
        name="remote",
    )(stencil, *halos, base, inverse)


def neighbour(plane, axis, step):
    count = lax.axis_size(axis)
    return lax.ppermute(plane, axis, [((i + step) % count, i) for i in range(count)])


def partner(shard, axis):
    return lax.ppermute(shard, axis, [(i, i ^ 1) for i in range(lax.axis_size(axis))])


def shards(restricted, stencil):
    columns = lax.axis_size("xy")
    parts = columns // 4
    planes = columns // 2
    width = LX // parts
    height = LY // 4
    components, count = restricted.shape[2], restricted.shape[3]
    parity = lax.axis_index("zt") % 2
    stencil = stencil[0, 0]
    off, inverse = prepare(stencil)

    pieces = restricted[0, 0].reshape(components, count, 2, planes, height, width)
    kept = lax.dynamic_index_in_dim(pieces, parity, 2, keepdims=False)
    outgoing = lax.dynamic_index_in_dim(pieces, 1 - parity, 2, keepdims=False)
    incoming = partner(outgoing, "zt")
    lower = jnp.where(parity == 0, kept, incoming)
    upper = jnp.where(parity == 0, incoming, kept)
    column = jnp.concatenate([lower, upper], axis=2)[:, :, :, None]
    spread = lax.all_to_all(column, "xy", split_axis=2, concat_axis=3, tiled=True)
    spread = spread.reshape(components, count, 4, parts, height, width)
    source = spread.transpose(1, 0, 2, 4, 3, 5).reshape(count, components, LY * LX)

    iterate, rounded = start(source, inverse)
    for sweep in range(SWEEPS - 1):
        last = sweep == SWEEPS - 2
        halos = [
            neighbour(rounded, "xy", 1),
            neighbour(rounded, "xy", -1),
            neighbour(rounded, "zt", 1),
            neighbour(rounded, "zt", -1),
        ]
        base = local(off, stencil, source, iterate, rounded, inverse)
        results = remote(stencil, halos, base, inverse, last)
        if last:
            (rounded,) = results
        else:
            iterate, rounded = results

    regrouped = rounded.reshape(count, components, 4, height, parts, width)
    regrouped = regrouped.transpose(1, 0, 2, 4, 3, 5).reshape(components, count, 1, columns, height, width)
    returned = lax.all_to_all(regrouped, "xy", split_axis=3, concat_axis=2, tiled=True)[:, :, :, 0]
    own = lax.dynamic_slice_in_dim(returned, parity * planes, planes, 2)
    other = lax.dynamic_slice_in_dim(returned, (1 - parity) * planes, planes, 2)
    other = partner(other, "zt")
    first = jnp.where(parity == 0, own, other)
    second = jnp.where(parity == 0, other, own)
    result = jnp.stack([first, second], axis=2).astype(F32)
    return result.reshape(1, 1, components, count, 2 * planes * height * width)


def solution(mesh):
    placed = (P("zt", "xy", None, None, None), P("zt", "xy", None, None, None, None))
    return jax.shard_map(
        shards,
        mesh=mesh,
        in_specs=placed,
        out_specs=P("zt", "xy", None, None, None),
        check_vma=False,
    )
```

time: 278 us -> 145 us (0.52)
  local copies, waits for them, and re-layouts: 124 us -> 12.4 us
  Pallas kernels: 0 us -> 60.1 us
  matrix products: 36 us -> 0 us
  waiting for transfers between devices: 46.5 us -> 25.8 us
  other arithmetic: 15.5 us -> 0.3 us
  starting transfers between devices: 52.8 us -> 44.7 us
    pallas_call x0 -> x8, Pallas kernels: none -> 60.1 us  [the longest x3 30.1 us: local(): pl.pallas_call(local_kernel, grid=(components // ROWS,), in_specs=[pl.Blo...]
    unnamed x49 -> x21, local copies, waits for them, and re-layouts: 48.2 us -> 9.72 us
    reshape x5 -> x1, local copies, waits for them, and re-layouts: 38.4 us -> 1.03 us  [shards(): spread.transpose(1, 0, 2, 4, 3, 5).reshape(count, components, LY * LX)]
    dot_general x3 -> x0, matrix products: 36 us -> none  [apply_local(): lax.dot_general(site_blocks, site_vectors, (((2,), (2,)), ((0,), (0,))),...]
    ppermute x14, waiting for transfers between devices: 35 us -> 12.5 us  [the longest x2 12.5 us: partner(): lax.ppermute(shard, axis, [(i, i ^ 1) for i in range(lax.axis_size(axis))])]
    transpose x4 -> x2, local copies, waits for them, and re-layouts: 18.4 us -> 0.1 us  [the longest x1 0.05 us: shards(): spread.transpose(1, 0, 2, 4, 3, 5).reshape(count, components, LY * LX)]
    concatenate x14 -> x0, other arithmetic: 10.6 us -> none  [the longest x3 3.65 us: apply_local(): jnp.roll(planar, -1, 2).reshape(flat_shape)]
    slice x18 -> x0, local copies, waits for them, and re-layouts: 8.57 us -> none  [the longest x6 3.22 us: apply_local(): jnp.roll(planar, 1, 2).reshape(flat_shape)]
  transfers between devices with their start and end apart: 16 -> 16, of which waited for: 11 -> 4; matrix products, arithmetic and copies ran while one was open for 28% -> 0% of each run, Pallas kernels for 0% -> 24%
where the time goes in v1:
time: 145 us; the launch traced here: 144 us
  Pallas kernels  60.1 us (41%)
  starting transfers between devices  44.7 us (31%)
  waiting for transfers between devices  25.8 us (18%)
  local copies, waits for them, and re-layouts  12.4 us (9%)
    pallas_call x3, Pallas kernels, local(): pl.pallas_call(local_kernel, grid=(components // ROWS,), in_specs=[pl.Blo...  30.1 us
    ppermute x12, starting transfers between devices, neighbour(): lax.ppermute(plane, axis, [((i + step) % count, i) for i in range(count)])  24.1 us
    pallas_call x3, Pallas kernels, remote(): pl.pallas_call(functools.partial(remote_kernel, last), grid=(components /...  23.9 us
    ppermute x2, waiting for transfers between devices, partner(): lax.ppermute(shard, axis, [(i, i ^ 1) for i in range(lax.axis_size(axis))])  12.5 us
    all_to_all x1, starting transfers between devices, shards(): lax.all_to_all(column, 'xy', split_axis=2, concat_axis=3, tiled=True)  9.78 us
    unnamed x21, local copies, waits for them, and re-layouts  9.72 us
    all_to_all x1, waiting for transfers between devices, shards(): lax.all_to_all(regrouped, 'xy', split_axis=3, concat_axis=2, tiled=True)  8.75 us
    all_to_all x1, starting transfers between devices, shards(): lax.all_to_all(regrouped, 'xy', split_axis=3, concat_axis=2, tiled=True)  8.68 us
  transfers between devices with their start and end apart: 16, of which 4 were waited for; matrix products, arithmetic and copies ran while one was open for 0% of the time, Pallas kernels for 24%

profile of v1, /device:TPU:1, one launch (start us, length us, event | category | flops | bytes accessed | tf_op | source)
XLA Modules:
  0.0 143.7 jit_solution(7627990560660925704)
XLA Ops:
  0.0 1.4 copy.13
  1.5 2.1 %collective-permute-start = (bf16[64,8,8,4,4]{0,1,4,3,2:T(8,128)(2,1)S(1)}, bf16[64,8,8,4,4]{0,1,4,3,2:T(8,128)(2,1)S(1)}, u32[]{:S(2)}, u32[]{:S(2)}) collective-permute-start(bf16[64,8,8,4,4]{0,1,4,3,2:T(8,128)(2,1)S(1)} %dynamic-slice_bitcast_fusion.1), channel_id=1, source_target_pairs={{0,16},{16,0},{32,48},{48,32},{64,80},{80,64},{96,112},{112,96},{1... | collective-permute-start | bytes 393224 | tf_op jit(solution)/shard_map/ppermute | solution.py:223
  3.6 5.5 %collective-permute-done = bf16[64,8,8,4,4]{0,1,4,3,2:T(8,128)(2,1)S(1)} collective-permute-done((bf16[64,8,8,4,4]{0,1,4,3,2:T(8,128)(2,1)S(1)}, bf16[64,8,8,4,4]{0,1,4,3,2:T(8,128)(2,1)S(1)}, u32[]{:S(2)}, u32[]{:S(2)}) %collective-permute-start) | collective-permute-done | bytes 131104 | tf_op jit(solution)/shard_map/ppermute | solution.py:223
  10.4 9.8 %all-to-all-start = ((bf16[16,2,4096]{2,1,0:T(2,128)(2,1)}), bf16[16,2,4096]{2,1,0:T(2,128)(2,1)S(1)}, u32[]{:S(2)}, u32[]{:S(2)}) async-start(bf16[16,2,4096]{2,1,0:T(2,128)(2,1)} %reshape.42), calls=%async_computation | async-start | bytes 524288 | tf_op jit(solution)/shard_map/all_to_all | solution.py:244
  20.2 4.2 %prepare.1 = (bf16[64,64,256]{2,1,0:T(8,128)(2,1)}, f32[64,256]{1,0:T(8,128)}) custom-call(bf16[9,64,64,256]{3,2,1,0:T(8,128)(2,1)} %bitcast.41), custom_call_target="tpu_custom_call" | custom-call | flops 10000000 | bytes 4194304 | tf_op jit(solution)/shard_map/prepare/pallas_call | solution.py:72
  24.3 4.5 %all-to-all-done = bf16[16,2,4096]{2,1,0:T(2,128)(2,1)S(1)} async-done(((bf16[16,2,4096]{2,1,0:T(2,128)(2,1)}), bf16[16,2,4096]{2,1,0:T(2,128)(2,1)S(1)}, u32[]{:S(2)}, u32[]{:S(2)}) %all-to-all-start) | async-done | bytes 262176 | tf_op jit(solution)/shard_map/all_to_all | solution.py:244
  30.3 1.9 %start.1 = (f32[8,64,256]{2,1,0:T(8,128)}, bf16[8,64,256]{2,1,0:T(8,128)(2,1)}) custom-call(bf16[8,64,256]{2,1,0:T(8,128)(2,1)} %copy.15.source_ref, f32[64,256]{1,0:T(8,128)} %get-tuple-element.13.inverse_ref), custom_call_target="tpu_custom_call" | custom-call | tf_op jit(solution)/shard_map/start/pallas_call | solution.py:98
  32.2 1.2 collective-permute-start.4
  33.4 2.4 %collective-permute-start.3 = (bf16[8,64,256]{2,1,0:T(8,128)(2,1)}, bf16[8,64,256]{2,1,0:T(8,128)(2,1)S(1)}, u32[]{:S(2)}, u32[]{:S(2)}) collective-permute-start(bf16[8,64,256]{2,1,0:T(8,128)(2,1)} %get-tuple-element.14.rounded_ref), channel_id=1, source_target_pairs={{16,0},{32,16},{48,32},{64,48},{80,64},{96,80},{112,96},{0,112},{1... | collective-permute-start | bytes 786440 | tf_op jit(solution)/shard_map/ppermute | solution.py:219
  37.1 1.6 %copy-done = bf16[64,64,256]{2,1,0:T(8,128)(2,1)S(1)} copy-done((bf16[64,64,256]{2,1,0:T(8,128)(2,1)S(1)}, bf16[64,64,256]{2,1,0:T(8,128)(2,1)}, u32[]{:S(2)}) %copy-start) | copy-done | bytes 2097176
  42.5 10.1 %local.3.base_ref = f32[8,64,256]{2,1,0:T(8,128)S(1)} custom-call(bf16[64,64,256]{2,1,0:T(8,128)(2,1)S(1)} %copy-done, bf16[9,64,64,256]{3,2,1,0:T(8,128)(2,1)} %bitcast.42, bf16[8,64,256]{2,1,0:T(8,128)(2,1)S(1)} %copy-done.2, f32[8,64,256]{2,1,0:T(8,128)S(1)} %copy-done.6, bf16[8,64,256]{2,1,0:T(8,128)(2,1)S(1)} %copy-done.7, f32[64,256]{1,0:T(8,128)S(1)} %copy-done.4), custom_call_target="tpu_custom_call" | custom-call | flops 1000000000 | bytes 12582912 | tf_op jit(solution)/shard_map/local/pallas_call | solution.py:145
  52.7 8.0 %remote.3 = (f32[8,64,256]{2,1,0:T(8,128)S(1)}, bf16[8,64,256]{2,1,0:T(8,128)(2,1)S(1)}) custom-call(bf16[9,64,64,256]{3,2,1,0:T(8,128)(2,1)} %bitcast.43, bf16[8,64,256]{2,1,0:T(8,128)(2,1)S(1)} %collective-permute-done.1.above_ref, bf16[8,64,256]{2,1,0:T(8,128)(2,1)S(1)} %collective-permute-done.2.below_ref, ...), custom_call_target="tpu_custom_call" | custom-call | flops 1000000000 | bytes 12582912 | tf_op jit(solution)/shard_map/remote/pallas_call | solution.py:198
  60.8 3.6 %collective-permute-start.7 = (bf16[8,64,256]{2,1,0:T(8,128)(2,1)S(1)}, bf16[8,64,256]{2,1,0:T(8,128)(2,1)S(1)}, u32[]{:S(2)}, u32[]{:S(2)}) collective-permute-start(bf16[8,64,256]{2,1,0:T(8,128)(2,1)S(1)} %get-tuple-element.17.rounded_ref), channel_id=1, source_target_pairs={{16,0},{32,16},{48,32},{64,48},{80,64},{96,80},{112,96},{0,112},{1... | collective-permute-start | bytes 786440 | tf_op jit(solution)/shard_map/ppermute | solution.py:219
  64.4 1.4 collective-permute-start.6
  65.8 4.5 %collective-permute-start.5 = (bf16[8,64,256]{2,1,0:T(8,128)(2,1)S(1)}, bf16[8,64,256]{2,1,0:T(8,128)(2,1)S(1)}, u32[]{:S(2)}, u32[]{:S(2)}) collective-permute-start(bf16[8,64,256]{2,1,0:T(8,128)(2,1)S(1)} %get-tuple-element.17.rounded_ref), channel_id=1, source_target_pairs={{1,0},{2,1},{3,2},{4,3},{5,4},{6,5},{7,6},{8,7},{9,8},{10,9},{11,1... | collective-permute-start | bytes 786440 | tf_op jit(solution)/shard_map/ppermute | solution.py:219
  70.3 10.0 %local.4.base_ref = f32[8,64,256]{2,1,0:T(8,128)S(1)} custom-call(bf16[64,64,256]{2,1,0:T(8,128)(2,1)S(1)} %copy-done.1, bf16[9,64,64,256]{3,2,1,0:T(8,128)(2,1)} %bitcast.44, bf16[8,64,256]{2,1,0:T(8,128)(2,1)S(1)} %copy-done.3, f32[8,64,256]{2,1,0:T(8,128)S(1)} %get-tuple-element.18.iterate_ref, bf16[8,64,256]{2,1,0:T(8,128)(2,1)S(1)} %get-tuple-element.17.rounded_ref, ...), custom_call_target="tpu_custom_call" | custom-call | flops 1000000000 | bytes 12582912 | tf_op jit(solution)/shard_map/local/pallas_call | solution.py:145
  80.3 8.0 %remote.4 = (f32[8,64,256]{2,1,0:T(8,128)S(1)}, bf16[8,64,256]{2,1,0:T(8,128)(2,1)S(1)}) custom-call(bf16[9,64,64,256]{3,2,1,0:T(8,128)(2,1)} %bitcast.45, bf16[8,64,256]{2,1,0:T(8,128)(2,1)S(1)} %collective-permute-done.5.above_ref, bf16[8,64,256]{2,1,0:T(8,128)(2,1)S(1)} %collective-permute-done.6.below_ref, ...), custom_call_target="tpu_custom_call" | custom-call | flops 1000000000 | bytes 12582912 | tf_op jit(solution)/shard_map/remote/pallas_call | solution.py:198
  88.4 3.6 %collective-permute-start.11 = (bf16[8,64,256]{2,1,0:T(8,128)(2,1)S(1)}, bf16[8,64,256]{2,1,0:T(8,128)(2,1)S(1)}, u32[]{:S(2)}, u32[]{:S(2)}) collective-permute-start(bf16[8,64,256]{2,1,0:T(8,128)(2,1)S(1)} %get-tuple-element.19.rounded_ref), channel_id=1, source_target_pairs={{16,0},{32,16},{48,32},{64,48},{80,64},{96,80},{112,96},{0,112},{1... | collective-permute-start | bytes 786440 | tf_op jit(solution)/shard_map/ppermute | solution.py:219
  92.0 5.9 %collective-permute-start.9 = (bf16[8,64,256]{2,1,0:T(8,128)(2,1)S(1)}, bf16[8,64,256]{2,1,0:T(8,128)(2,1)S(1)}, u32[]{:S(2)}, u32[]{:S(2)}) collective-permute-start(bf16[8,64,256]{2,1,0:T(8,128)(2,1)S(1)} %get-tuple-element.19.rounded_ref), channel_id=1, source_target_pairs={{1,0},{2,1},{3,2},{4,3},{5,4},{6,5},{7,6},{8,7},{9,8},{10,9},{11,1... | collective-permute-start | bytes 786440 | tf_op jit(solution)/shard_map/ppermute | solution.py:219
  97.9 10.0 %local.5.base_ref = f32[8,64,256]{2,1,0:T(8,128)S(1)} custom-call(bf16[64,64,256]{2,1,0:T(8,128)(2,1)S(1)} %copy-done.1, bf16[9,64,64,256]{3,2,1,0:T(8,128)(2,1)} %bitcast.46, bf16[8,64,256]{2,1,0:T(8,128)(2,1)S(1)} %copy-done.3, f32[8,64,256]{2,1,0:T(8,128)S(1)} %get-tuple-element.20.iterate_ref, bf16[8,64,256]{2,1,0:T(8,128)(2,1)S(1)} %get-tuple-element.19.rounded_ref, ...), custom_call_target="tpu_custom_call" | custom-call | flops 1000000000 | bytes 12582912 | tf_op jit(solution)/shard_map/local/pallas_call | solution.py:145
  108.0 7.9 %remote.5 = bf16[8,64,256]{2,1,0:T(8,128)(2,1)S(1)} custom-call(bf16[9,64,64,256]{3,2,1,0:T(8,128)(2,1)} %bitcast.47, bf16[8,64,256]{2,1,0:T(8,128)(2,1)S(1)} %collective-permute-done.9.above_ref, bf16[8,64,256]{2,1,0:T(8,128)(2,1)S(1)} %collective-permute-done.10.below_ref, bf16[8,64,256]{2,1,0:T(8,128)(2,1)S(1)} %collective-permute-done.11.after_ref, ...), custom_call_target="tpu_custom_call" | custom-call | flops 1000000000 | bytes 12582912 | tf_op jit(solution)/shard_map/remote/pallas_call | solution.py:198
  117.4 8.7 %all-to-all-start.1 = ((bf16[16,2,4096]{2,1,0:T(2,128)(2,1)}), bf16[16,2,4096]{2,1,0:T(2,128)(2,1)S(1)}, u32[]{:S(2)}, u32[]{:S(2)}) async-start(bf16[16,2,4096]{2,1,0:T(2,128)(2,1)} %reshape.44), calls=%async_computation.1 | async-start | bytes 524288 | tf_op jit(solution)/shard_map/all_to_all | solution.py:266
  126.1 8.7 %all-to-all-done.1 = bf16[16,2,4096]{2,1,0:T(2,128)(2,1)S(1)} async-done(((bf16[16,2,4096]{2,1,0:T(2,128)(2,1)}), bf16[16,2,4096]{2,1,0:T(2,128)(2,1)S(1)}, u32[]{:S(2)}, u32[]{:S(2)}) %all-to-all-start.1) | async-done | bytes 262176 | tf_op jit(solution)/shard_map/all_to_all | solution.py:266
  135.3 7.0 %collective-permute-done.13 = bf16[64,8,8,4,4]{0,1,4,3,2:T(8,128)(2,1)S(1)} collective-permute-done((bf16[64,8,8,4,4]{0,1,4,3,2:T(8,128)(2,1)S(1)}, bf16[64,8,8,4,4]{0,1,4,3,2:T(8,128)(2,1)S(1)}, u32[]{:S(2)}, u32[]{:S(2)}) %collective-permute-start.13) | collective-permute-done | bytes 131104 | tf_op jit(solution)/shard_map/ppermute | solution.py:223
  (48 shorter events, 11.3 us)
Async XLA Ops:
  1.5 7.6 %collective-permute-start = (bf16[64,8,8,4,4]{0,1,4,3,2:T(8,128)(2,1)S(1)}, bf16[64,8,8,4,4]{0,1,4,3,2:T(8,128)(2,1)S(1)}, u32[]{:S(2)}, u32[]{:S(2)}) collective-permute-start(bf16[64,8,8,4,4]{0,1,4,3,2:T(8,128)(2,1)S(1)} %dynamic-slice_bitcast_fusion.1), channel_id=1, source_target_pairs={{0,16},{16,0},{32,48},{48,32},{64,80},{80,64},{96,112},{112,96},{1... | collective-permute-start | bytes 393224 | tf_op jit(solution)/shard_map/ppermute | solution.py:223
  10.4 18.5 %all-to-all-start = ((bf16[16,2,4096]{2,1,0:T(2,128)(2,1)}), bf16[16,2,4096]{2,1,0:T(2,128)(2,1)S(1)}, u32[]{:S(2)}, u32[]{:S(2)}) async-start(bf16[16,2,4096]{2,1,0:T(2,128)(2,1)} %reshape.42), calls=%async_computation | async-start | bytes 524288 | tf_op jit(solution)/shard_map/all_to_all | solution.py:244
  24.3 28.4 %copy-start.5 = (f32[64,256]{1,0:T(8,128)S(1)}, f32[64,256]{1,0:T(8,128)}, u32[]{:S(2)}) copy-start(f32[64,256]{1,0:T(8,128)} %get-tuple-element.13.inverse_ref) | copy-start | bytes 196612
  32.2 20.5 %collective-permute-start.4 = (bf16[8,64,256]{2,1,0:T(8,128)(2,1)}, bf16[8,64,256]{2,1,0:T(8,128)(2,1)S(1)}, u32[]{:S(2)}, u32[]{:S(2)}) collective-permute-start(bf16[8,64,256]{2,1,0:T(8,128)(2,1)} %get-tuple-element.14.rounded_ref), channel_id=1, source_target_pairs={{112,0},{0,16},{16,32},{32,48},{48,64},{64,80},{80,96},{96,112},{1... | collective-permute-start | bytes 786440 | tf_op jit(solution)/shard_map/ppermute | solution.py:219
  33.4 19.3 %collective-permute-start.3 = (bf16[8,64,256]{2,1,0:T(8,128)(2,1)}, bf16[8,64,256]{2,1,0:T(8,128)(2,1)S(1)}, u32[]{:S(2)}, u32[]{:S(2)}) collective-permute-start(bf16[8,64,256]{2,1,0:T(8,128)(2,1)} %get-tuple-element.14.rounded_ref), channel_id=1, source_target_pairs={{16,0},{32,16},{48,32},{64,48},{80,64},{96,80},{112,96},{0,112},{1... | collective-permute-start | bytes 786440 | tf_op jit(solution)/shard_map/ppermute | solution.py:219
  35.8 16.9 %collective-permute-start.2 = (bf16[8,64,256]{2,1,0:T(8,128)(2,1)}, bf16[8,64,256]{2,1,0:T(8,128)(2,1)S(1)}, u32[]{:S(2)}, u32[]{:S(2)}) collective-permute-start(bf16[8,64,256]{2,1,0:T(8,128)(2,1)} %get-tuple-element.14.rounded_ref), channel_id=1, source_target_pairs={{15,0},{0,1},{1,2},{2,3},{3,4},{4,5},{5,6},{6,7},{7,8},{8,9},{9,10... | collective-permute-start | bytes 786440 | tf_op jit(solution)/shard_map/ppermute | solution.py:219
  36.2 16.5 %collective-permute-start.1 = (bf16[8,64,256]{2,1,0:T(8,128)(2,1)}, bf16[8,64,256]{2,1,0:T(8,128)(2,1)S(1)}, u32[]{:S(2)}, u32[]{:S(2)}) collective-permute-start(bf16[8,64,256]{2,1,0:T(8,128)(2,1)} %get-tuple-element.14.rounded_ref), channel_id=1, source_target_pairs={{1,0},{2,1},{3,2},{4,3},{5,4},{6,5},{7,6},{8,7},{9,8},{10,9},{11,1... | collective-permute-start | bytes 786440 | tf_op jit(solution)/shard_map/ppermute | solution.py:219
  37.1 1.6 %copy-start = (bf16[64,64,256]{2,1,0:T(8,128)(2,1)S(1)}, bf16[64,64,256]{2,1,0:T(8,128)(2,1)}, u32[]{:S(2)}) copy-start(bf16[64,64,256]{2,1,0:T(8,128)(2,1)} %get-tuple-element.15.off_ref) | copy-start | bytes 6291460
  38.7 0.9 copy-start.2
  39.7 0.8 copy-start.4
  40.5 1.0 copy-start.6
  41.6 0.9 copy-start.7
  42.5 27.8 %copy-start.1 = (bf16[64,64,256]{2,1,0:T(8,128)(2,1)S(1)}, bf16[64,64,256]{2,1,0:T(8,128)(2,1)}, u32[]{:S(2)}) copy-start(bf16[64,64,256]{2,1,0:T(8,128)(2,1)} %get-tuple-element.15.off_ref) | copy-start | bytes 6291460
  42.5 27.8 %copy-start.3 = (bf16[8,64,256]{2,1,0:T(8,128)(2,1)S(1)}, bf16[8,64,256]{2,1,0:T(8,128)(2,1)}, u32[]{:S(2)}) copy-start(bf16[8,64,256]{2,1,0:T(8,128)(2,1)} %copy.15.source_ref) | copy-start | bytes 786436
  60.7 19.6 %collective-permute-start.8 = (bf16[8,64,256]{2,1,0:T(8,128)(2,1)S(1)}, bf16[8,64,256]{2,1,0:T(8,128)(2,1)S(1)}, u32[]{:S(2)}, u32[]{:S(2)}) collective-permute-start(bf16[8,64,256]{2,1,0:T(8,128)(2,1)S(1)} %get-tuple-element.17.rounded_ref), channel_id=1, source_target_pairs={{112,0},{0,16},{16,32},{32,48},{48,64},{64,80},{80,96},{96,112},{1... | collective-permute-start | bytes 786440 | tf_op jit(solution)/shard_map/ppermute | solution.py:219
  60.8 19.5 %collective-permute-start.7 = (bf16[8,64,256]{2,1,0:T(8,128)(2,1)S(1)}, bf16[8,64,256]{2,1,0:T(8,128)(2,1)S(1)}, u32[]{:S(2)}, u32[]{:S(2)}) collective-permute-start(bf16[8,64,256]{2,1,0:T(8,128)(2,1)S(1)} %get-tuple-element.17.rounded_ref), channel_id=1, source_target_pairs={{16,0},{32,16},{48,32},{64,48},{80,64},{96,80},{112,96},{0,112},{1... | collective-permute-start | bytes 786440 | tf_op jit(solution)/shard_map/ppermute | solution.py:219
  64.4 16.0 %collective-permute-start.6 = (bf16[8,64,256]{2,1,0:T(8,128)(2,1)S(1)}, bf16[8,64,256]{2,1,0:T(8,128)(2,1)S(1)}, u32[]{:S(2)}, u32[]{:S(2)}) collective-permute-start(bf16[8,64,256]{2,1,0:T(8,128)(2,1)S(1)} %get-tuple-element.17.rounded_ref), channel_id=1, source_target_pairs={{15,0},{0,1},{1,2},{2,3},{3,4},{4,5},{5,6},{6,7},{7,8},{8,9},{9,10... | collective-permute-start | bytes 786440 | tf_op jit(solution)/shard_map/ppermute | solution.py:219
  65.8 14.6 %collective-permute-start.5 = (bf16[8,64,256]{2,1,0:T(8,128)(2,1)S(1)}, bf16[8,64,256]{2,1,0:T(8,128)(2,1)S(1)}, u32[]{:S(2)}, u32[]{:S(2)}) collective-permute-start(bf16[8,64,256]{2,1,0:T(8,128)(2,1)S(1)} %get-tuple-element.17.rounded_ref), channel_id=1, source_target_pairs={{1,0},{2,1},{3,2},{4,3},{5,4},{6,5},{7,6},{8,7},{9,8},{10,9},{11,1... | collective-permute-start | bytes 786440 | tf_op jit(solution)/shard_map/ppermute | solution.py:219
  88.4 19.6 %collective-permute-start.12 = (bf16[8,64,256]{2,1,0:T(8,128)(2,1)S(1)}, bf16[8,64,256]{2,1,0:T(8,128)(2,1)S(1)}, u32[]{:S(2)}, u32[]{:S(2)}) collective-permute-start(bf16[8,64,256]{2,1,0:T(8,128)(2,1)S(1)} %get-tuple-element.19.rounded_ref), channel_id=1, source_target_pairs={{112,0},{0,16},{16,32},{32,48},{48,64},{64,80},{80,96},{96,112},{1... | collective-permute-start | bytes 786440 | tf_op jit(solution)/shard_map/ppermute | solution.py:219
  88.4 19.5 %collective-permute-start.11 = (bf16[8,64,256]{2,1,0:T(8,128)(2,1)S(1)}, bf16[8,64,256]{2,1,0:T(8,128)(2,1)S(1)}, u32[]{:S(2)}, u32[]{:S(2)}) collective-permute-start(bf16[8,64,256]{2,1,0:T(8,128)(2,1)S(1)} %get-tuple-element.19.rounded_ref), channel_id=1, source_target_pairs={{16,0},{32,16},{48,32},{64,48},{80,64},{96,80},{112,96},{0,112},{1... | collective-permute-start | bytes 786440 | tf_op jit(solution)/shard_map/ppermute | solution.py:219
  92.0 15.9 %collective-permute-start.10 = (bf16[8,64,256]{2,1,0:T(8,128)(2,1)S(1)}, bf16[8,64,256]{2,1,0:T(8,128)(2,1)S(1)}, u32[]{:S(2)}, u32[]{:S(2)}) collective-permute-start(bf16[8,64,256]{2,1,0:T(8,128)(2,1)S(1)} %get-tuple-element.19.rounded_ref), channel_id=1, source_target_pairs={{15,0},{0,1},{1,2},{2,3},{3,4},{4,5},{5,6},{6,7},{7,8},{8,9},{9,10... | collective-permute-start | bytes 786440 | tf_op jit(solution)/shard_map/ppermute | solution.py:219
  92.0 16.0 %collective-permute-start.9 = (bf16[8,64,256]{2,1,0:T(8,128)(2,1)S(1)}, bf16[8,64,256]{2,1,0:T(8,128)(2,1)S(1)}, u32[]{:S(2)}, u32[]{:S(2)}) collective-permute-start(bf16[8,64,256]{2,1,0:T(8,128)(2,1)S(1)} %get-tuple-element.19.rounded_ref), channel_id=1, source_target_pairs={{1,0},{2,1},{3,2},{4,3},{5,4},{6,5},{7,6},{8,7},{9,8},{10,9},{11,1... | collective-permute-start | bytes 786440 | tf_op jit(solution)/shard_map/ppermute | solution.py:219
  117.4 17.4 %all-to-all-start.1 = ((bf16[16,2,4096]{2,1,0:T(2,128)(2,1)}), bf16[16,2,4096]{2,1,0:T(2,128)(2,1)S(1)}, u32[]{:S(2)}, u32[]{:S(2)}) async-start(bf16[16,2,4096]{2,1,0:T(2,128)(2,1)} %reshape.44), calls=%async_computation.1 | async-start | bytes 524288 | tf_op jit(solution)/shard_map/all_to_all | solution.py:266
  135.2 7.1 %collective-permute-start.13 = (bf16[64,8,8,4,4]{0,1,4,3,2:T(8,128)(2,1)S(1)}, bf16[64,8,8,4,4]{0,1,4,3,2:T(8,128)(2,1)S(1)}, u32[]{:S(2)}, u32[]{:S(2)}) collective-permute-start(bf16[64,8,8,4,4]{0,1,4,3,2:T(8,128)(2,1)S(1)} %dynamic-slice_bitcast_fusion), channel_id=1, source_target_pairs={{0,16},{16,0},{32,48},{48,32},{64,80},{80,64},{96,112},{112,96},{1... | collective-permute-start | bytes 393224 | tf_op jit(solution)/shard_map/ppermute | solution.py:223

commit v2 on v1

--- a/solution.py
+++ b/solution.py
@@ -86,20 +86,111 @@
     )(stencil)
 
 
-def start_kernel(source_ref, inverse_ref, iterate_ref, rounded_ref):
+def one_hot(index, size):
+    column = lax.broadcasted_iota(jnp.int32, (size, size), 1)
+    return jnp.where(column == index, 1.0, 0.0).astype(BF16)
+
+
+def fine_order(sites):
+    place = lax.broadcasted_iota(jnp.int32, (sites, sites), 0)
+    u, w, g, h = place // 64, place // 16 % 4, place // 4 % 4, place % 4
+    return u * 64 + g * 16 + w * 4 + h
+
+
+def split_kernel(fine_ref, out_ref):
+    rows, sites = fine_ref.shape
+    _, _, planes, cells, _ = out_ref.shape
+    unit = one_hot(lax.broadcasted_iota(jnp.int32, (sites, sites), 0), sites)
+    turned = lax.dot_general(unit, fine_ref[...], (((1,), (1,)), ((), ())), preferred_element_type=F32)
+    turned = turned.astype(BF16).reshape(2, planes, cells, rows)
+    for half in range(2):
+        out_ref[:, half] = turned
+
+
+def split(fine, planes, cells):
+    rows, _ = fine.shape
+    return pl.pallas_call(
+        split_kernel,
+        out_shape=jax.ShapeDtypeStruct((2, 2, planes, cells, rows), BF16),
+        name="split",
+    )(fine)
+
+
+def start_kernel(received_ref, inverse_ref, source_ref, iterate_ref, rounded_ref, turned_ref):
+    count, components, sites = rounded_ref.shape
+    half = lax.axis_index("xy") // (lax.axis_size("xy") // 2)
+    order = one_hot(fine_order(sites), sites)
+    turned = lax.dot_general(
+        received_ref[half], order, (((0,), (0,)), ((), ())), preferred_element_type=F32
+    )
+    for i in range(sites // LANES):
+        turned_ref[i] = turned[:, i * LANES : (i + 1) * LANES]
     inverse = inverse_ref[...]
-    for r in range(source_ref.shape[0]):
-        iterate = source_ref[r].astype(F32) * inverse
+    for r in range(count):
+        source = jnp.concatenate(
+            [turned_ref[i, pl.ds(r, components, stride=count), :] for i in range(sites // LANES)], axis=1
+        )
+        iterate = source * inverse
+        source_ref[r] = source.astype(BF16)
         iterate_ref[r] = iterate
         rounded_ref[r] = iterate.astype(BF16)
 
 
-def start(source, inverse):
+def start(received, inverse):
+    _, sites, rows = received.shape
+    components = inverse.shape[0]
+    shape = (rows // components, components, sites)
     return pl.pallas_call(
         start_kernel,
-        out_shape=[jax.ShapeDtypeStruct(source.shape, F32), jax.ShapeDtypeStruct(source.shape, BF16)],
+        out_shape=[jax.ShapeDtypeStruct(shape, t) for t in (BF16, F32, BF16)],
+        scratch_shapes=[pltpu.VMEM((sites // LANES, rows, LANES), F32)],
         name="start",
-    )(source, inverse)
+    )(received, inverse)
+
+
+def leave_kernel(rounded_ref, out_ref, mixed_ref):
+    count, components, sites = rounded_ref.shape
+    _, columns, cells, rows = out_ref.shape
+    for r in range(count):
+        value = rounded_ref[r].astype(F32)
+        for i in range(sites // LANES):
+            mixed_ref[i, pl.ds(r, components, stride=count), :] = value[:, i * LANES : (i + 1) * LANES]
+    mixed = jnp.concatenate([mixed_ref[i].astype(BF16) for i in range(sites // LANES)], axis=1)
+    order = one_hot(fine_order(sites), sites)
+    turned = lax.dot_general(order, mixed, (((1,), (1,)), ((), ())), preferred_element_type=F32)
+    turned = turned.astype(BF16).reshape(columns, cells, rows)
+    for half in range(2):
+        out_ref[half] = turned
+
+
+def leave(rounded, columns):
+    count, components, sites = rounded.shape
+    rows = count * components
+    return pl.pallas_call(
+        leave_kernel,
+        out_shape=jax.ShapeDtypeStruct((2, columns, sites // columns, rows), BF16),
+        scratch_shapes=[pltpu.VMEM((sites // LANES, rows, LANES), F32)],
+        name="leave",
+    )(rounded)
+
+
+def join_kernel(received_ref, out_ref):
+    places = received_ref.shape[2]
+    half = lax.axis_index("zt") % 2
+    unit = one_hot(lax.broadcasted_iota(jnp.int32, (places, places), 0), places)
+    for e in range(2):
+        out_ref[:, places * e : places * (e + 1)] = lax.dot_general(
+            received_ref[e, half], unit, (((0,), (0,)), ((), ())), preferred_element_type=F32
+        )
+
+
+def join(received):
+    _, _, places, rows = received.shape
+    return pl.pallas_call(
+        join_kernel,
+        out_shape=jax.ShapeDtypeStruct((rows, 2 * places), F32),
+        name="join",
+    )(received)
 
 
 def local_kernel(off_ref, hops_ref, source_ref, iterate_ref, rounded_ref, inverse_ref, base_ref, near_ref, partial_ref):
@@ -166,7 +257,7 @@
     )(off, stencil, source, iterate, rounded, inverse)
 
 
-def remote_kernel(last, hops_ref, above_ref, below_ref, after_ref, earlier_ref, base_ref, inverse_ref, *rest):
+def remote_kernel(last, hops_ref, z0_ref, z1_ref, t0_ref, t1_ref, base_ref, inverse_ref, *rest):
     if last:
         rounded_ref, partial_ref = rest
     else:
@@ -175,8 +266,10 @@
     def sixteen(i):
         return slice(16 * i, 16 * i + 16)
 
+    z_odd = lax.axis_index("xy") % 2
+    t_odd = lax.axis_index("zt") % 2
     blocks, vectors = [], []
-    for k, ref in enumerate((above_ref, below_ref, after_ref, earlier_ref)):
+    for k, ref in ((z_odd, z0_ref), (1 - z_odd, z1_ref), (2 + t_odd, t0_ref), (3 - t_odd, t1_ref)):
         blocks.append(lambda o, i, k=k: hops_ref[k, o, sixteen(i), :])
         vectors.append(lambda r, i, ref=ref: ref[r, sixteen(i), :])
 
@@ -214,45 +307,43 @@
     )(stencil, *halos, base, inverse)
 
 
-def neighbour(plane, axis, step):
+def pairs(plane, axis, first):
     count = lax.axis_size(axis)
-    return lax.ppermute(plane, axis, [((i + step) % count, i) for i in range(count)])
-
-
-def partner(shard, axis):
-    return lax.ppermute(shard, axis, [(i, i ^ 1) for i in range(lax.axis_size(axis))])
+    swaps = []
+    for i in range(first, first + count, 2):
+        a, b = i % count, (i + 1) % count
+        swaps += [(a, b), (b, a)]
+    return lax.ppermute(plane, axis, swaps)
+
+
+def groups():
+    columns = lax.axis_size("xy")
+    return [list(range(i * columns, (i + 2) * columns)) for i in range(0, lax.axis_size("zt"), 2)]
+
+
+def exchange(chunks):
+    return lax.all_to_all(chunks, ("zt", "xy"), 0, 0, axis_index_groups=groups(), tiled=True)
 
 
 def shards(restricted, stencil):
     columns = lax.axis_size("xy")
-    parts = columns // 4
     planes = columns // 2
-    width = LX // parts
-    height = LY // 4
-    components, count = restricted.shape[2], restricted.shape[3]
-    parity = lax.axis_index("zt") % 2
+    components, count, sites = restricted.shape[2:]
+    rows = components * count
+    cells = sites // columns
     stencil = stencil[0, 0]
     off, inverse = prepare(stencil)
 
-    pieces = restricted[0, 0].reshape(components, count, 2, planes, height, width)
-    kept = lax.dynamic_index_in_dim(pieces, parity, 2, keepdims=False)
-    outgoing = lax.dynamic_index_in_dim(pieces, 1 - parity, 2, keepdims=False)
-    incoming = partner(outgoing, "zt")
-    lower = jnp.where(parity == 0, kept, incoming)
-    upper = jnp.where(parity == 0, incoming, kept)
-    column = jnp.concatenate([lower, upper], axis=2)[:, :, :, None]
-    spread = lax.all_to_all(column, "xy", split_axis=2, concat_axis=3, tiled=True)
-    spread = spread.reshape(components, count, 4, parts, height, width)
-    source = spread.transpose(1, 0, 2, 4, 3, 5).reshape(count, components, LY * LX)
-
-    iterate, rounded = start(source, inverse)
+    chunks = split(restricted.reshape(rows, sites), planes, cells)
+    received = exchange(chunks.reshape(2 * columns, cells, rows))
+    source, iterate, rounded = start(received.reshape(2, sites, rows), inverse)
     for sweep in range(SWEEPS - 1):
         last = sweep == SWEEPS - 2
         halos = [
-            neighbour(rounded, "xy", 1),
-            neighbour(rounded, "xy", -1),
-            neighbour(rounded, "zt", 1),
-            neighbour(rounded, "zt", -1),
+            pairs(rounded, "xy", 0),
+            pairs(rounded, "xy", 1),
+            pairs(rounded, "zt", 0),
+            pairs(rounded, "zt", 1),
         ]
         base = local(off, stencil, source, iterate, rounded, inverse)
         results = remote(stencil, halos, base, inverse, last)
@@ -261,16 +352,10 @@
         else:
             iterate, rounded = results
 
-    regrouped = rounded.reshape(count, components, 4, height, parts, width)
-    regrouped = regrouped.transpose(1, 0, 2, 4, 3, 5).reshape(components, count, 1, columns, height, width)
-    returned = lax.all_to_all(regrouped, "xy", split_axis=3, concat_axis=2, tiled=True)[:, :, :, 0]
-    own = lax.dynamic_slice_in_dim(returned, parity * planes, planes, 2)
-    other = lax.dynamic_slice_in_dim(returned, (1 - parity) * planes, planes, 2)
-    other = partner(other, "zt")
-    first = jnp.where(parity == 0, own, other)
-    second = jnp.where(parity == 0, other, own)
-    result = jnp.stack([first, second], axis=2).astype(F32)
-    return result.reshape(1, 1, components, count, 2 * planes * height * width)
+    chunks = leave(rounded, columns)
+    received = exchange(chunks.reshape(2 * columns, cells, rows))
+    result = join(received.reshape(2, 2, planes * cells, rows))
+    return result.reshape(1, 1, components, count, sites)
 
 
 def solution(mesh):

time: 145 us -> 127 us (0.88)
  starting transfers between devices: 44.7 us -> 24.6 us
  blocking collectives: 0 us -> 19.6 us
  waiting for transfers between devices: 25.8 us -> 8.42 us
  Pallas kernels: 60.1 us -> 67 us
  local copies, waits for them, and re-layouts: 12.4 us -> 6.86 us
    all_to_all x0 -> x1, blocking collectives: none -> 19.6 us  [exchange(): lax.all_to_all(chunks, ('zt', 'xy'), 0, 0, axis_index_groups=groups(), ti...]
    ppermute x14 -> x12, waiting for transfers between devices: 12.5 us -> 0.03 us  [pairs(): return lax.ppermute(plane, axis, swaps)]
    ppermute x14 -> x12, starting transfers between devices: 26.3 us -> 14.2 us  [pairs(): return lax.ppermute(plane, axis, swaps)]
    all_to_all x2 -> x1, starting transfers between devices: 18.5 us -> 10.4 us  [exchange(): lax.all_to_all(chunks, ('zt', 'xy'), 0, 0, axis_index_groups=groups(), ti...]
    pallas_call x1 -> x4, Pallas kernels: 1.89 us -> 8.59 us  [the longest x1 2.4 us: start(): pl.pallas_call(start_kernel, out_shape=[jax.ShapeDtypeStruct(shape, t) fo...]
    all_to_all x2 -> x1, waiting for transfers between devices: 13.3 us -> 8.39 us  [exchange(): lax.all_to_all(chunks, ('zt', 'xy'), 0, 0, axis_index_groups=groups(), ti...]
    unnamed x21 -> x20, local copies, waits for them, and re-layouts: 9.72 us -> 6.86 us
  transfers between devices with their start and end apart: 16 -> 13, of which waited for: 4 -> 1; matrix products, arithmetic and copies ran while one was open for 0% -> 0% of each run, Pallas kernels for 24% -> 27%
where the time goes in v2:
time: 127 us
  Pallas kernels  67 us (53%)
  starting transfers between devices  24.6 us (19%)
  blocking collectives  19.6 us (15%)
  waiting for transfers between devices  8.42 us (7%)
  local copies, waits for them, and re-layouts  6.86 us (5%)
    pallas_call x3, Pallas kernels, local(): pl.pallas_call(local_kernel, grid=(components // ROWS,), in_specs=[pl.Blo...  30.1 us
    pallas_call x3, Pallas kernels, remote(): pl.pallas_call(functools.partial(remote_kernel, last), grid=(components /...  24.1 us
    all_to_all x1, blocking collectives, exchange(): lax.all_to_all(chunks, ('zt', 'xy'), 0, 0, axis_index_groups=groups(), ti...  19.6 us
    ppermute x12, starting transfers between devices, pairs(): return lax.ppermute(plane, axis, swaps)  14.2 us
    all_to_all x1, starting transfers between devices, exchange(): lax.all_to_all(chunks, ('zt', 'xy'), 0, 0, axis_index_groups=groups(), ti...  10.4 us
    all_to_all x1, waiting for transfers between devices, exchange(): lax.all_to_all(chunks, ('zt', 'xy'), 0, 0, axis_index_groups=groups(), ti...  8.39 us
    unnamed x20, local copies, waits for them, and re-layouts  6.86 us
    pallas_call x1, Pallas kernels, prepare(): pl.pallas_call(prepare_kernel, grid=(components // ROWS,), in_specs=[pl.B...  4.14 us
  transfers between devices with their start and end apart: 13, of which 1 were waited for; matrix products, arithmetic and copies ran while one was open for 0% of the time, Pallas kernels for 27%

profile of v2, /device:TPU:1, one launch (start us, length us, event | category | flops | bytes accessed | tf_op | source)
XLA Modules:
  0.0 126.7 jit_solution(8170920960549078986)
XLA Ops:
  0.0 2.0 %split.1 = bf16[2,2,8,16,512]{4,3,2,1,0:T(8,128)(2,1)} custom-call(bf16[512,256]{1,0:T(8,128)(2,1)} %bitcast.18), custom_call_target="tpu_custom_call" | custom-call | tf_op jit(solution)/shard_map/split/pallas_call | solution.py:112
  2.0 10.4 %all-to-all-start = ((bf16[32,16,512]{2,1,0:T(8,128)(2,1)}), bf16[32,16,512]{2,1,0:T(8,128)(2,1)S(1)}, u32[]{:S(2)}, u32[]{:S(2)}) async-start(bf16[32,16,512]{2,1,0:T(8,128)(2,1)} %bitcast.15), calls=%async_computation | async-start | bytes 1048576 | tf_op jit(solution)/shard_map/all_to_all | solution.py:325
  12.4 4.1 %prepare.1 = (bf16[64,64,256]{2,1,0:T(8,128)(2,1)}, f32[64,256]{1,0:T(8,128)}) custom-call(bf16[9,64,64,256]{3,2,1,0:T(8,128)(2,1)} %bitcast.7), custom_call_target="tpu_custom_call" | custom-call | flops 10000000 | bytes 4194304 | tf_op jit(solution)/shard_map/prepare/pallas_call | solution.py:72
  16.5 8.4 %all-to-all-done = bf16[32,16,512]{2,1,0:T(8,128)(2,1)S(1)} async-done(((bf16[32,16,512]{2,1,0:T(8,128)(2,1)}), bf16[32,16,512]{2,1,0:T(8,128)(2,1)S(1)}, u32[]{:S(2)}, u32[]{:S(2)}) %all-to-all-start) | async-done | bytes 524320 | tf_op jit(solution)/shard_map/all_to_all | solution.py:325
  25.7 2.4 %start.1 = (bf16[8,64,256]{2,1,0:T(8,128)(2,1)}, f32[8,64,256]{2,1,0:T(8,128)}, bf16[8,64,256]{2,1,0:T(8,128)(2,1)}) custom-call(bf16[2,256,512]{2,1,0:T(8,128)(2,1)} %bitcast.14, f32[64,256]{1,0:T(8,128)} %get-tuple-element.14.inverse_ref), custom_call_target="tpu_custom_call" | custom-call | tf_op jit(solution)/shard_map/start/pallas_call | solution.py:143
  28.1 2.2 %collective-permute-start.3 = (bf16[8,64,256]{2,1,0:T(8,128)(2,1)}, bf16[8,64,256]{2,1,0:T(8,128)(2,1)S(1)}, u32[]{:S(2)}, u32[]{:S(2)}) collective-permute-start(bf16[8,64,256]{2,1,0:T(8,128)(2,1)} %get-tuple-element.15.rounded_ref), channel_id=1, source_target_pairs={{16,32},{32,16},{48,64},{64,48},{80,96},{96,80},{112,0},{0,112},{1... | collective-permute-start | bytes 786440 | tf_op jit(solution)/shard_map/ppermute | solution.py:316
  31.2 1.1 collective-permute-start
  32.3 1.6 %copy-done = bf16[64,64,256]{2,1,0:T(8,128)(2,1)S(1)} copy-done((bf16[64,64,256]{2,1,0:T(8,128)(2,1)S(1)}, bf16[64,64,256]{2,1,0:T(8,128)(2,1)}, u32[]{:S(2)}) %copy-start) | copy-done | bytes 2097176
  34.8 0.9 copy-done.4
  35.7 1.0 copy-done.7
  36.8 0.9 copy-done.8
  37.7 10.1 %local.3.base_ref = f32[8,64,256]{2,1,0:T(8,128)S(1)} custom-call(bf16[64,64,256]{2,1,0:T(8,128)(2,1)S(1)} %copy-done, bf16[9,64,64,256]{3,2,1,0:T(8,128)(2,1)} %bitcast.8, bf16[8,64,256]{2,1,0:T(8,128)(2,1)S(1)} %copy-done.4, f32[8,64,256]{2,1,0:T(8,128)S(1)} %copy-done.7, bf16[8,64,256]{2,1,0:T(8,128)(2,1)S(1)} %copy-done.8, f32[64,256]{1,0:T(8,128)S(1)} %copy-done.2), custom_call_target="tpu_custom_call" | custom-call | flops 1000000000 | bytes 12582912 | tf_op jit(solution)/shard_map/local/pallas_call | solution.py:236
  47.9 8.1 %remote.3 = (f32[8,64,256]{2,1,0:T(8,128)S(1)}, bf16[8,64,256]{2,1,0:T(8,128)(2,1)S(1)}) custom-call(bf16[9,64,64,256]{3,2,1,0:T(8,128)(2,1)} %bitcast.9, bf16[8,64,256]{2,1,0:T(8,128)(2,1)S(1)} %collective-permute-done.z0_ref, bf16[8,64,256]{2,1,0:T(8,128)(2,1)S(1)} %collective-permute-done.1.z1_ref, bf16[8,64,256]{2,1,0:T(8,128)(2,1)S(1)} %collective-permute-done.2.t0_ref, ...), custom_call_target="tpu_custom_call" | custom-call | flops 1000000000 | bytes 12582912 | tf_op jit(solution)/shard_map/remote/pallas_call | solution.py:291
  56.5 1.4 %collective-permute-start.6 = (bf16[8,64,256]{2,1,0:T(8,128)(2,1)S(1)}, bf16[8,64,256]{2,1,0:T(8,128)(2,1)S(1)}, u32[]{:S(2)}, u32[]{:S(2)}) collective-permute-start(bf16[8,64,256]{2,1,0:T(8,128)(2,1)S(1)} %get-tuple-element.19.rounded_ref), channel_id=1, source_target_pairs={{0,16},{16,0},{32,48},{48,32},{64,80},{80,64},{96,112},{112,96},{1... | collective-permute-start | bytes 786440 | tf_op jit(solution)/shard_map/ppermute | solution.py:316
  58.2 3.9 %collective-permute-start.4 = (bf16[8,64,256]{2,1,0:T(8,128)(2,1)S(1)}, bf16[8,64,256]{2,1,0:T(8,128)(2,1)S(1)}, u32[]{:S(2)}, u32[]{:S(2)}) collective-permute-start(bf16[8,64,256]{2,1,0:T(8,128)(2,1)S(1)} %get-tuple-element.19.rounded_ref), channel_id=1, source_target_pairs={{0,1},{1,0},{2,3},{3,2},{4,5},{5,4},{6,7},{7,6},{8,9},{9,8},{10,11... | collective-permute-start | bytes 786440 | tf_op jit(solution)/shard_map/ppermute | solution.py:316
  62.0 10.0 %local.4.base_ref = f32[8,64,256]{2,1,0:T(8,128)S(1)} custom-call(bf16[64,64,256]{2,1,0:T(8,128)(2,1)S(1)} %copy-done.1, bf16[9,64,64,256]{3,2,1,0:T(8,128)(2,1)} %bitcast.10, bf16[8,64,256]{2,1,0:T(8,128)(2,1)S(1)} %copy-done.5, f32[8,64,256]{2,1,0:T(8,128)S(1)} %get-tuple-element.20.iterate_ref, bf16[8,64,256]{2,1,0:T(8,128)(2,1)S(1)} %get-tuple-element.19.rounded_ref, ...), custom_call_target="tpu_custom_call" | custom-call | flops 1000000000 | bytes 12582912 | tf_op jit(solution)/shard_map/local/pallas_call | solution.py:236
  72.1 8.1 %remote.4 = (f32[8,64,256]{2,1,0:T(8,128)S(1)}, bf16[8,64,256]{2,1,0:T(8,128)(2,1)S(1)}) custom-call(bf16[9,64,64,256]{3,2,1,0:T(8,128)(2,1)} %bitcast.11, bf16[8,64,256]{2,1,0:T(8,128)(2,1)S(1)} %collective-permute-done.4.z0_ref, bf16[8,64,256]{2,1,0:T(8,128)(2,1)S(1)} %collective-permute-done.5.z1_ref, ...), custom_call_target="tpu_custom_call" | custom-call | flops 1000000000 | bytes 12582912 | tf_op jit(solution)/shard_map/remote/pallas_call | solution.py:291
  80.2 2.0 %collective-permute-start.11 = (bf16[8,64,256]{2,1,0:T(8,128)(2,1)S(1)}, bf16[8,64,256]{2,1,0:T(8,128)(2,1)S(1)}, u32[]{:S(2)}, u32[]{:S(2)}) collective-permute-start(bf16[8,64,256]{2,1,0:T(8,128)(2,1)S(1)} %get-tuple-element.21.rounded_ref), channel_id=1, source_target_pairs={{16,32},{32,16},{48,64},{64,48},{80,96},{96,80},{112,0},{0,112},{1... | collective-permute-start | bytes 786440 | tf_op jit(solution)/shard_map/ppermute | solution.py:316
  83.0 1.2 collective-permute-start.8
  84.2 10.0 %local.5.base_ref = f32[8,64,256]{2,1,0:T(8,128)S(1)} custom-call(bf16[64,64,256]{2,1,0:T(8,128)(2,1)S(1)} %copy-done.1, bf16[9,64,64,256]{3,2,1,0:T(8,128)(2,1)} %bitcast.12, bf16[8,64,256]{2,1,0:T(8,128)(2,1)S(1)} %copy-done.5, f32[8,64,256]{2,1,0:T(8,128)S(1)} %get-tuple-element.22.iterate_ref, bf16[8,64,256]{2,1,0:T(8,128)(2,1)S(1)} %get-tuple-element.21.rounded_ref, ...), custom_call_target="tpu_custom_call" | custom-call | flops 1000000000 | bytes 12582912 | tf_op jit(solution)/shard_map/local/pallas_call | solution.py:236
  94.2 8.0 %remote.5.rounded_ref = bf16[8,64,256]{2,1,0:T(8,128)(2,1)S(1)} custom-call(bf16[9,64,64,256]{3,2,1,0:T(8,128)(2,1)} %bitcast.13, bf16[8,64,256]{2,1,0:T(8,128)(2,1)S(1)} %collective-permute-done.8.z0_ref, bf16[8,64,256]{2,1,0:T(8,128)(2,1)S(1)} %collective-permute-done.9.z1_ref, bf16[8,64,256]{2,1,0:T(8,128)(2,1)S(1)} %collective-permute-done.10.t0_ref, ...), custom_call_target="tpu_custom_call" | custom-call | flops 1000000000 | bytes 12582912 | tf_op jit(solution)/shard_map/remote/pallas_call | solution.py:291
  102.9 2.1 %leave.1 = bf16[2,16,16,512]{3,2,1,0:T(8,128)(2,1)} custom-call(bf16[8,64,256]{2,1,0:T(8,128)(2,1)} %copy-done.6), custom_call_target="tpu_custom_call" | custom-call | tf_op jit(solution)/shard_map/leave/pallas_call | solution.py:169
  104.9 19.6 %all_to_all.10 = bf16[32,16,512]{2,1,0:T(8,128)(2,1)} all-to-all(bf16[32,16,512]{2,1,0:T(8,128)(2,1)} %bitcast.16), channel_id=1, replica_groups={{0,1,2,3,4,5,6,7,8,9,10,11,12,13,14,15,16,17,18,19,20,21,22,23,24,25,26..., dimensions={0} | all-to-all | bytes 1048576 | tf_op jit(solution)/shard_map/all_to_all | solution.py:325
  124.5 2.1 %join.1 = f32[512,256]{1,0:T(8,128)} custom-call(bf16[2,2,128,512]{3,2,1,0:T(8,128)(2,1)} %bitcast.17), custom_call_target="tpu_custom_call" | custom-call | tf_op jit(solution)/shard_map/join/pallas_call | solution.py:189
  (34 shorter events, 4.8 us)
Async XLA Ops:
  2.0 22.9 %all-to-all-start = ((bf16[32,16,512]{2,1,0:T(8,128)(2,1)}), bf16[32,16,512]{2,1,0:T(8,128)(2,1)S(1)}, u32[]{:S(2)}, u32[]{:S(2)}) async-start(bf16[32,16,512]{2,1,0:T(8,128)(2,1)} %bitcast.15), calls=%async_computation | async-start | bytes 1048576 | tf_op jit(solution)/shard_map/all_to_all | solution.py:325
  16.5 31.4 %copy-start.3 = (f32[64,256]{1,0:T(8,128)S(1)}, f32[64,256]{1,0:T(8,128)}, u32[]{:S(2)}) copy-start(f32[64,256]{1,0:T(8,128)} %get-tuple-element.14.inverse_ref) | copy-start | bytes 196612
  24.9 0.8 copy-start.9
  28.1 19.8 %collective-permute-start.3 = (bf16[8,64,256]{2,1,0:T(8,128)(2,1)}, bf16[8,64,256]{2,1,0:T(8,128)(2,1)S(1)}, u32[]{:S(2)}, u32[]{:S(2)}) collective-permute-start(bf16[8,64,256]{2,1,0:T(8,128)(2,1)} %get-tuple-element.15.rounded_ref), channel_id=1, source_target_pairs={{16,32},{32,16},{48,64},{64,48},{80,96},{96,80},{112,0},{0,112},{1... | collective-permute-start | bytes 786440 | tf_op jit(solution)/shard_map/ppermute | solution.py:316
  30.3 17.6 %collective-permute-start.2 = (bf16[8,64,256]{2,1,0:T(8,128)(2,1)}, bf16[8,64,256]{2,1,0:T(8,128)(2,1)S(1)}, u32[]{:S(2)}, u32[]{:S(2)}) collective-permute-start(bf16[8,64,256]{2,1,0:T(8,128)(2,1)} %get-tuple-element.15.rounded_ref), channel_id=1, source_target_pairs={{0,16},{16,0},{32,48},{48,32},{64,80},{80,64},{96,112},{112,96},{1... | collective-permute-start | bytes 786440 | tf_op jit(solution)/shard_map/ppermute | solution.py:316
  30.3 17.6 %collective-permute-start.1 = (bf16[8,64,256]{2,1,0:T(8,128)(2,1)}, bf16[8,64,256]{2,1,0:T(8,128)(2,1)S(1)}, u32[]{:S(2)}, u32[]{:S(2)}) collective-permute-start(bf16[8,64,256]{2,1,0:T(8,128)(2,1)} %get-tuple-element.15.rounded_ref), channel_id=1, source_target_pairs={{1,2},{2,1},{3,4},{4,3},{5,6},{6,5},{7,8},{8,7},{9,10},{10,9},{11,... | collective-permute-start | bytes 786440 | tf_op jit(solution)/shard_map/ppermute | solution.py:316
  31.2 16.7 %collective-permute-start = (bf16[8,64,256]{2,1,0:T(8,128)(2,1)}, bf16[8,64,256]{2,1,0:T(8,128)(2,1)S(1)}, u32[]{:S(2)}, u32[]{:S(2)}) collective-permute-start(bf16[8,64,256]{2,1,0:T(8,128)(2,1)} %get-tuple-element.15.rounded_ref), channel_id=1, source_target_pairs={{0,1},{1,0},{2,3},{3,2},{4,5},{5,4},{6,7},{7,6},{8,9},{9,8},{10,11... | collective-permute-start | bytes 786440 | tf_op jit(solution)/shard_map/ppermute | solution.py:316
  32.3 1.6 %copy-start = (bf16[64,64,256]{2,1,0:T(8,128)(2,1)S(1)}, bf16[64,64,256]{2,1,0:T(8,128)(2,1)}, u32[]{:S(2)}) copy-start(bf16[64,64,256]{2,1,0:T(8,128)(2,1)} %get-tuple-element.16.off_ref) | copy-start | bytes 6291460
  33.9 0.8 copy-start.2
  34.8 0.9 copy-start.4
  35.7 1.0 copy-start.7
  36.8 0.9 copy-start.8
  37.7 24.3 %copy-start.1 = (bf16[64,64,256]{2,1,0:T(8,128)(2,1)S(1)}, bf16[64,64,256]{2,1,0:T(8,128)(2,1)}, u32[]{:S(2)}) copy-start(bf16[64,64,256]{2,1,0:T(8,128)(2,1)} %get-tuple-element.16.off_ref) | copy-start | bytes 6291460
  37.7 24.3 %copy-start.5 = (bf16[8,64,256]{2,1,0:T(8,128)(2,1)S(1)}, bf16[8,64,256]{2,1,0:T(8,128)(2,1)}, u32[]{:S(2)}) copy-start(bf16[8,64,256]{2,1,0:T(8,128)(2,1)} %get-tuple-element.17.source_ref) | copy-start | bytes 786436
  56.0 16.0 %collective-permute-start.7 = (bf16[8,64,256]{2,1,0:T(8,128)(2,1)S(1)}, bf16[8,64,256]{2,1,0:T(8,128)(2,1)S(1)}, u32[]{:S(2)}, u32[]{:S(2)}) collective-permute-start(bf16[8,64,256]{2,1,0:T(8,128)(2,1)S(1)} %get-tuple-element.19.rounded_ref), channel_id=1, source_target_pairs={{16,32},{32,16},{48,64},{64,48},{80,96},{96,80},{112,0},{0,112},{1... | collective-permute-start | bytes 786440 | tf_op jit(solution)/shard_map/ppermute | solution.py:316
  56.5 15.5 %collective-permute-start.6 = (bf16[8,64,256]{2,1,0:T(8,128)(2,1)S(1)}, bf16[8,64,256]{2,1,0:T(8,128)(2,1)S(1)}, u32[]{:S(2)}, u32[]{:S(2)}) collective-permute-start(bf16[8,64,256]{2,1,0:T(8,128)(2,1)S(1)} %get-tuple-element.19.rounded_ref), channel_id=1, source_target_pairs={{0,16},{16,0},{32,48},{48,32},{64,80},{80,64},{96,112},{112,96},{1... | collective-permute-start | bytes 786440 | tf_op jit(solution)/shard_map/ppermute | solution.py:316
  58.0 14.1 %collective-permute-start.5 = (bf16[8,64,256]{2,1,0:T(8,128)(2,1)S(1)}, bf16[8,64,256]{2,1,0:T(8,128)(2,1)S(1)}, u32[]{:S(2)}, u32[]{:S(2)}) collective-permute-start(bf16[8,64,256]{2,1,0:T(8,128)(2,1)S(1)} %get-tuple-element.19.rounded_ref), channel_id=1, source_target_pairs={{1,2},{2,1},{3,4},{4,3},{5,6},{6,5},{7,8},{8,7},{9,10},{10,9},{11,... | collective-permute-start | bytes 786440 | tf_op jit(solution)/shard_map/ppermute | solution.py:316
  58.2 13.9 %collective-permute-start.4 = (bf16[8,64,256]{2,1,0:T(8,128)(2,1)S(1)}, bf16[8,64,256]{2,1,0:T(8,128)(2,1)S(1)}, u32[]{:S(2)}, u32[]{:S(2)}) collective-permute-start(bf16[8,64,256]{2,1,0:T(8,128)(2,1)S(1)} %get-tuple-element.19.rounded_ref), channel_id=1, source_target_pairs={{0,1},{1,0},{2,3},{3,2},{4,5},{5,4},{6,7},{7,6},{8,9},{9,8},{10,11... | collective-permute-start | bytes 786440 | tf_op jit(solution)/shard_map/ppermute | solution.py:316
  80.2 14.0 %collective-permute-start.11 = (bf16[8,64,256]{2,1,0:T(8,128)(2,1)S(1)}, bf16[8,64,256]{2,1,0:T(8,128)(2,1)S(1)}, u32[]{:S(2)}, u32[]{:S(2)}) collective-permute-start(bf16[8,64,256]{2,1,0:T(8,128)(2,1)S(1)} %get-tuple-element.21.rounded_ref), channel_id=1, source_target_pairs={{16,32},{32,16},{48,64},{64,48},{80,96},{96,80},{112,0},{0,112},{1... | collective-permute-start | bytes 786440 | tf_op jit(solution)/shard_map/ppermute | solution.py:316
  82.2 12.0 %collective-permute-start.10 = (bf16[8,64,256]{2,1,0:T(8,128)(2,1)S(1)}, bf16[8,64,256]{2,1,0:T(8,128)(2,1)S(1)}, u32[]{:S(2)}, u32[]{:S(2)}) collective-permute-start(bf16[8,64,256]{2,1,0:T(8,128)(2,1)S(1)} %get-tuple-element.21.rounded_ref), channel_id=1, source_target_pairs={{0,16},{16,0},{32,48},{48,32},{64,80},{80,64},{96,112},{112,96},{1... | collective-permute-start | bytes 786440 | tf_op jit(solution)/shard_map/ppermute | solution.py:316
  83.0 11.2 %collective-permute-start.9 = (bf16[8,64,256]{2,1,0:T(8,128)(2,1)S(1)}, bf16[8,64,256]{2,1,0:T(8,128)(2,1)S(1)}, u32[]{:S(2)}, u32[]{:S(2)}) collective-permute-start(bf16[8,64,256]{2,1,0:T(8,128)(2,1)S(1)} %get-tuple-element.21.rounded_ref), channel_id=1, source_target_pairs={{1,2},{2,1},{3,4},{4,3},{5,6},{6,5},{7,8},{8,7},{9,10},{10,9},{11,... | collective-permute-start | bytes 786440 | tf_op jit(solution)/shard_map/ppermute | solution.py:316
  83.0 11.2 %collective-permute-start.8 = (bf16[8,64,256]{2,1,0:T(8,128)(2,1)S(1)}, bf16[8,64,256]{2,1,0:T(8,128)(2,1)S(1)}, u32[]{:S(2)}, u32[]{:S(2)}) collective-permute-start(bf16[8,64,256]{2,1,0:T(8,128)(2,1)S(1)} %get-tuple-element.21.rounded_ref), channel_id=1, source_target_pairs={{0,1},{1,0},{2,3},{3,2},{4,5},{5,4},{6,7},{7,6},{8,9},{9,8},{10,11... | collective-permute-start | bytes 786440 | tf_op jit(solution)/shard_map/ppermute | solution.py:316
  102.2 0.7 copy-start.6

commit v3 on v2

v3 whole, which is shorter than its diff:
```python
import functools

import jax
import jax.numpy as jnp
from jax import lax
from jax.experimental import pallas as pl
from jax.experimental.pallas import tpu as pltpu
from jax.sharding import PartitionSpec as P

LX = 16
LY = 16
SWEEPS = 4
ROWS = 16
NEAR = 5
PAIR = 2
GROUP = 4
LANES = 128
F32 = jnp.float32
BF16 = jnp.bfloat16
SMALL = pltpu.CompilerParams(vmem_limit_bytes=8 * 2**20)


def total(terms):
    while len(terms) > 1:
        terms = [sum(terms[i : i + 2][1:], terms[i]) for i in range(0, len(terms), 2)]
    return terms[0]


def multiply(blocks, vectors, partial_ref, finish, arrive=None):
    _, count, _, _ = partial_ref.shape
    components = 64

    @pl.loop(0, components // ROWS)
    def _(step):
        start = pl.multiple_of(step * ROWS, ROWS)
        if arrive is not None:
            arrive(step)

        @pl.loop(0, ROWS // PAIR)
        def _(pair):
            row = start + pair * PAIR
            for first in range(0, count, GROUP):
                sums = {}
                for block, vector in zip(blocks, vectors):
                    rows = [[block(row + o, i) for i in range(components // 16)] for o in range(PAIR)]
                    for r in range(first, first + GROUP):
                        column = [vector(r, i) for i in range(components // 16)]
                        for o in range(PAIR):
                            term = total([a * v for a, v in zip(rows[o], column)])
                            term = (term[:8] + term[8:]).astype(F32)
                            sums[o, r] = sums[o, r] + term if (o, r) in sums else term
                for (o, r), value in sums.items():
                    place = pl.ds(pl.multiple_of((pair * PAIR + o) * 8, 8), 8)
                    partial_ref[0, r, place, :] = value[:, :LANES]
                    partial_ref[1, r, place, :] = value[:, LANES:]

        for r in range(count):
            for half in range(2):
                parts = []
                for eight in range(ROWS // 8):
                    parts.append(
                        total([partial_ref[half, r, pl.ds(eight * 64 + j, 8, stride=8), :] for j in range(8)])
                    )
                finish(r, pl.ds(start, ROWS), half, jnp.concatenate(parts, axis=0))


def prepare_kernel(block_ref, off_ref, inverse_ref):
    components, _, sites = off_ref.shape
    off_ref[...] = block_ref[0]

    @pl.loop(0, components // 16)
    def _(group):
        first = pl.multiple_of(group * 16, 16)
        here = lax.broadcasted_iota(jnp.int32, (16, sites), 0)
        diagonal = jnp.zeros((16, sites), F32)
        for o in range(16):
            block = block_ref[0, first + o, pl.ds(first, 16), :].astype(F32)
            diagonal = jnp.where(here == o, block, diagonal)
            off_ref[first + o, pl.ds(first, 16), :] = jnp.where(here == o, 0.0, block).astype(BF16)
        inverse_ref[pl.ds(first, 16), :] = 1.0 / diagonal


def prepare(stencil):
    _, components, _, sites = stencil.shape
    shape = (components, components, sites)
    return pl.pallas_call(
        prepare_kernel,
        grid=(1,),
        in_specs=[pl.BlockSpec((1, *shape), lambda g: (0, 0, 0, 0))],
        out_specs=[pl.BlockSpec(shape, lambda g: (0, 0, 0)), pl.BlockSpec((components, sites), lambda g: (0, 0))],
        out_shape=[jax.ShapeDtypeStruct(shape, BF16), jax.ShapeDtypeStruct((components, sites), F32)],
        compiler_params=pltpu.CompilerParams(vmem_limit_bytes=16 * 2**20),
        cost_estimate=pl.CostEstimate(flops=10**7, bytes_accessed=4 * 2**20, transcendentals=0),
        name="prepare",
    )(stencil)


def one_hot(index, size):
    column = lax.broadcasted_iota(jnp.int32, (size, size), 1)
    return jnp.where(column == index, 1.0, 0.0).astype(BF16)


def fine_order(sites):
    place = lax.broadcasted_iota(jnp.int32, (sites, sites), 0)
    u, w, g, h = place // 64, place // 16 % 4, place // 4 % 4, place % 4
    return u * 64 + g * 16 + w * 4 + h


def split_kernel(fine_ref, out_ref):
    rows, sites = fine_ref.shape
    _, _, planes, cells, _ = out_ref.shape
    unit = one_hot(lax.broadcasted_iota(jnp.int32, (sites, sites), 0), sites)
    turned = lax.dot_general(unit, fine_ref[...], (((1,), (1,)), ((), ())), preferred_element_type=F32)
    turned = turned.astype(BF16).reshape(2, planes, cells, rows)
    for half in range(2):
        out_ref[:, half] = turned


def split(fine, planes, cells):
    rows, _ = fine.shape
    return pl.pallas_call(
        split_kernel,
        out_shape=jax.ShapeDtypeStruct((2, 2, planes, cells, rows), BF16),
        compiler_params=SMALL,
        name="split",
    )(fine)


def start_kernel(received_ref, inverse_ref, source_ref, iterate_ref, rounded_ref, turned_ref):
    count, components, sites = rounded_ref.shape
    half = lax.axis_index("xy") // (lax.axis_size("xy") // 2)
    order = one_hot(fine_order(sites), sites)
    turned = lax.dot_general(
        received_ref[half], order, (((0,), (0,)), ((), ())), preferred_element_type=F32
    )
    for i in range(sites // LANES):
        turned_ref[i] = turned[:, i * LANES : (i + 1) * LANES]
    inverse = inverse_ref[...]
    for r in range(count):
        source = jnp.concatenate(
            [turned_ref[i, pl.ds(r, components, stride=count), :] for i in range(sites // LANES)], axis=1
        )
        iterate = source * inverse
        source_ref[r] = source.astype(BF16)
        iterate_ref[r] = iterate
        rounded_ref[r] = iterate.astype(BF16)


def start(received, inverse):
    _, sites, rows = received.shape
    components = inverse.shape[0]
    shape = (rows // components, components, sites)
    return pl.pallas_call(
        start_kernel,
        out_shape=[jax.ShapeDtypeStruct(shape, t) for t in (BF16, F32, BF16)],
        scratch_shapes=[pltpu.VMEM((sites // LANES, rows, LANES), F32)],
        compiler_params=SMALL,
        name="start",
    )(received, inverse)


def leave_kernel(rounded_ref, out_ref, mixed_ref):
    count, components, sites = rounded_ref.shape
    _, columns, cells, rows = out_ref.shape
    for r in range(count):
        value = rounded_ref[r].astype(F32)
        for i in range(sites // LANES):
            mixed_ref[i, pl.ds(r, components, stride=count), :] = value[:, i * LANES : (i + 1) * LANES]
    mixed = jnp.concatenate([mixed_ref[i].astype(BF16) for i in range(sites // LANES)], axis=1)
    order = one_hot(fine_order(sites), sites)
    turned = lax.dot_general(order, mixed, (((1,), (1,)), ((), ())), preferred_element_type=F32)
    turned = turned.astype(BF16).reshape(columns, cells, rows)
    for half in range(2):
        out_ref[half] = turned


def leave(rounded, columns):
    count, components, sites = rounded.shape
    rows = count * components
    return pl.pallas_call(
        leave_kernel,
        out_shape=jax.ShapeDtypeStruct((2, columns, sites // columns, rows), BF16),
        scratch_shapes=[pltpu.VMEM((sites // LANES, rows, LANES), F32)],
        compiler_params=SMALL,
        name="leave",
    )(rounded)


def join_kernel(received_ref, out_ref):
    places = received_ref.shape[2]
    half = lax.axis_index("zt") % 2
    unit = one_hot(lax.broadcasted_iota(jnp.int32, (places, places), 0), places)
    for e in range(2):
        out_ref[:, places * e : places * (e + 1)] = lax.dot_general(
            received_ref[e, half], unit, (((0,), (0,)), ((), ())), preferred_element_type=F32
        )


def join(received):
    _, _, places, rows = received.shape
    return pl.pallas_call(
        join_kernel,
        out_shape=jax.ShapeDtypeStruct((rows, 2 * places), F32),
        compiler_params=SMALL,
        name="join",
    )(received)


def sixteen(i):
    return slice(16 * i, 16 * i + 16)


def lanes(half):
    return slice(half * LANES, half * LANES + LANES)


def loads(pieces, kept_ref, sems):
    copies = []
    for step in range(kept_ref.shape[1] // ROWS):
        rows = pl.ds(step * ROWS, ROWS)
        for piece, (source, there, here, terms) in enumerate(pieces):
            from_ref = source.at[pl.ds(there, terms), rows]
            copies.append(
                pltpu.make_async_copy(from_ref, kept_ref.at[pl.ds(here, terms), rows], sems.at[piece, step])
            )
    return copies


def arrival(pieces, kept_ref, sems):
    def arrive(step):
        rows = pl.ds(pl.multiple_of(step * ROWS, ROWS), ROWS)
        for piece, (source, there, here, terms) in enumerate(pieces):
            from_ref = source.at[pl.ds(there, terms), rows]
            pltpu.make_async_copy(from_ref, kept_ref.at[pl.ds(here, terms), rows], sems.at[piece, step]).wait()

    return arrive


def local_kernel(first, *refs):
    if first:
        off_ref, far_ref, source_ref, iterate_ref, rounded_ref, inverse_ref = refs[:6]
        base_ref, stencil_ref, near_ref, partial_ref, sems = refs[6:]
        pieces = [(off_ref, 0, 0, 1), (far_ref, 1, 1, NEAR - 1)]
        for copy in loads(pieces, stencil_ref, sems):
            copy.start()
        arrive = arrival(pieces, stencil_ref, sems)
    else:
        stencil_ref, source_ref, iterate_ref, rounded_ref, inverse_ref, base_ref, near_ref, partial_ref = refs
        arrive = None
    count, components, sites = rounded_ref.shape
    lane = lax.broadcasted_iota(jnp.int32, (components, sites), 1) % LX

    @pl.loop(0, count)
    def _(r):
        value = rounded_ref[r].astype(F32)
        after = jnp.where(lane == LX - 1, pltpu.roll(value, LX - 1, 1), pltpu.roll(value, sites - 1, 1))
        before = jnp.where(lane == 0, pltpu.roll(value, sites - LX + 1, 1), pltpu.roll(value, 1, 1))
        near_ref[0, r] = after.astype(BF16)
        near_ref[1, r] = before.astype(BF16)
        near_ref[2, r] = pltpu.roll(value, sites - LX, 1).astype(BF16)
        near_ref[3, r] = pltpu.roll(value, LX, 1).astype(BF16)

    blocks = [lambda o, i, k=k: stencil_ref[k, o, sixteen(i), :] for k in range(NEAR)]
    vectors = [lambda r, i: rounded_ref[r, sixteen(i), :]]
    for k in range(NEAR - 1):
        vectors.append(lambda r, i, k=k: near_ref[k, r, sixteen(i), :])

    def finish(r, rows, half, sums):
        part = lanes(half)
        left = source_ref[r, rows, part].astype(F32) - sums
        kept = iterate_ref[r, rows, part] - rounded_ref[r, rows, part].astype(F32)
        base_ref[r, rows, part] = kept + left * inverse_ref[rows, part]

    multiply(blocks, vectors, partial_ref, finish, arrive)


def vmem(count):
    return [pl.BlockSpec(memory_space=pltpu.VMEM)] * count


def hbm(count):
    return [pl.BlockSpec(memory_space=pltpu.HBM)] * count


def local(stencil, source, iterate, rounded, inverse):
    count, components, sites = rounded.shape
    first = isinstance(stencil, tuple)
    kept = (NEAR, components, components, sites)
    scratch = [
        pltpu.VMEM((4, count, components, sites), BF16),
        pltpu.VMEM((2, count, ROWS * 8, LANES), F32),
    ]
    if first:
        scratch.append(pltpu.SemaphoreType.DMA((2, components // ROWS)))
    base = jax.ShapeDtypeStruct(rounded.shape, F32)
    blocks = stencil if first else (stencil,)
    return pl.pallas_call(
        functools.partial(local_kernel, first),
        in_specs=(hbm(2) if first else vmem(1)) + vmem(4),
        out_specs=vmem(2) if first else vmem(1)[0],
        out_shape=[base, pltpu.VMEM(kept, BF16)] if first else base,
        scratch_shapes=scratch,
        compiler_params=SMALL,
        cost_estimate=pl.CostEstimate(flops=10**9, bytes_accessed=12 * 2**20, transcendentals=0),
        name="local",
    )(*blocks, source, iterate, rounded, inverse)


def remote_kernel(first, last, *refs):
    if first:
        whole_ref, z0_ref, z1_ref, t0_ref, t1_ref, base_ref, inverse_ref = refs[:7]
        iterate_ref, rounded_ref, stencil_ref, partial_ref, sems = refs[7:]
        pieces = [(whole_ref, NEAR, 0, stencil_ref.shape[0])]
        for copy in loads(pieces, stencil_ref, sems):
            copy.start()
        arrive = arrival(pieces, stencil_ref, sems)
    else:
        stencil_ref, z0_ref, z1_ref, t0_ref, t1_ref, base_ref, inverse_ref = refs[:7]
        if last:
            rounded_ref, partial_ref = refs[7:]
        else:
            iterate_ref, rounded_ref, partial_ref = refs[7:]
        arrive = None

    z_odd = lax.axis_index("xy") % 2
    t_odd = lax.axis_index("zt") % 2
    blocks, vectors = [], []
    for k, ref in ((z_odd, z0_ref), (1 - z_odd, z1_ref), (2 + t_odd, t0_ref), (3 - t_odd, t1_ref)):
        blocks.append(lambda o, i, k=k: stencil_ref[k, o, sixteen(i), :])
        vectors.append(lambda r, i, ref=ref: ref[r, sixteen(i), :])

    def finish(r, rows, half, sums):
        part = lanes(half)
        iterate = base_ref[r, rows, part] - sums * inverse_ref[rows, part]
        if not last:
            iterate_ref[r, rows, part] = iterate
        rounded_ref[r, rows, part] = iterate.astype(BF16)

    multiply(blocks, vectors, partial_ref, finish, arrive)


def remote(stencil, halos, base, inverse, first, last):
    count, components, sites = base.shape
    types = [BF16] if last else [F32, BF16]
    shapes = [jax.ShapeDtypeStruct(base.shape, t) for t in types]
    scratch = [pltpu.VMEM((2, count, ROWS * 8, LANES), F32)]
    if first:
        shapes.append(pltpu.VMEM((stencil.shape[0] - NEAR, components, components, sites), BF16))
        scratch.append(pltpu.SemaphoreType.DMA((1, components // ROWS)))
    return pl.pallas_call(
        functools.partial(remote_kernel, first, last),
        in_specs=(hbm(1) if first else vmem(1)) + vmem(6),
        out_specs=vmem(len(shapes)),
        out_shape=shapes,
        scratch_shapes=scratch,
        compiler_params=SMALL,
        cost_estimate=pl.CostEstimate(flops=10**9, bytes_accessed=12 * 2**20, transcendentals=0),
        name="remote",
    )(stencil, *halos, base, inverse)


def pairs(plane, axis, first):
    count = lax.axis_size(axis)
    swaps = []
    for i in range(first, first + count, 2):
        a, b = i % count, (i + 1) % count
        swaps += [(a, b), (b, a)]
    return lax.ppermute(plane, axis, swaps)


def groups():
    columns = lax.axis_size("xy")
    return [list(range(i * columns, (i + 2) * columns)) for i in range(0, lax.axis_size("zt"), 2)]


def exchange(chunks):
    return lax.all_to_all(chunks, ("zt", "xy"), 0, 0, axis_index_groups=groups(), tiled=True)


def shards(restricted, stencil):
    columns = lax.axis_size("xy")
    planes = columns // 2
    components, count, sites = restricted.shape[2:]
    rows = components * count
    cells = sites // columns
    stencil = pltpu.with_memory_space_constraint(stencil[0, 0], pltpu.HBM)
    off, inverse = prepare(stencil)

    chunks = split(restricted.reshape(rows, sites), planes, cells)
    received = exchange(chunks.reshape(2 * columns, cells, rows))
    source, iterate, rounded = start(received.reshape(2, sites, rows), inverse)
    for sweep in range(SWEEPS - 1):
        last = sweep == SWEEPS - 2
        halos = [
            pairs(rounded, "xy", 0),
            pairs(rounded, "xy", 1),
            pairs(rounded, "zt", 0),
            pairs(rounded, "zt", 1),
        ]
        if sweep == 0:
            base, near = local((off[None], stencil), source, iterate, rounded, inverse)
            iterate, rounded, far = remote(stencil, halos, base, inverse, True, False)
        elif not last:
            base = local(near, source, iterate, rounded, inverse)
            iterate, rounded = remote(far, halos, base, inverse, False, False)
        else:
            base = local(near, source, iterate, rounded, inverse)
            (rounded,) = remote(far, halos, base, inverse, False, True)

    chunks = leave(rounded, columns)
    received = exchange(chunks.reshape(2 * columns, cells, rows))
    result = join(received.reshape(2, 2, planes * cells, rows))
    return result.reshape(1, 1, components, count, sites)


def solution(mesh):
    placed = (P("zt", "xy", None, None, None), P("zt", "xy", None, None, None, None))
    return jax.shard_map(
        shards,
        mesh=mesh,
        in_specs=placed,
        out_specs=P("zt", "xy", None, None, None),
        check_vma=False,
    )
```

time: 127 us -> 108 us (0.85)
  Pallas kernels: 67 us -> 51.9 us
  local copies, waits for them, and re-layouts: 6.86 us -> 0.95 us
  waiting for transfers between devices: 8.42 us -> 10.7 us
    pallas_call x7, Pallas kernels: 58.4 us -> 49.1 us  [the longest x3 26.9 us: local(): pl.pallas_call(functools.partial(local_kernel, first), in_specs=(hbm(2) i...]
    unnamed x20 -> x2, local copies, waits for them, and re-layouts: 6.86 us -> 0.95 us
    all_to_all x1, waiting for transfers between devices: 8.39 us -> 10.7 us  [exchange(): lax.all_to_all(chunks, ('zt', 'xy'), 0, 0, axis_index_groups=groups(), ti...]
    pallas_call x1, Pallas kernels: 2.4 us -> 0.37 us  [start(): pl.pallas_call(start_kernel, out_shape=[jax.ShapeDtypeStruct(shape, t) fo...]
    pallas_call x1, Pallas kernels: 2.08 us -> 0.33 us  [leave(): pl.pallas_call(leave_kernel, out_shape=jax.ShapeDtypeStruct((2, columns,...]
where the time goes in v3:
time: 108 us
  Pallas kernels  51.9 us (48%)
  starting transfers between devices  24.9 us (23%)
  blocking collectives  19.1 us (18%)
  waiting for transfers between devices  10.7 us (10%)
    pallas_call x3, Pallas kernels, local(): pl.pallas_call(functools.partial(local_kernel, first), in_specs=(hbm(2) i...  26.9 us
    pallas_call x3, Pallas kernels, remote(): pl.pallas_call(functools.partial(remote_kernel, first, last), in_specs=(h...  20.3 us
    all_to_all x1, blocking collectives, exchange(): lax.all_to_all(chunks, ('zt', 'xy'), 0, 0, axis_index_groups=groups(), ti...  19.1 us
    ppermute x12, starting transfers between devices, pairs(): return lax.ppermute(plane, axis, swaps)  14.5 us
    all_to_all x1, waiting for transfers between devices, exchange(): lax.all_to_all(chunks, ('zt', 'xy'), 0, 0, axis_index_groups=groups(), ti...  10.7 us
    all_to_all x1, starting transfers between devices, exchange(): lax.all_to_all(chunks, ('zt', 'xy'), 0, 0, axis_index_groups=groups(), ti...  10.4 us
  transfers between devices with their start and end apart: 13, of which 1 were waited for; matrix products, arithmetic and copies ran while one was open for 0% of the time, Pallas kernels for 27%

profile of v3, /device:TPU:1, one launch (start us, length us, event | category | flops | bytes accessed | tf_op | source)
XLA Modules:
  0.0 107.7 jit_solution(10383670580982265953)
XLA Ops:
  0.0 0.9 copy-done
  1.0 1.1 split.1
  2.0 10.4 %all-to-all-start = ((bf16[32,16,512]{2,1,0:T(8,128)(2,1)}), bf16[32,16,512]{2,1,0:T(8,128)(2,1)S(1)}, u32[]{:S(2)}, u32[]{:S(2)}) async-start(bf16[32,16,512]{2,1,0:T(8,128)(2,1)} %bitcast.2), calls=%async_computation | async-start | bytes 1048576 | tf_op jit(solution)/shard_map/all_to_all | solution.py:377
  12.4 1.8 %prepare.1 = (bf16[64,64,256]{2,1,0:T(8,128)(2,1)S(1)}, f32[64,256]{1,0:T(8,128)S(1)}) custom-call(bf16[9,64,64,256]{3,2,1,0:T(8,128)(2,1)} %bitcast.13), custom_call_target="tpu_custom_call" | custom-call | flops 10000000 | bytes 4194304 | tf_op jit(solution)/shard_map/prepare/pallas_call | solution.py:86
  14.2 10.7 %all-to-all-done = bf16[32,16,512]{2,1,0:T(8,128)(2,1)S(1)} async-done(((bf16[32,16,512]{2,1,0:T(8,128)(2,1)}), bf16[32,16,512]{2,1,0:T(8,128)(2,1)S(1)}, u32[]{:S(2)}, u32[]{:S(2)}) %all-to-all-start) | async-done | bytes 524320 | tf_op jit(solution)/shard_map/all_to_all | solution.py:377
  24.9 0.4 start.1
  25.3 2.3 %collective-permute-start.3 = (bf16[8,64,256]{2,1,0:T(8,128)(2,1)S(1)}, bf16[8,64,256]{2,1,0:T(8,128)(2,1)S(1)}, u32[]{:S(2)}, u32[]{:S(2)}) collective-permute-start(bf16[8,64,256]{2,1,0:T(8,128)(2,1)S(1)} %get-tuple-element.18.refs_4_), channel_id=1, source_target_pairs={{16,32},{32,16},{48,64},{64,48},{80,96},{96,80},{112,0},{0,112},{1... | collective-permute-start | bytes 786440 | tf_op jit(solution)/shard_map/ppermute | solution.py:368
  27.6 0.9 collective-permute-start.1
  28.5 1.1 %collective-permute-start = (bf16[8,64,256]{2,1,0:T(8,128)(2,1)S(1)}, bf16[8,64,256]{2,1,0:T(8,128)(2,1)S(1)}, u32[]{:S(2)}, u32[]{:S(2)}) collective-permute-start(bf16[8,64,256]{2,1,0:T(8,128)(2,1)S(1)} %get-tuple-element.18.refs_4_), channel_id=1, source_target_pairs={{0,1},{1,0},{2,3},{3,2},{4,5},{5,4},{6,7},{7,6},{8,9},{9,8},{10,11... | collective-permute-start | bytes 786440 | tf_op jit(solution)/shard_map/ppermute | solution.py:368
  29.6 9.4 %local.3 = (f32[8,64,256]{2,1,0:T(8,128)S(1)}, bf16[5,64,64,256]{3,2,1,0:T(8,128)(2,1)S(1)}) custom-call(bf16[1,64,64,256]{3,2,1,0:T(8,128)(2,1)S(1)} %bitcast.11, bf16[9,64,64,256]{3,2,1,0:T(8,128)(2,1)} %bitcast.14, bf16[8,64,256]{2,1,0:T(8,128)(2,1)S(1)} %get-tuple-element.20.refs_2_.refs_1_, f32[8,64,256]{2,1,0:T(8,128)S(1)} %get-tuple-element.21.refs_3_, ...), custom_call_target="tpu_custom_call" | custom-call | flops 1000000000 | bytes 12582912 | tf_op jit(solution)/shard_map/local/pallas_call | solution.py:297
  39.1 7.9 %remote.3 = (f32[8,64,256]{2,1,0:T(8,128)S(1)}, bf16[8,64,256]{2,1,0:T(8,128)(2,1)S(1)}, bf16[4,64,64,256]{3,2,1,0:T(8,128)(2,1)S(1)}) custom-call(bf16[9,64,64,256]{3,2,1,0:T(8,128)(2,1)} %bitcast.15, bf16[8,64,256]{2,1,0:T(8,128)(2,1)S(1)} %collective-permute-done.refs_1_, bf16[8,64,256]{2,1,0:T(8,128)(2,1)S(1)} %collective-permute-done.1.refs_2_, ...), custom_call_target="tpu_custom_call" | custom-call | flops 1000000000 | bytes 12582912 | tf_op jit(solution)/shard_map/remote/pallas_call | solution.py:350
  46.9 1.2 %collective-permute-start.7 = (bf16[8,64,256]{2,1,0:T(8,128)(2,1)S(1)}, bf16[8,64,256]{2,1,0:T(8,128)(2,1)S(1)}, u32[]{:S(2)}, u32[]{:S(2)}) collective-permute-start(bf16[8,64,256]{2,1,0:T(8,128)(2,1)S(1)} %get-tuple-element.24.refs_3_), channel_id=1, source_target_pairs={{16,32},{32,16},{48,64},{64,48},{80,96},{96,80},{112,0},{0,112},{1... | collective-permute-start | bytes 786440 | tf_op jit(solution)/shard_map/ppermute | solution.py:368
  48.1 0.7 collective-permute-start.6
  49.1 3.9 %collective-permute-start.4 = (bf16[8,64,256]{2,1,0:T(8,128)(2,1)S(1)}, bf16[8,64,256]{2,1,0:T(8,128)(2,1)S(1)}, u32[]{:S(2)}, u32[]{:S(2)}) collective-permute-start(bf16[8,64,256]{2,1,0:T(8,128)(2,1)S(1)} %get-tuple-element.24.refs_3_), channel_id=1, source_target_pairs={{0,1},{1,0},{2,3},{3,2},{4,5},{5,4},{6,7},{7,6},{8,9},{9,8},{10,11... | collective-permute-start | bytes 786440 | tf_op jit(solution)/shard_map/ppermute | solution.py:368
  53.0 8.7 %local.4.refs_5_ = f32[8,64,256]{2,1,0:T(8,128)S(1)} custom-call(bf16[5,64,64,256]{3,2,1,0:T(8,128)(2,1)S(1)} %get-tuple-element.25.refs_0_, bf16[8,64,256]{2,1,0:T(8,128)(2,1)S(1)} %get-tuple-element.20.refs_2_.refs_1_, f32[8,64,256]{2,1,0:T(8,128)S(1)} %get-tuple-element.26.refs_2_, bf16[8,64,256]{2,1,0:T(8,128)(2,1)S(1)} %get-tuple-element.24.refs_3_, ...), custom_call_target="tpu_custom_call" | custom-call | flops 1000000000 | bytes 12582912 | tf_op jit(solution)/shard_map/local/pallas_call | solution.py:297
  61.8 6.2 %remote.4 = (f32[8,64,256]{2,1,0:T(8,128)S(1)}, bf16[8,64,256]{2,1,0:T(8,128)(2,1)S(1)}) custom-call(bf16[4,64,64,256]{3,2,1,0:T(8,128)(2,1)S(1)} %get-tuple-element.23.refs_0_, bf16[8,64,256]{2,1,0:T(8,128)(2,1)S(1)} %collective-permute-done.4.refs_1_, bf16[8,64,256]{2,1,0:T(8,128)(2,1)S(1)} %collective-permute-done.5.refs_2_, ...), custom_call_target="tpu_custom_call" | custom-call | flops 1000000000 | bytes 12582912 | tf_op jit(solution)/shard_map/remote/pallas_call | solution.py:350
  68.0 2.0 %collective-permute-start.11 = (bf16[8,64,256]{2,1,0:T(8,128)(2,1)S(1)}, bf16[8,64,256]{2,1,0:T(8,128)(2,1)S(1)}, u32[]{:S(2)}, u32[]{:S(2)}) collective-permute-start(bf16[8,64,256]{2,1,0:T(8,128)(2,1)S(1)} %get-tuple-element.27.refs_3_), channel_id=1, source_target_pairs={{16,32},{32,16},{48,64},{64,48},{80,96},{96,80},{112,0},{0,112},{1... | collective-permute-start | bytes 786440 | tf_op jit(solution)/shard_map/ppermute | solution.py:368
  70.0 0.8 collective-permute-start.10
  70.8 1.4 %collective-permute-start.8 = (bf16[8,64,256]{2,1,0:T(8,128)(2,1)S(1)}, bf16[8,64,256]{2,1,0:T(8,128)(2,1)S(1)}, u32[]{:S(2)}, u32[]{:S(2)}) collective-permute-start(bf16[8,64,256]{2,1,0:T(8,128)(2,1)S(1)} %get-tuple-element.27.refs_3_), channel_id=1, source_target_pairs={{0,1},{1,0},{2,3},{3,2},{4,5},{5,4},{6,7},{7,6},{8,9},{9,8},{10,11... | collective-permute-start | bytes 786440 | tf_op jit(solution)/shard_map/ppermute | solution.py:368
  72.2 8.7 %local.5.refs_5_ = f32[8,64,256]{2,1,0:T(8,128)S(1)} custom-call(bf16[5,64,64,256]{3,2,1,0:T(8,128)(2,1)S(1)} %get-tuple-element.25.refs_0_, bf16[8,64,256]{2,1,0:T(8,128)(2,1)S(1)} %get-tuple-element.20.refs_2_.refs_1_, f32[8,64,256]{2,1,0:T(8,128)S(1)} %get-tuple-element.28.refs_2_, bf16[8,64,256]{2,1,0:T(8,128)(2,1)S(1)} %get-tuple-element.27.refs_3_, ...), custom_call_target="tpu_custom_call" | custom-call | flops 1000000000 | bytes 12582912 | tf_op jit(solution)/shard_map/local/pallas_call | solution.py:297
  81.0 6.2 %remote.5.rounded_ref = bf16[8,64,256]{2,1,0:T(8,128)(2,1)S(1)} custom-call(bf16[4,64,64,256]{3,2,1,0:T(8,128)(2,1)S(1)} %get-tuple-element.23.refs_0_, bf16[8,64,256]{2,1,0:T(8,128)(2,1)S(1)} %collective-permute-done.8.refs_1_, bf16[8,64,256]{2,1,0:T(8,128)(2,1)S(1)} %collective-permute-done.9.refs_2_, ...), custom_call_target="tpu_custom_call" | custom-call | flops 1000000000 | bytes 12582912 | tf_op jit(solution)/shard_map/remote/pallas_call | solution.py:350
  87.3 0.3 leave.1
  87.6 19.1 %all_to_all.10 = bf16[32,16,512]{2,1,0:T(8,128)(2,1)S(1)} all-to-all(bf16[32,16,512]{2,1,0:T(8,128)(2,1)S(1)} %bitcast.9), channel_id=1, replica_groups={{0,1,2,3,4,5,6,7,8,9,10,11,12,13,14,15,16,17,18,19,20,21,22,23,24,25,26..., dimensions={0} | all-to-all | bytes 1048576 | tf_op jit(solution)/shard_map/all_to_all | solution.py:377
  106.6 1.1 join.1
  (16 shorter events, 0.3 us)
Async XLA Ops:
  0.0 0.9 copy-start
  2.0 22.9 %all-to-all-start = ((bf16[32,16,512]{2,1,0:T(8,128)(2,1)}), bf16[32,16,512]{2,1,0:T(8,128)(2,1)S(1)}, u32[]{:S(2)}, u32[]{:S(2)}) async-start(bf16[32,16,512]{2,1,0:T(8,128)(2,1)} %bitcast.2), calls=%async_computation | async-start | bytes 1048576 | tf_op jit(solution)/shard_map/all_to_all | solution.py:377
  25.3 13.7 %collective-permute-start.3 = (bf16[8,64,256]{2,1,0:T(8,128)(2,1)S(1)}, bf16[8,64,256]{2,1,0:T(8,128)(2,1)S(1)}, u32[]{:S(2)}, u32[]{:S(2)}) collective-permute-start(bf16[8,64,256]{2,1,0:T(8,128)(2,1)S(1)} %get-tuple-element.18.refs_4_), channel_id=1, source_target_pairs={{16,32},{32,16},{48,64},{64,48},{80,96},{96,80},{112,0},{0,112},{1... | collective-permute-start | bytes 786440 | tf_op jit(solution)/shard_map/ppermute | solution.py:368
  27.6 11.5 %collective-permute-start.2 = (bf16[8,64,256]{2,1,0:T(8,128)(2,1)S(1)}, bf16[8,64,256]{2,1,0:T(8,128)(2,1)S(1)}, u32[]{:S(2)}, u32[]{:S(2)}) collective-permute-start(bf16[8,64,256]{2,1,0:T(8,128)(2,1)S(1)} %get-tuple-element.18.refs_4_), channel_id=1, source_target_pairs={{0,16},{16,0},{32,48},{48,32},{64,80},{80,64},{96,112},{112,96},{1... | collective-permute-start | bytes 786440 | tf_op jit(solution)/shard_map/ppermute | solution.py:368
  27.6 11.5 %collective-permute-start.1 = (bf16[8,64,256]{2,1,0:T(8,128)(2,1)S(1)}, bf16[8,64,256]{2,1,0:T(8,128)(2,1)S(1)}, u32[]{:S(2)}, u32[]{:S(2)}) collective-permute-start(bf16[8,64,256]{2,1,0:T(8,128)(2,1)S(1)} %get-tuple-element.18.refs_4_), channel_id=1, source_target_pairs={{1,2},{2,1},{3,4},{4,3},{5,6},{6,5},{7,8},{8,7},{9,10},{10,9},{11,... | collective-permute-start | bytes 786440 | tf_op jit(solution)/shard_map/ppermute | solution.py:368
  28.5 10.6 %collective-permute-start = (bf16[8,64,256]{2,1,0:T(8,128)(2,1)S(1)}, bf16[8,64,256]{2,1,0:T(8,128)(2,1)S(1)}, u32[]{:S(2)}, u32[]{:S(2)}) collective-permute-start(bf16[8,64,256]{2,1,0:T(8,128)(2,1)S(1)} %get-tuple-element.18.refs_4_), channel_id=1, source_target_pairs={{0,1},{1,0},{2,3},{3,2},{4,5},{5,4},{6,7},{7,6},{8,9},{9,8},{10,11... | collective-permute-start | bytes 786440 | tf_op jit(solution)/shard_map/ppermute | solution.py:368
  46.9 14.8 %collective-permute-start.7 = (bf16[8,64,256]{2,1,0:T(8,128)(2,1)S(1)}, bf16[8,64,256]{2,1,0:T(8,128)(2,1)S(1)}, u32[]{:S(2)}, u32[]{:S(2)}) collective-permute-start(bf16[8,64,256]{2,1,0:T(8,128)(2,1)S(1)} %get-tuple-element.24.refs_3_), channel_id=1, source_target_pairs={{16,32},{32,16},{48,64},{64,48},{80,96},{96,80},{112,0},{0,112},{1... | collective-permute-start | bytes 786440 | tf_op jit(solution)/shard_map/ppermute | solution.py:368
  48.1 13.6 %collective-permute-start.6 = (bf16[8,64,256]{2,1,0:T(8,128)(2,1)S(1)}, bf16[8,64,256]{2,1,0:T(8,128)(2,1)S(1)}, u32[]{:S(2)}, u32[]{:S(2)}) collective-permute-start(bf16[8,64,256]{2,1,0:T(8,128)(2,1)S(1)} %get-tuple-element.24.refs_3_), channel_id=1, source_target_pairs={{0,16},{16,0},{32,48},{48,32},{64,80},{80,64},{96,112},{112,96},{1... | collective-permute-start | bytes 786440 | tf_op jit(solution)/shard_map/ppermute | solution.py:368
  48.9 12.9 %collective-permute-start.5 = (bf16[8,64,256]{2,1,0:T(8,128)(2,1)S(1)}, bf16[8,64,256]{2,1,0:T(8,128)(2,1)S(1)}, u32[]{:S(2)}, u32[]{:S(2)}) collective-permute-start(bf16[8,64,256]{2,1,0:T(8,128)(2,1)S(1)} %get-tuple-element.24.refs_3_), channel_id=1, source_target_pairs={{1,2},{2,1},{3,4},{4,3},{5,6},{6,5},{7,8},{8,7},{9,10},{10,9},{11,... | collective-permute-start | bytes 786440 | tf_op jit(solution)/shard_map/ppermute | solution.py:368
  49.1 12.6 %collective-permute-start.4 = (bf16[8,64,256]{2,1,0:T(8,128)(2,1)S(1)}, bf16[8,64,256]{2,1,0:T(8,128)(2,1)S(1)}, u32[]{:S(2)}, u32[]{:S(2)}) collective-permute-start(bf16[8,64,256]{2,1,0:T(8,128)(2,1)S(1)} %get-tuple-element.24.refs_3_), channel_id=1, source_target_pairs={{0,1},{1,0},{2,3},{3,2},{4,5},{5,4},{6,7},{7,6},{8,9},{9,8},{10,11... | collective-permute-start | bytes 786440 | tf_op jit(solution)/shard_map/ppermute | solution.py:368
  68.0 13.0 %collective-permute-start.11 = (bf16[8,64,256]{2,1,0:T(8,128)(2,1)S(1)}, bf16[8,64,256]{2,1,0:T(8,128)(2,1)S(1)}, u32[]{:S(2)}, u32[]{:S(2)}) collective-permute-start(bf16[8,64,256]{2,1,0:T(8,128)(2,1)S(1)} %get-tuple-element.27.refs_3_), channel_id=1, source_target_pairs={{16,32},{32,16},{48,64},{64,48},{80,96},{96,80},{112,0},{0,112},{1... | collective-permute-start | bytes 786440 | tf_op jit(solution)/shard_map/ppermute | solution.py:368
  70.0 11.0 %collective-permute-start.10 = (bf16[8,64,256]{2,1,0:T(8,128)(2,1)S(1)}, bf16[8,64,256]{2,1,0:T(8,128)(2,1)S(1)}, u32[]{:S(2)}, u32[]{:S(2)}) collective-permute-start(bf16[8,64,256]{2,1,0:T(8,128)(2,1)S(1)} %get-tuple-element.27.refs_3_), channel_id=1, source_target_pairs={{0,16},{16,0},{32,48},{48,32},{64,80},{80,64},{96,112},{112,96},{1... | collective-permute-start | bytes 786440 | tf_op jit(solution)/shard_map/ppermute | solution.py:368
  70.8 10.2 %collective-permute-start.9 = (bf16[8,64,256]{2,1,0:T(8,128)(2,1)S(1)}, bf16[8,64,256]{2,1,0:T(8,128)(2,1)S(1)}, u32[]{:S(2)}, u32[]{:S(2)}) collective-permute-start(bf16[8,64,256]{2,1,0:T(8,128)(2,1)S(1)} %get-tuple-element.27.refs_3_), channel_id=1, source_target_pairs={{1,2},{2,1},{3,4},{4,3},{5,6},{6,5},{7,8},{8,7},{9,10},{10,9},{11,... | collective-permute-start | bytes 786440 | tf_op jit(solution)/shard_map/ppermute | solution.py:368
  70.8 10.2 %collective-permute-start.8 = (bf16[8,64,256]{2,1,0:T(8,128)(2,1)S(1)}, bf16[8,64,256]{2,1,0:T(8,128)(2,1)S(1)}, u32[]{:S(2)}, u32[]{:S(2)}) collective-permute-start(bf16[8,64,256]{2,1,0:T(8,128)(2,1)S(1)} %get-tuple-element.27.refs_3_), channel_id=1, source_target_pairs={{0,1},{1,0},{2,3},{3,2},{4,5},{5,4},{6,7},{7,6},{8,9},{9,8},{10,11... | collective-permute-start | bytes 786440 | tf_op jit(solution)/shard_map/ppermute | solution.py:368

commit v4 on v3

--- a/solution.py
+++ b/solution.py
@@ -12,8 +12,9 @@
 SWEEPS = 4
 ROWS = 16
 NEAR = 5
-PAIR = 2
-GROUP = 4
+PAIR = 1
+GROUP = 8
+TERMS = 2
 LANES = 128
 F32 = jnp.float32
 BF16 = jnp.bfloat16
@@ -41,10 +42,13 @@
             row = start + pair * PAIR
             for first in range(0, count, GROUP):
                 sums = {}
-                for block, vector in zip(blocks, vectors):
-                    rows = [[block(row + o, i) for i in range(components // 16)] for o in range(PAIR)]
+                for k in range(0, len(blocks), TERMS):
+                    some = list(zip(blocks, vectors))[k : k + TERMS]
+                    rows = [
+                        [block(row + o, i) for block, _ in some for i in range(components // 16)] for o in range(PAIR)
+                    ]
                     for r in range(first, first + GROUP):
-                        column = [vector(r, i) for i in range(components // 16)]
+                        column = [vector(r, i) for _, vector in some for i in range(components // 16)]
                         for o in range(PAIR):
                             term = total([a * v for a, v in zip(rows[o], column)])
                             term = (term[:8] + term[8:]).astype(F32)

time: 108 us -> 106 us (0.981)
  Pallas kernels: 51.9 us -> 49.8 us
    pallas_call x3, Pallas kernels: 26.9 us -> 25.7 us  [local(): pl.pallas_call(functools.partial(local_kernel, first), in_specs=(hbm(2) i...]
  transfers between devices with their start and end apart: 13 -> 13, of which waited for: 1 -> 1; matrix products, arithmetic and copies ran while one was open for 0% -> 0% of each run, Pallas kernels for 27% -> 26%
where the time goes in v4:
time: 106 us
  Pallas kernels  49.8 us (47%)
  starting transfers between devices  25.4 us (24%)
  blocking collectives  18.6 us (18%)
  waiting for transfers between devices  10.7 us (10%)
    pallas_call x3, Pallas kernels, local(): pl.pallas_call(functools.partial(local_kernel, first), in_specs=(hbm(2) i...  25.7 us
    pallas_call x3, Pallas kernels, remote(): pl.pallas_call(functools.partial(remote_kernel, first, last), in_specs=(h...  19.4 us
    all_to_all x1, blocking collectives, exchange(): lax.all_to_all(chunks, ('zt', 'xy'), 0, 0, axis_index_groups=groups(), ti...  18.6 us
    ppermute x12, starting transfers between devices, pairs(): return lax.ppermute(plane, axis, swaps)  15 us
    all_to_all x1, waiting for transfers between devices, exchange(): lax.all_to_all(chunks, ('zt', 'xy'), 0, 0, axis_index_groups=groups(), ti...  10.7 us
    all_to_all x1, starting transfers between devices, exchange(): lax.all_to_all(chunks, ('zt', 'xy'), 0, 0, axis_index_groups=groups(), ti...  10.4 us
  transfers between devices with their start and end apart: 13, of which 1 were waited for; matrix products, arithmetic and copies ran while one was open for 0% of the time, Pallas kernels for 26%

profile of v4, /device:TPU:1, one launch (start us, length us, event | category | flops | bytes accessed | tf_op | source)
XLA Modules:
  0.0 105.6 jit_solution(16886352553857764643)
XLA Ops:
  0.0 0.9 copy-done
  1.0 1.1 %split.1 = bf16[2,2,8,16,512]{4,3,2,1,0:T(8,128)(2,1)} custom-call(bf16[512,256]{1,0:T(8,128)(2,1)S(1)} %bitcast.12), custom_call_target="tpu_custom_call" | custom-call | tf_op jit(solution)/shard_map/split/pallas_call | solution.py:125
  2.0 10.4 %all-to-all-start = ((bf16[32,16,512]{2,1,0:T(8,128)(2,1)}), bf16[32,16,512]{2,1,0:T(8,128)(2,1)S(1)}, u32[]{:S(2)}, u32[]{:S(2)}) async-start(bf16[32,16,512]{2,1,0:T(8,128)(2,1)} %bitcast.2), calls=%async_computation | async-start | bytes 1048576 | tf_op jit(solution)/shard_map/all_to_all | solution.py:381
  12.4 1.8 %prepare.1 = (bf16[64,64,256]{2,1,0:T(8,128)(2,1)S(1)}, f32[64,256]{1,0:T(8,128)S(1)}) custom-call(bf16[9,64,64,256]{3,2,1,0:T(8,128)(2,1)} %bitcast.13), custom_call_target="tpu_custom_call" | custom-call | flops 10000000 | bytes 4194304 | tf_op jit(solution)/shard_map/prepare/pallas_call | solution.py:90
  14.2 10.7 %all-to-all-done = bf16[32,16,512]{2,1,0:T(8,128)(2,1)S(1)} async-done(((bf16[32,16,512]{2,1,0:T(8,128)(2,1)}), bf16[32,16,512]{2,1,0:T(8,128)(2,1)S(1)}, u32[]{:S(2)}, u32[]{:S(2)}) %all-to-all-start) | async-done | bytes 524320 | tf_op jit(solution)/shard_map/all_to_all | solution.py:381
  24.9 0.4 start.1
  25.3 2.3 %collective-permute-start.3 = (bf16[8,64,256]{2,1,0:T(8,128)(2,1)S(1)}, bf16[8,64,256]{2,1,0:T(8,128)(2,1)S(1)}, u32[]{:S(2)}, u32[]{:S(2)}) collective-permute-start(bf16[8,64,256]{2,1,0:T(8,128)(2,1)S(1)} %get-tuple-element.18.refs_4_), channel_id=1, source_target_pairs={{16,32},{32,16},{48,64},{64,48},{80,96},{96,80},{112,0},{0,112},{1... | collective-permute-start | bytes 786440 | tf_op jit(solution)/shard_map/ppermute | solution.py:372
  27.6 0.9 collective-permute-start.1
  28.5 1.1 %collective-permute-start = (bf16[8,64,256]{2,1,0:T(8,128)(2,1)S(1)}, bf16[8,64,256]{2,1,0:T(8,128)(2,1)S(1)}, u32[]{:S(2)}, u32[]{:S(2)}) collective-permute-start(bf16[8,64,256]{2,1,0:T(8,128)(2,1)S(1)} %get-tuple-element.18.refs_4_), channel_id=1, source_target_pairs={{0,1},{1,0},{2,3},{3,2},{4,5},{5,4},{6,7},{7,6},{8,9},{9,8},{10,11... | collective-permute-start | bytes 786440 | tf_op jit(solution)/shard_map/ppermute | solution.py:372
  29.6 9.0 %local.3 = (f32[8,64,256]{2,1,0:T(8,128)S(1)}, bf16[5,64,64,256]{3,2,1,0:T(8,128)(2,1)S(1)}) custom-call(bf16[1,64,64,256]{3,2,1,0:T(8,128)(2,1)S(1)} %bitcast.11, bf16[9,64,64,256]{3,2,1,0:T(8,128)(2,1)} %bitcast.14, bf16[8,64,256]{2,1,0:T(8,128)(2,1)S(1)} %get-tuple-element.20.refs_2_.refs_1_, f32[8,64,256]{2,1,0:T(8,128)S(1)} %get-tuple-element.21.refs_3_, ...), custom_call_target="tpu_custom_call" | custom-call | flops 1000000000 | bytes 12582912 | tf_op jit(solution)/shard_map/local/pallas_call | solution.py:301
  38.7 7.6 %remote.3 = (f32[8,64,256]{2,1,0:T(8,128)S(1)}, bf16[8,64,256]{2,1,0:T(8,128)(2,1)S(1)}, bf16[4,64,64,256]{3,2,1,0:T(8,128)(2,1)S(1)}) custom-call(bf16[9,64,64,256]{3,2,1,0:T(8,128)(2,1)} %bitcast.15, bf16[8,64,256]{2,1,0:T(8,128)(2,1)S(1)} %collective-permute-done.refs_1_, bf16[8,64,256]{2,1,0:T(8,128)(2,1)S(1)} %collective-permute-done.1.refs_2_, ...), custom_call_target="tpu_custom_call" | custom-call | flops 1000000000 | bytes 12582912 | tf_op jit(solution)/shard_map/remote/pallas_call | solution.py:354
  46.3 1.6 %collective-permute-start.7 = (bf16[8,64,256]{2,1,0:T(8,128)(2,1)S(1)}, bf16[8,64,256]{2,1,0:T(8,128)(2,1)S(1)}, u32[]{:S(2)}, u32[]{:S(2)}) collective-permute-start(bf16[8,64,256]{2,1,0:T(8,128)(2,1)S(1)} %get-tuple-element.24.refs_3_), channel_id=1, source_target_pairs={{16,32},{32,16},{48,64},{64,48},{80,96},{96,80},{112,0},{0,112},{1... | collective-permute-start | bytes 786440 | tf_op jit(solution)/shard_map/ppermute | solution.py:372
  47.8 0.4 collective-permute-start.6
  48.4 3.9 %collective-permute-start.4 = (bf16[8,64,256]{2,1,0:T(8,128)(2,1)S(1)}, bf16[8,64,256]{2,1,0:T(8,128)(2,1)S(1)}, u32[]{:S(2)}, u32[]{:S(2)}) collective-permute-start(bf16[8,64,256]{2,1,0:T(8,128)(2,1)S(1)} %get-tuple-element.24.refs_3_), channel_id=1, source_target_pairs={{0,1},{1,0},{2,3},{3,2},{4,5},{5,4},{6,7},{7,6},{8,9},{9,8},{10,11... | collective-permute-start | bytes 786440 | tf_op jit(solution)/shard_map/ppermute | solution.py:372
  52.3 8.3 %local.4.refs_5_ = f32[8,64,256]{2,1,0:T(8,128)S(1)} custom-call(bf16[5,64,64,256]{3,2,1,0:T(8,128)(2,1)S(1)} %get-tuple-element.25.refs_0_, bf16[8,64,256]{2,1,0:T(8,128)(2,1)S(1)} %get-tuple-element.20.refs_2_.refs_1_, f32[8,64,256]{2,1,0:T(8,128)S(1)} %get-tuple-element.26.refs_2_, bf16[8,64,256]{2,1,0:T(8,128)(2,1)S(1)} %get-tuple-element.24.refs_3_, ...), custom_call_target="tpu_custom_call" | custom-call | flops 1000000000 | bytes 12582912 | tf_op jit(solution)/shard_map/local/pallas_call | solution.py:301
  60.7 5.9 %remote.4 = (f32[8,64,256]{2,1,0:T(8,128)S(1)}, bf16[8,64,256]{2,1,0:T(8,128)(2,1)S(1)}) custom-call(bf16[4,64,64,256]{3,2,1,0:T(8,128)(2,1)S(1)} %get-tuple-element.23.refs_0_, bf16[8,64,256]{2,1,0:T(8,128)(2,1)S(1)} %collective-permute-done.4.refs_1_, bf16[8,64,256]{2,1,0:T(8,128)(2,1)S(1)} %collective-permute-done.5.refs_2_, ...), custom_call_target="tpu_custom_call" | custom-call | flops 1000000000 | bytes 12582912 | tf_op jit(solution)/shard_map/remote/pallas_call | solution.py:354
  66.6 2.0 %collective-permute-start.11 = (bf16[8,64,256]{2,1,0:T(8,128)(2,1)S(1)}, bf16[8,64,256]{2,1,0:T(8,128)(2,1)S(1)}, u32[]{:S(2)}, u32[]{:S(2)}) collective-permute-start(bf16[8,64,256]{2,1,0:T(8,128)(2,1)S(1)} %get-tuple-element.27.refs_3_), channel_id=1, source_target_pairs={{16,32},{32,16},{48,64},{64,48},{80,96},{96,80},{112,0},{0,112},{1... | collective-permute-start | bytes 786440 | tf_op jit(solution)/shard_map/ppermute | solution.py:372
  68.6 0.8 collective-permute-start.10
  69.4 1.8 %collective-permute-start.8 = (bf16[8,64,256]{2,1,0:T(8,128)(2,1)S(1)}, bf16[8,64,256]{2,1,0:T(8,128)(2,1)S(1)}, u32[]{:S(2)}, u32[]{:S(2)}) collective-permute-start(bf16[8,64,256]{2,1,0:T(8,128)(2,1)S(1)} %get-tuple-element.27.refs_3_), channel_id=1, source_target_pairs={{0,1},{1,0},{2,3},{3,2},{4,5},{5,4},{6,7},{7,6},{8,9},{9,8},{10,11... | collective-permute-start | bytes 786440 | tf_op jit(solution)/shard_map/ppermute | solution.py:372
  71.3 8.3 %local.5.refs_5_ = f32[8,64,256]{2,1,0:T(8,128)S(1)} custom-call(bf16[5,64,64,256]{3,2,1,0:T(8,128)(2,1)S(1)} %get-tuple-element.25.refs_0_, bf16[8,64,256]{2,1,0:T(8,128)(2,1)S(1)} %get-tuple-element.20.refs_2_.refs_1_, f32[8,64,256]{2,1,0:T(8,128)S(1)} %get-tuple-element.28.refs_2_, bf16[8,64,256]{2,1,0:T(8,128)(2,1)S(1)} %get-tuple-element.27.refs_3_, ...), custom_call_target="tpu_custom_call" | custom-call | flops 1000000000 | bytes 12582912 | tf_op jit(solution)/shard_map/local/pallas_call | solution.py:301
  79.6 5.9 %remote.5.rounded_ref = bf16[8,64,256]{2,1,0:T(8,128)(2,1)S(1)} custom-call(bf16[4,64,64,256]{3,2,1,0:T(8,128)(2,1)S(1)} %get-tuple-element.23.refs_0_, bf16[8,64,256]{2,1,0:T(8,128)(2,1)S(1)} %collective-permute-done.8.refs_1_, bf16[8,64,256]{2,1,0:T(8,128)(2,1)S(1)} %collective-permute-done.9.refs_2_, ...), custom_call_target="tpu_custom_call" | custom-call | flops 1000000000 | bytes 12582912 | tf_op jit(solution)/shard_map/remote/pallas_call | solution.py:354
  85.5 0.3 leave.1
  85.9 18.6 %all_to_all.10 = bf16[32,16,512]{2,1,0:T(8,128)(2,1)S(1)} all-to-all(bf16[32,16,512]{2,1,0:T(8,128)(2,1)S(1)} %bitcast.9), channel_id=1, replica_groups={{0,1,2,3,4,5,6,7,8,9,10,11,12,13,14,15,16,17,18,19,20,21,22,23,24,25,26..., dimensions={0} | all-to-all | bytes 1048576 | tf_op jit(solution)/shard_map/all_to_all | solution.py:381
  104.5 1.1 %join.1 = f32[512,256]{1,0:T(8,128)} custom-call(bf16[2,2,128,512]{3,2,1,0:T(8,128)(2,1)S(1)} %bitcast.10), custom_call_target="tpu_custom_call" | custom-call | tf_op jit(solution)/shard_map/join/pallas_call | solution.py:205
  (16 shorter events, 0.3 us)
Async XLA Ops:
  0.0 0.9 copy-start
  2.0 22.9 %all-to-all-start = ((bf16[32,16,512]{2,1,0:T(8,128)(2,1)}), bf16[32,16,512]{2,1,0:T(8,128)(2,1)S(1)}, u32[]{:S(2)}, u32[]{:S(2)}) async-start(bf16[32,16,512]{2,1,0:T(8,128)(2,1)} %bitcast.2), calls=%async_computation | async-start | bytes 1048576 | tf_op jit(solution)/shard_map/all_to_all | solution.py:381
  25.3 13.4 %collective-permute-start.3 = (bf16[8,64,256]{2,1,0:T(8,128)(2,1)S(1)}, bf16[8,64,256]{2,1,0:T(8,128)(2,1)S(1)}, u32[]{:S(2)}, u32[]{:S(2)}) collective-permute-start(bf16[8,64,256]{2,1,0:T(8,128)(2,1)S(1)} %get-tuple-element.18.refs_4_), channel_id=1, source_target_pairs={{16,32},{32,16},{48,64},{64,48},{80,96},{96,80},{112,0},{0,112},{1... | collective-permute-start | bytes 786440 | tf_op jit(solution)/shard_map/ppermute | solution.py:372
  27.6 11.1 %collective-permute-start.2 = (bf16[8,64,256]{2,1,0:T(8,128)(2,1)S(1)}, bf16[8,64,256]{2,1,0:T(8,128)(2,1)S(1)}, u32[]{:S(2)}, u32[]{:S(2)}) collective-permute-start(bf16[8,64,256]{2,1,0:T(8,128)(2,1)S(1)} %get-tuple-element.18.refs_4_), channel_id=1, source_target_pairs={{0,16},{16,0},{32,48},{48,32},{64,80},{80,64},{96,112},{112,96},{1... | collective-permute-start | bytes 786440 | tf_op jit(solution)/shard_map/ppermute | solution.py:372
  27.6 11.1 %collective-permute-start.1 = (bf16[8,64,256]{2,1,0:T(8,128)(2,1)S(1)}, bf16[8,64,256]{2,1,0:T(8,128)(2,1)S(1)}, u32[]{:S(2)}, u32[]{:S(2)}) collective-permute-start(bf16[8,64,256]{2,1,0:T(8,128)(2,1)S(1)} %get-tuple-element.18.refs_4_), channel_id=1, source_target_pairs={{1,2},{2,1},{3,4},{4,3},{5,6},{6,5},{7,8},{8,7},{9,10},{10,9},{11,... | collective-permute-start | bytes 786440 | tf_op jit(solution)/shard_map/ppermute | solution.py:372
  28.5 10.2 %collective-permute-start = (bf16[8,64,256]{2,1,0:T(8,128)(2,1)S(1)}, bf16[8,64,256]{2,1,0:T(8,128)(2,1)S(1)}, u32[]{:S(2)}, u32[]{:S(2)}) collective-permute-start(bf16[8,64,256]{2,1,0:T(8,128)(2,1)S(1)} %get-tuple-element.18.refs_4_), channel_id=1, source_target_pairs={{0,1},{1,0},{2,3},{3,2},{4,5},{5,4},{6,7},{7,6},{8,9},{9,8},{10,11... | collective-permute-start | bytes 786440 | tf_op jit(solution)/shard_map/ppermute | solution.py:372
  46.3 14.4 %collective-permute-start.7 = (bf16[8,64,256]{2,1,0:T(8,128)(2,1)S(1)}, bf16[8,64,256]{2,1,0:T(8,128)(2,1)S(1)}, u32[]{:S(2)}, u32[]{:S(2)}) collective-permute-start(bf16[8,64,256]{2,1,0:T(8,128)(2,1)S(1)} %get-tuple-element.24.refs_3_), channel_id=1, source_target_pairs={{16,32},{32,16},{48,64},{64,48},{80,96},{96,80},{112,0},{0,112},{1... | collective-permute-start | bytes 786440 | tf_op jit(solution)/shard_map/ppermute | solution.py:372
  47.8 12.8 %collective-permute-start.6 = (bf16[8,64,256]{2,1,0:T(8,128)(2,1)S(1)}, bf16[8,64,256]{2,1,0:T(8,128)(2,1)S(1)}, u32[]{:S(2)}, u32[]{:S(2)}) collective-permute-start(bf16[8,64,256]{2,1,0:T(8,128)(2,1)S(1)} %get-tuple-element.24.refs_3_), channel_id=1, source_target_pairs={{0,16},{16,0},{32,48},{48,32},{64,80},{80,64},{96,112},{112,96},{1... | collective-permute-start | bytes 786440 | tf_op jit(solution)/shard_map/ppermute | solution.py:372
  48.2 12.4 %collective-permute-start.5 = (bf16[8,64,256]{2,1,0:T(8,128)(2,1)S(1)}, bf16[8,64,256]{2,1,0:T(8,128)(2,1)S(1)}, u32[]{:S(2)}, u32[]{:S(2)}) collective-permute-start(bf16[8,64,256]{2,1,0:T(8,128)(2,1)S(1)} %get-tuple-element.24.refs_3_), channel_id=1, source_target_pairs={{1,2},{2,1},{3,4},{4,3},{5,6},{6,5},{7,8},{8,7},{9,10},{10,9},{11,... | collective-permute-start | bytes 786440 | tf_op jit(solution)/shard_map/ppermute | solution.py:372
  48.4 12.2 %collective-permute-start.4 = (bf16[8,64,256]{2,1,0:T(8,128)(2,1)S(1)}, bf16[8,64,256]{2,1,0:T(8,128)(2,1)S(1)}, u32[]{:S(2)}, u32[]{:S(2)}) collective-permute-start(bf16[8,64,256]{2,1,0:T(8,128)(2,1)S(1)} %get-tuple-element.24.refs_3_), channel_id=1, source_target_pairs={{0,1},{1,0},{2,3},{3,2},{4,5},{5,4},{6,7},{7,6},{8,9},{9,8},{10,11... | collective-permute-start | bytes 786440 | tf_op jit(solution)/shard_map/ppermute | solution.py:372
  66.6 13.0 %collective-permute-start.11 = (bf16[8,64,256]{2,1,0:T(8,128)(2,1)S(1)}, bf16[8,64,256]{2,1,0:T(8,128)(2,1)S(1)}, u32[]{:S(2)}, u32[]{:S(2)}) collective-permute-start(bf16[8,64,256]{2,1,0:T(8,128)(2,1)S(1)} %get-tuple-element.27.refs_3_), channel_id=1, source_target_pairs={{16,32},{32,16},{48,64},{64,48},{80,96},{96,80},{112,0},{0,112},{1... | collective-permute-start | bytes 786440 | tf_op jit(solution)/shard_map/ppermute | solution.py:372
  68.6 11.0 %collective-permute-start.10 = (bf16[8,64,256]{2,1,0:T(8,128)(2,1)S(1)}, bf16[8,64,256]{2,1,0:T(8,128)(2,1)S(1)}, u32[]{:S(2)}, u32[]{:S(2)}) collective-permute-start(bf16[8,64,256]{2,1,0:T(8,128)(2,1)S(1)} %get-tuple-element.27.refs_3_), channel_id=1, source_target_pairs={{0,16},{16,0},{32,48},{48,32},{64,80},{80,64},{96,112},{112,96},{1... | collective-permute-start | bytes 786440 | tf_op jit(solution)/shard_map/ppermute | solution.py:372
  69.4 10.2 %collective-permute-start.9 = (bf16[8,64,256]{2,1,0:T(8,128)(2,1)S(1)}, bf16[8,64,256]{2,1,0:T(8,128)(2,1)S(1)}, u32[]{:S(2)}, u32[]{:S(2)}) collective-permute-start(bf16[8,64,256]{2,1,0:T(8,128)(2,1)S(1)} %get-tuple-element.27.refs_3_), channel_id=1, source_target_pairs={{1,2},{2,1},{3,4},{4,3},{5,6},{6,5},{7,8},{8,7},{9,10},{10,9},{11,... | collective-permute-start | bytes 786440 | tf_op jit(solution)/shard_map/ppermute | solution.py:372
  69.4 10.2 %collective-permute-start.8 = (bf16[8,64,256]{2,1,0:T(8,128)(2,1)S(1)}, bf16[8,64,256]{2,1,0:T(8,128)(2,1)S(1)}, u32[]{:S(2)}, u32[]{:S(2)}) collective-permute-start(bf16[8,64,256]{2,1,0:T(8,128)(2,1)S(1)} %get-tuple-element.27.refs_3_), channel_id=1, source_target_pairs={{0,1},{1,0},{2,3},{3,2},{4,5},{5,4},{6,7},{7,6},{8,9},{9,8},{10,11... | collective-permute-start | bytes 786440 | tf_op jit(solution)/shard_map/ppermute | solution.py:372

commit v5 on v4

--- a/solution.py
+++ b/solution.py
@@ -37,7 +37,7 @@
         if arrive is not None:
             arrive(step)
 
-        @pl.loop(0, ROWS // PAIR)
+        @pl.loop(0, ROWS // PAIR, unroll=4)
         def _(pair):
             row = start + pair * PAIR
             for first in range(0, count, GROUP):
@@ -59,13 +59,15 @@
                     partial_ref[1, r, place, :] = value[:, LANES:]
 
         for r in range(count):
-            for half in range(2):
-                parts = []
-                for eight in range(ROWS // 8):
-                    parts.append(
-                        total([partial_ref[half, r, pl.ds(eight * 64 + j, 8, stride=8), :] for j in range(8)])
-                    )
-                finish(r, pl.ds(start, ROWS), half, jnp.concatenate(parts, axis=0))
+            sums = [
+                [
+                    total([partial_ref[half, r, pl.ds(eight * 64 + j, 8, stride=8), :] for j in range(8)])
+                    for half in range(2)
+                ]
+                for eight in range(ROWS // 8)
+            ]
+            sums = jnp.concatenate([jnp.concatenate(halves, axis=1) for halves in sums], axis=0)
+            finish(r, pl.ds(start, ROWS), sums)
 
 
 def prepare_kernel(block_ref, off_ref, inverse_ref):
@@ -214,10 +216,6 @@
     return slice(16 * i, 16 * i + 16)
 
 
-def lanes(half):
-    return slice(half * LANES, half * LANES + LANES)
-
-
 def loads(pieces, kept_ref, sems):
     copies = []
     for step in range(kept_ref.shape[1] // ROWS):
@@ -254,7 +252,7 @@
     count, components, sites = rounded_ref.shape
     lane = lax.broadcasted_iota(jnp.int32, (components, sites), 1) % LX
 
-    @pl.loop(0, count)
+    @pl.loop(0, count, unroll=8)
     def _(r):
         value = rounded_ref[r].astype(F32)
         after = jnp.where(lane == LX - 1, pltpu.roll(value, LX - 1, 1), pltpu.roll(value, sites - 1, 1))
@@ -269,11 +267,10 @@
     for k in range(NEAR - 1):
         vectors.append(lambda r, i, k=k: near_ref[k, r, sixteen(i), :])
 
-    def finish(r, rows, half, sums):
-        part = lanes(half)
-        left = source_ref[r, rows, part].astype(F32) - sums
-        kept = iterate_ref[r, rows, part] - rounded_ref[r, rows, part].astype(F32)
-        base_ref[r, rows, part] = kept + left * inverse_ref[rows, part]
+    def finish(r, rows, sums):
+        left = source_ref[r, rows, :].astype(F32) - sums
+        kept = iterate_ref[r, rows, :] - rounded_ref[r, rows, :].astype(F32)
+        base_ref[r, rows, :] = kept + left * inverse_ref[rows, :]
 
     multiply(blocks, vectors, partial_ref, finish, arrive)
 
@@ -333,12 +330,11 @@
         blocks.append(lambda o, i, k=k: stencil_ref[k, o, sixteen(i), :])
         vectors.append(lambda r, i, ref=ref: ref[r, sixteen(i), :])
 
-    def finish(r, rows, half, sums):
-        part = lanes(half)
-        iterate = base_ref[r, rows, part] - sums * inverse_ref[rows, part]
+    def finish(r, rows, sums):
+        iterate = base_ref[r, rows, :] - sums * inverse_ref[rows, :]
         if not last:
-            iterate_ref[r, rows, part] = iterate
-        rounded_ref[r, rows, part] = iterate.astype(BF16)
+            iterate_ref[r, rows, :] = iterate
+        rounded_ref[r, rows, :] = iterate.astype(BF16)
 
     multiply(blocks, vectors, partial_ref, finish, arrive)
 

time: 106 us -> 102 us (0.962)
  Pallas kernels: 49.8 us -> 45.9 us
  starting transfers between devices: 25.4 us -> 26.9 us
    pallas_call x3, Pallas kernels: 25.7 us -> 23.2 us  [local(): pl.pallas_call(functools.partial(local_kernel, first), in_specs=(hbm(2) i...]
    ppermute x12, starting transfers between devices: 15 us -> 16.5 us  [pairs(): return lax.ppermute(plane, axis, swaps)]
    pallas_call x3, Pallas kernels: 19.4 us -> 18 us  [remote(): pl.pallas_call(functools.partial(remote_kernel, first, last), in_specs=(h...]
  transfers between devices with their start and end apart: 13 -> 13, of which waited for: 1 -> 1; matrix products, arithmetic and copies ran while one was open for 0% -> 0% of each run, Pallas kernels for 26% -> 24%
where the time goes in v5:
time: 102 us
  Pallas kernels  45.9 us (45%)
  starting transfers between devices  26.9 us (26%)
  blocking collectives  17.6 us (17%)
  waiting for transfers between devices  10.7 us (10%)
    pallas_call x3, Pallas kernels, local(): pl.pallas_call(functools.partial(local_kernel, first), in_specs=(hbm(2) i...  23.2 us
    pallas_call x3, Pallas kernels, remote(): pl.pallas_call(functools.partial(remote_kernel, first, last), in_specs=(h...  18 us
    all_to_all x1, blocking collectives, exchange(): lax.all_to_all(chunks, ('zt', 'xy'), 0, 0, axis_index_groups=groups(), ti...  17.6 us
    ppermute x12, starting transfers between devices, pairs(): return lax.ppermute(plane, axis, swaps)  16.5 us
    all_to_all x1, waiting for transfers between devices, exchange(): lax.all_to_all(chunks, ('zt', 'xy'), 0, 0, axis_index_groups=groups(), ti...  10.7 us
    all_to_all x1, starting transfers between devices, exchange(): lax.all_to_all(chunks, ('zt', 'xy'), 0, 0, axis_index_groups=groups(), ti...  10.4 us
  transfers between devices with their start and end apart: 13, of which 1 were waited for; matrix products, arithmetic and copies ran while one was open for 0% of the time, Pallas kernels for 24%

profile of v5, /device:TPU:1, one launch (start us, length us, event | category | flops | bytes accessed | tf_op | source)
XLA Modules:
  0.0 102.2 jit_solution(1258374240274633172)
XLA Ops:
  0.0 0.9 copy-done
  1.0 1.1 %split.1 = bf16[2,2,8,16,512]{4,3,2,1,0:T(8,128)(2,1)} custom-call(bf16[512,256]{1,0:T(8,128)(2,1)S(1)} %bitcast.12), custom_call_target="tpu_custom_call" | custom-call | tf_op jit(solution)/shard_map/split/pallas_call | solution.py:127
  2.0 10.4 %all-to-all-start = ((bf16[32,16,512]{2,1,0:T(8,128)(2,1)}), bf16[32,16,512]{2,1,0:T(8,128)(2,1)S(1)}, u32[]{:S(2)}, u32[]{:S(2)}) async-start(bf16[32,16,512]{2,1,0:T(8,128)(2,1)} %bitcast.2), calls=%async_computation | async-start | bytes 1048576 | tf_op jit(solution)/shard_map/all_to_all | solution.py:377
  12.4 1.8 %prepare.1 = (bf16[64,64,256]{2,1,0:T(8,128)(2,1)S(1)}, f32[64,256]{1,0:T(8,128)S(1)}) custom-call(bf16[9,64,64,256]{3,2,1,0:T(8,128)(2,1)} %bitcast.13), custom_call_target="tpu_custom_call" | custom-call | flops 10000000 | bytes 4194304 | tf_op jit(solution)/shard_map/prepare/pallas_call | solution.py:92
  14.2 10.7 %all-to-all-done = bf16[32,16,512]{2,1,0:T(8,128)(2,1)S(1)} async-done(((bf16[32,16,512]{2,1,0:T(8,128)(2,1)}), bf16[32,16,512]{2,1,0:T(8,128)(2,1)S(1)}, u32[]{:S(2)}, u32[]{:S(2)}) %all-to-all-start) | async-done | bytes 524320 | tf_op jit(solution)/shard_map/all_to_all | solution.py:377
  24.9 0.4 start.1
  25.3 2.3 %collective-permute-start.3 = (bf16[8,64,256]{2,1,0:T(8,128)(2,1)S(1)}, bf16[8,64,256]{2,1,0:T(8,128)(2,1)S(1)}, u32[]{:S(2)}, u32[]{:S(2)}) collective-permute-start(bf16[8,64,256]{2,1,0:T(8,128)(2,1)S(1)} %get-tuple-element.18.refs_4_), channel_id=1, source_target_pairs={{16,32},{32,16},{48,64},{64,48},{80,96},{96,80},{112,0},{0,112},{1... | collective-permute-start | bytes 786440 | tf_op jit(solution)/shard_map/ppermute | solution.py:368
  27.6 0.9 collective-permute-start.1
  28.5 1.1 %collective-permute-start = (bf16[8,64,256]{2,1,0:T(8,128)(2,1)S(1)}, bf16[8,64,256]{2,1,0:T(8,128)(2,1)S(1)}, u32[]{:S(2)}, u32[]{:S(2)}) collective-permute-start(bf16[8,64,256]{2,1,0:T(8,128)(2,1)S(1)} %get-tuple-element.18.refs_4_), channel_id=1, source_target_pairs={{0,1},{1,0},{2,3},{3,2},{4,5},{5,4},{6,7},{7,6},{8,9},{9,8},{10,11... | collective-permute-start | bytes 786440 | tf_op jit(solution)/shard_map/ppermute | solution.py:368
  29.6 8.5 %local.3 = (f32[8,64,256]{2,1,0:T(8,128)S(1)}, bf16[5,64,64,256]{3,2,1,0:T(8,128)(2,1)S(1)}) custom-call(bf16[1,64,64,256]{3,2,1,0:T(8,128)(2,1)S(1)} %bitcast.11, bf16[9,64,64,256]{3,2,1,0:T(8,128)(2,1)} %bitcast.14, bf16[8,64,256]{2,1,0:T(8,128)(2,1)S(1)} %get-tuple-element.20.refs_2_.refs_1_, f32[8,64,256]{2,1,0:T(8,128)S(1)} %get-tuple-element.21.refs_3_, ...), custom_call_target="tpu_custom_call" | custom-call | flops 1000000000 | bytes 12582912 | tf_op jit(solution)/shard_map/local/pallas_call | solution.py:298
  38.2 7.1 %remote.3 = (f32[8,64,256]{2,1,0:T(8,128)S(1)}, bf16[8,64,256]{2,1,0:T(8,128)(2,1)S(1)}, bf16[4,64,64,256]{3,2,1,0:T(8,128)(2,1)S(1)}) custom-call(bf16[9,64,64,256]{3,2,1,0:T(8,128)(2,1)} %bitcast.15, bf16[8,64,256]{2,1,0:T(8,128)(2,1)S(1)} %collective-permute-done.refs_1_, bf16[8,64,256]{2,1,0:T(8,128)(2,1)S(1)} %collective-permute-done.1.refs_2_, ...), custom_call_target="tpu_custom_call" | custom-call | flops 1000000000 | bytes 12582912 | tf_op jit(solution)/shard_map/remote/pallas_call | solution.py:350
  45.3 2.1 %collective-permute-start.7 = (bf16[8,64,256]{2,1,0:T(8,128)(2,1)S(1)}, bf16[8,64,256]{2,1,0:T(8,128)(2,1)S(1)}, u32[]{:S(2)}, u32[]{:S(2)}) collective-permute-start(bf16[8,64,256]{2,1,0:T(8,128)(2,1)S(1)} %get-tuple-element.24.refs_3_), channel_id=1, source_target_pairs={{16,32},{32,16},{48,64},{64,48},{80,96},{96,80},{112,0},{0,112},{1... | collective-permute-start | bytes 786440 | tf_op jit(solution)/shard_map/ppermute | solution.py:368
  47.4 0.1 collective-permute-start.5
  47.5 3.9 %collective-permute-start.4 = (bf16[8,64,256]{2,1,0:T(8,128)(2,1)S(1)}, bf16[8,64,256]{2,1,0:T(8,128)(2,1)S(1)}, u32[]{:S(2)}, u32[]{:S(2)}) collective-permute-start(bf16[8,64,256]{2,1,0:T(8,128)(2,1)S(1)} %get-tuple-element.24.refs_3_), channel_id=1, source_target_pairs={{0,1},{1,0},{2,3},{3,2},{4,5},{5,4},{6,7},{7,6},{8,9},{9,8},{10,11... | collective-permute-start | bytes 786440 | tf_op jit(solution)/shard_map/ppermute | solution.py:368
  51.3 7.3 %local.4.refs_5_ = f32[8,64,256]{2,1,0:T(8,128)S(1)} custom-call(bf16[5,64,64,256]{3,2,1,0:T(8,128)(2,1)S(1)} %get-tuple-element.25.refs_0_, bf16[8,64,256]{2,1,0:T(8,128)(2,1)S(1)} %get-tuple-element.20.refs_2_.refs_1_, f32[8,64,256]{2,1,0:T(8,128)S(1)} %get-tuple-element.26.refs_2_, bf16[8,64,256]{2,1,0:T(8,128)(2,1)S(1)} %get-tuple-element.24.refs_3_, ...), custom_call_target="tpu_custom_call" | custom-call | flops 1000000000 | bytes 12582912 | tf_op jit(solution)/shard_map/local/pallas_call | solution.py:298
  58.7 5.5 %remote.4 = (f32[8,64,256]{2,1,0:T(8,128)S(1)}, bf16[8,64,256]{2,1,0:T(8,128)(2,1)S(1)}) custom-call(bf16[4,64,64,256]{3,2,1,0:T(8,128)(2,1)S(1)} %get-tuple-element.23.refs_0_, bf16[8,64,256]{2,1,0:T(8,128)(2,1)S(1)} %collective-permute-done.4.refs_1_, bf16[8,64,256]{2,1,0:T(8,128)(2,1)S(1)} %collective-permute-done.5.refs_2_, ...), custom_call_target="tpu_custom_call" | custom-call | flops 1000000000 | bytes 12582912 | tf_op jit(solution)/shard_map/remote/pallas_call | solution.py:350
  64.2 2.0 %collective-permute-start.11 = (bf16[8,64,256]{2,1,0:T(8,128)(2,1)S(1)}, bf16[8,64,256]{2,1,0:T(8,128)(2,1)S(1)}, u32[]{:S(2)}, u32[]{:S(2)}) collective-permute-start(bf16[8,64,256]{2,1,0:T(8,128)(2,1)S(1)} %get-tuple-element.27.refs_3_), channel_id=1, source_target_pairs={{16,32},{32,16},{48,64},{64,48},{80,96},{96,80},{112,0},{0,112},{1... | collective-permute-start | bytes 786440 | tf_op jit(solution)/shard_map/ppermute | solution.py:368
  66.2 0.8 collective-permute-start.10
  67.0 3.3 %collective-permute-start.8 = (bf16[8,64,256]{2,1,0:T(8,128)(2,1)S(1)}, bf16[8,64,256]{2,1,0:T(8,128)(2,1)S(1)}, u32[]{:S(2)}, u32[]{:S(2)}) collective-permute-start(bf16[8,64,256]{2,1,0:T(8,128)(2,1)S(1)} %get-tuple-element.27.refs_3_), channel_id=1, source_target_pairs={{0,1},{1,0},{2,3},{3,2},{4,5},{5,4},{6,7},{7,6},{8,9},{9,8},{10,11... | collective-permute-start | bytes 786440 | tf_op jit(solution)/shard_map/ppermute | solution.py:368
  70.3 7.3 %local.5.refs_5_ = f32[8,64,256]{2,1,0:T(8,128)S(1)} custom-call(bf16[5,64,64,256]{3,2,1,0:T(8,128)(2,1)S(1)} %get-tuple-element.25.refs_0_, bf16[8,64,256]{2,1,0:T(8,128)(2,1)S(1)} %get-tuple-element.20.refs_2_.refs_1_, f32[8,64,256]{2,1,0:T(8,128)S(1)} %get-tuple-element.28.refs_2_, bf16[8,64,256]{2,1,0:T(8,128)(2,1)S(1)} %get-tuple-element.27.refs_3_, ...), custom_call_target="tpu_custom_call" | custom-call | flops 1000000000 | bytes 12582912 | tf_op jit(solution)/shard_map/local/pallas_call | solution.py:298
  77.7 5.4 %remote.5.rounded_ref = bf16[8,64,256]{2,1,0:T(8,128)(2,1)S(1)} custom-call(bf16[4,64,64,256]{3,2,1,0:T(8,128)(2,1)S(1)} %get-tuple-element.23.refs_0_, bf16[8,64,256]{2,1,0:T(8,128)(2,1)S(1)} %collective-permute-done.8.refs_1_, bf16[8,64,256]{2,1,0:T(8,128)(2,1)S(1)} %collective-permute-done.9.refs_2_, ...), custom_call_target="tpu_custom_call" | custom-call | flops 1000000000 | bytes 12582912 | tf_op jit(solution)/shard_map/remote/pallas_call | solution.py:350
  83.2 0.3 leave.1
  83.5 17.6 %all_to_all.10 = bf16[32,16,512]{2,1,0:T(8,128)(2,1)S(1)} all-to-all(bf16[32,16,512]{2,1,0:T(8,128)(2,1)S(1)} %bitcast.9), channel_id=1, replica_groups={{0,1,2,3,4,5,6,7,8,9,10,11,12,13,14,15,16,17,18,19,20,21,22,23,24,25,26..., dimensions={0} | all-to-all | bytes 1048576 | tf_op jit(solution)/shard_map/all_to_all | solution.py:377
  101.1 1.1 %join.1 = f32[512,256]{1,0:T(8,128)} custom-call(bf16[2,2,128,512]{3,2,1,0:T(8,128)(2,1)S(1)} %bitcast.10), custom_call_target="tpu_custom_call" | custom-call | tf_op jit(solution)/shard_map/join/pallas_call | solution.py:207
  (16 shorter events, 0.0 us)
Async XLA Ops:
  0.0 0.9 copy-start
  2.0 22.9 %all-to-all-start = ((bf16[32,16,512]{2,1,0:T(8,128)(2,1)}), bf16[32,16,512]{2,1,0:T(8,128)(2,1)S(1)}, u32[]{:S(2)}, u32[]{:S(2)}) async-start(bf16[32,16,512]{2,1,0:T(8,128)(2,1)} %bitcast.2), calls=%async_computation | async-start | bytes 1048576 | tf_op jit(solution)/shard_map/all_to_all | solution.py:377
  25.3 12.9 %collective-permute-start.3 = (bf16[8,64,256]{2,1,0:T(8,128)(2,1)S(1)}, bf16[8,64,256]{2,1,0:T(8,128)(2,1)S(1)}, u32[]{:S(2)}, u32[]{:S(2)}) collective-permute-start(bf16[8,64,256]{2,1,0:T(8,128)(2,1)S(1)} %get-tuple-element.18.refs_4_), channel_id=1, source_target_pairs={{16,32},{32,16},{48,64},{64,48},{80,96},{96,80},{112,0},{0,112},{1... | collective-permute-start | bytes 786440 | tf_op jit(solution)/shard_map/ppermute | solution.py:368
  27.6 10.6 %collective-permute-start.2 = (bf16[8,64,256]{2,1,0:T(8,128)(2,1)S(1)}, bf16[8,64,256]{2,1,0:T(8,128)(2,1)S(1)}, u32[]{:S(2)}, u32[]{:S(2)}) collective-permute-start(bf16[8,64,256]{2,1,0:T(8,128)(2,1)S(1)} %get-tuple-element.18.refs_4_), channel_id=1, source_target_pairs={{0,16},{16,0},{32,48},{48,32},{64,80},{80,64},{96,112},{112,96},{1... | collective-permute-start | bytes 786440 | tf_op jit(solution)/shard_map/ppermute | solution.py:368
  27.6 10.6 %collective-permute-start.1 = (bf16[8,64,256]{2,1,0:T(8,128)(2,1)S(1)}, bf16[8,64,256]{2,1,0:T(8,128)(2,1)S(1)}, u32[]{:S(2)}, u32[]{:S(2)}) collective-permute-start(bf16[8,64,256]{2,1,0:T(8,128)(2,1)S(1)} %get-tuple-element.18.refs_4_), channel_id=1, source_target_pairs={{1,2},{2,1},{3,4},{4,3},{5,6},{6,5},{7,8},{8,7},{9,10},{10,9},{11,... | collective-permute-start | bytes 786440 | tf_op jit(solution)/shard_map/ppermute | solution.py:368
  28.5 9.7 %collective-permute-start = (bf16[8,64,256]{2,1,0:T(8,128)(2,1)S(1)}, bf16[8,64,256]{2,1,0:T(8,128)(2,1)S(1)}, u32[]{:S(2)}, u32[]{:S(2)}) collective-permute-start(bf16[8,64,256]{2,1,0:T(8,128)(2,1)S(1)} %get-tuple-element.18.refs_4_), channel_id=1, source_target_pairs={{0,1},{1,0},{2,3},{3,2},{4,5},{5,4},{6,7},{7,6},{8,9},{9,8},{10,11... | collective-permute-start | bytes 786440 | tf_op jit(solution)/shard_map/ppermute | solution.py:368
  45.3 13.3 %collective-permute-start.7 = (bf16[8,64,256]{2,1,0:T(8,128)(2,1)S(1)}, bf16[8,64,256]{2,1,0:T(8,128)(2,1)S(1)}, u32[]{:S(2)}, u32[]{:S(2)}) collective-permute-start(bf16[8,64,256]{2,1,0:T(8,128)(2,1)S(1)} %get-tuple-element.24.refs_3_), channel_id=1, source_target_pairs={{16,32},{32,16},{48,64},{64,48},{80,96},{96,80},{112,0},{0,112},{1... | collective-permute-start | bytes 786440 | tf_op jit(solution)/shard_map/ppermute | solution.py:368
  47.4 11.3 %collective-permute-start.6 = (bf16[8,64,256]{2,1,0:T(8,128)(2,1)S(1)}, bf16[8,64,256]{2,1,0:T(8,128)(2,1)S(1)}, u32[]{:S(2)}, u32[]{:S(2)}) collective-permute-start(bf16[8,64,256]{2,1,0:T(8,128)(2,1)S(1)} %get-tuple-element.24.refs_3_), channel_id=1, source_target_pairs={{0,16},{16,0},{32,48},{48,32},{64,80},{80,64},{96,112},{112,96},{1... | collective-permute-start | bytes 786440 | tf_op jit(solution)/shard_map/ppermute | solution.py:368
  47.4 11.3 %collective-permute-start.5 = (bf16[8,64,256]{2,1,0:T(8,128)(2,1)S(1)}, bf16[8,64,256]{2,1,0:T(8,128)(2,1)S(1)}, u32[]{:S(2)}, u32[]{:S(2)}) collective-permute-start(bf16[8,64,256]{2,1,0:T(8,128)(2,1)S(1)} %get-tuple-element.24.refs_3_), channel_id=1, source_target_pairs={{1,2},{2,1},{3,4},{4,3},{5,6},{6,5},{7,8},{8,7},{9,10},{10,9},{11,... | collective-permute-start | bytes 786440 | tf_op jit(solution)/shard_map/ppermute | solution.py:368
  47.5 11.2 %collective-permute-start.4 = (bf16[8,64,256]{2,1,0:T(8,128)(2,1)S(1)}, bf16[8,64,256]{2,1,0:T(8,128)(2,1)S(1)}, u32[]{:S(2)}, u32[]{:S(2)}) collective-permute-start(bf16[8,64,256]{2,1,0:T(8,128)(2,1)S(1)} %get-tuple-element.24.refs_3_), channel_id=1, source_target_pairs={{0,1},{1,0},{2,3},{3,2},{4,5},{5,4},{6,7},{7,6},{8,9},{9,8},{10,11... | collective-permute-start | bytes 786440 | tf_op jit(solution)/shard_map/ppermute | solution.py:368
  64.2 13.5 %collective-permute-start.11 = (bf16[8,64,256]{2,1,0:T(8,128)(2,1)S(1)}, bf16[8,64,256]{2,1,0:T(8,128)(2,1)S(1)}, u32[]{:S(2)}, u32[]{:S(2)}) collective-permute-start(bf16[8,64,256]{2,1,0:T(8,128)(2,1)S(1)} %get-tuple-element.27.refs_3_), channel_id=1, source_target_pairs={{16,32},{32,16},{48,64},{64,48},{80,96},{96,80},{112,0},{0,112},{1... | collective-permute-start | bytes 786440 | tf_op jit(solution)/shard_map/ppermute | solution.py:368
  66.2 11.5 %collective-permute-start.10 = (bf16[8,64,256]{2,1,0:T(8,128)(2,1)S(1)}, bf16[8,64,256]{2,1,0:T(8,128)(2,1)S(1)}, u32[]{:S(2)}, u32[]{:S(2)}) collective-permute-start(bf16[8,64,256]{2,1,0:T(8,128)(2,1)S(1)} %get-tuple-element.27.refs_3_), channel_id=1, source_target_pairs={{0,16},{16,0},{32,48},{48,32},{64,80},{80,64},{96,112},{112,96},{1... | collective-permute-start | bytes 786440 | tf_op jit(solution)/shard_map/ppermute | solution.py:368
  67.0 10.7 %collective-permute-start.9 = (bf16[8,64,256]{2,1,0:T(8,128)(2,1)S(1)}, bf16[8,64,256]{2,1,0:T(8,128)(2,1)S(1)}, u32[]{:S(2)}, u32[]{:S(2)}) collective-permute-start(bf16[8,64,256]{2,1,0:T(8,128)(2,1)S(1)} %get-tuple-element.27.refs_3_), channel_id=1, source_target_pairs={{1,2},{2,1},{3,4},{4,3},{5,6},{6,5},{7,8},{8,7},{9,10},{10,9},{11,... | collective-permute-start | bytes 786440 | tf_op jit(solution)/shard_map/ppermute | solution.py:368
  67.0 10.7 %collective-permute-start.8 = (bf16[8,64,256]{2,1,0:T(8,128)(2,1)S(1)}, bf16[8,64,256]{2,1,0:T(8,128)(2,1)S(1)}, u32[]{:S(2)}, u32[]{:S(2)}) collective-permute-start(bf16[8,64,256]{2,1,0:T(8,128)(2,1)S(1)} %get-tuple-element.27.refs_3_), channel_id=1, source_target_pairs={{0,1},{1,0},{2,3},{3,2},{4,5},{5,4},{6,7},{7,6},{8,9},{9,8},{10,11... | collective-permute-start | bytes 786440 | tf_op jit(solution)/shard_map/ppermute | solution.py:368

commit v6 on v5

--- a/solution.py
+++ b/solution.py
@@ -241,9 +241,10 @@
 def local_kernel(first, *refs):
     if first:
         off_ref, far_ref, source_ref, iterate_ref, rounded_ref, inverse_ref = refs[:6]
-        base_ref, stencil_ref, near_ref, partial_ref, sems = refs[6:]
+        base_ref, stencil_ref, far_kept_ref, near_ref, partial_ref, sems, far_sems = refs[6:]
         pieces = [(off_ref, 0, 0, 1), (far_ref, 1, 1, NEAR - 1)]
-        for copy in loads(pieces, stencil_ref, sems):
+        far_copies = loads([(far_ref, NEAR, 0, far_kept_ref.shape[0])], far_kept_ref, far_sems)
+        for copy in loads(pieces, stencil_ref, sems) + far_copies:
             copy.start()
         arrive = arrival(pieces, stencil_ref, sems)
     else:
@@ -273,6 +274,9 @@
         base_ref[r, rows, :] = kept + left * inverse_ref[rows, :]
 
     multiply(blocks, vectors, partial_ref, finish, arrive)
+    if first:
+        for copy in far_copies:
+            copy.wait()
 
 
 def vmem(count):
@@ -286,20 +290,25 @@
 def local(stencil, source, iterate, rounded, inverse):
     count, components, sites = rounded.shape
     first = isinstance(stencil, tuple)
-    kept = (NEAR, components, components, sites)
+    block = (components, components, sites)
     scratch = [
         pltpu.VMEM((4, count, components, sites), BF16),
         pltpu.VMEM((2, count, ROWS * 8, LANES), F32),
     ]
     if first:
         scratch.append(pltpu.SemaphoreType.DMA((2, components // ROWS)))
+        scratch.append(pltpu.SemaphoreType.DMA((1, components // ROWS)))
     base = jax.ShapeDtypeStruct(rounded.shape, F32)
     blocks = stencil if first else (stencil,)
     return pl.pallas_call(
         functools.partial(local_kernel, first),
         in_specs=(hbm(2) if first else vmem(1)) + vmem(4),
-        out_specs=vmem(2) if first else vmem(1)[0],
-        out_shape=[base, pltpu.VMEM(kept, BF16)] if first else base,
+        out_specs=vmem(3) if first else vmem(1)[0],
+        out_shape=(
+            [base, pltpu.VMEM((NEAR, *block), BF16), pltpu.VMEM((stencil[1].shape[0] - NEAR, *block), BF16)]
+            if first
+            else base
+        ),
         scratch_shapes=scratch,
         compiler_params=SMALL,
         cost_estimate=pl.CostEstimate(flops=10**9, bytes_accessed=12 * 2**20, transcendentals=0),
@@ -307,21 +316,12 @@
     )(*blocks, source, iterate, rounded, inverse)
 
 
-def remote_kernel(first, last, *refs):
-    if first:
-        whole_ref, z0_ref, z1_ref, t0_ref, t1_ref, base_ref, inverse_ref = refs[:7]
-        iterate_ref, rounded_ref, stencil_ref, partial_ref, sems = refs[7:]
-        pieces = [(whole_ref, NEAR, 0, stencil_ref.shape[0])]
-        for copy in loads(pieces, stencil_ref, sems):
-            copy.start()
-        arrive = arrival(pieces, stencil_ref, sems)
+def remote_kernel(last, *refs):
+    stencil_ref, t0_ref, t1_ref, z0_ref, z1_ref, base_ref, inverse_ref = refs[:7]
+    if last:
+        rounded_ref, partial_ref = refs[7:]
     else:
-        stencil_ref, z0_ref, z1_ref, t0_ref, t1_ref, base_ref, inverse_ref = refs[:7]
-        if last:
-            rounded_ref, partial_ref = refs[7:]
-        else:
-            iterate_ref, rounded_ref, partial_ref = refs[7:]
-        arrive = None
+        iterate_ref, rounded_ref, partial_ref = refs[7:]
 
     z_odd = lax.axis_index("xy") % 2
     t_odd = lax.axis_index("zt") % 2
@@ -336,23 +336,18 @@
             iterate_ref[r, rows, :] = iterate
         rounded_ref[r, rows, :] = iterate.astype(BF16)
 
-    multiply(blocks, vectors, partial_ref, finish, arrive)
-
-
-def remote(stencil, halos, base, inverse, first, last):
-    count, components, sites = base.shape
+    multiply(blocks, vectors, partial_ref, finish)
+
+
+def remote(stencil, halos, base, inverse, last):
+    count = base.shape[0]
     types = [BF16] if last else [F32, BF16]
-    shapes = [jax.ShapeDtypeStruct(base.shape, t) for t in types]
-    scratch = [pltpu.VMEM((2, count, ROWS * 8, LANES), F32)]
-    if first:
-        shapes.append(pltpu.VMEM((stencil.shape[0] - NEAR, components, components, sites), BF16))
-        scratch.append(pltpu.SemaphoreType.DMA((1, components // ROWS)))
-    return pl.pallas_call(
-        functools.partial(remote_kernel, first, last),
-        in_specs=(hbm(1) if first else vmem(1)) + vmem(6),
-        out_specs=vmem(len(shapes)),
-        out_shape=shapes,
-        scratch_shapes=scratch,
+    return pl.pallas_call(
+        functools.partial(remote_kernel, last),
+        in_specs=vmem(7),
+        out_specs=vmem(len(types)),
+        out_shape=[jax.ShapeDtypeStruct(base.shape, t) for t in types],
+        scratch_shapes=[pltpu.VMEM((2, count, ROWS * 8, LANES), F32)],
         compiler_params=SMALL,
         cost_estimate=pl.CostEstimate(flops=10**9, bytes_accessed=12 * 2**20, transcendentals=0),
         name="remote",
@@ -392,20 +387,17 @@
     for sweep in range(SWEEPS - 1):
         last = sweep == SWEEPS - 2
         halos = [
+            pairs(rounded, "zt", 0),
+            pairs(rounded, "zt", 1),
             pairs(rounded, "xy", 0),
             pairs(rounded, "xy", 1),
-            pairs(rounded, "zt", 0),
-            pairs(rounded, "zt", 1),
         ]
         if sweep == 0:
-            base, near = local((off[None], stencil), source, iterate, rounded, inverse)
-            iterate, rounded, far = remote(stencil, halos, base, inverse, True, False)
-        elif not last:
-            base = local(near, source, iterate, rounded, inverse)
-            iterate, rounded = remote(far, halos, base, inverse, False, False)
+            base, near, far = local((off[None], stencil), source, iterate, rounded, inverse)
         else:
             base = local(near, source, iterate, rounded, inverse)
-            (rounded,) = remote(far, halos, base, inverse, False, True)
+        *iterate, rounded = remote(far, halos, base, inverse, last)
+        iterate = None if last else iterate[0]
 
     chunks = leave(rounded, columns)
     received = exchange(chunks.reshape(2 * columns, cells, rows))

time: 102 us -> 101 us (level)
  blocking collectives: 17.6 us -> 20.8 us
  starting transfers between devices: 26.9 us -> 23.9 us
  Pallas kernels: 45.9 us -> 44.3 us
    all_to_all x1, blocking collectives: 17.6 us -> 20.8 us  [exchange(): lax.all_to_all(chunks, ('zt', 'xy'), 0, 0, axis_index_groups=groups(), ti...]
    ppermute x12, starting transfers between devices: 16.5 us -> 13.6 us  [pairs(): return lax.ppermute(plane, axis, swaps)]
    pallas_call x3, Pallas kernels: 18 us -> 16.4 us  [remote(): pl.pallas_call(functools.partial(remote_kernel, last), in_specs=vmem(7),...]
  transfers between devices with their start and end apart: 13 -> 13, of which waited for: 1 -> 2; matrix products, arithmetic and copies ran while one was open for 0% -> 0% of each run, Pallas kernels for 24% -> 25%
where the time goes in v6:
time: 101 us
  Pallas kernels  44.3 us (44%)
  starting transfers between devices  23.9 us (24%)
  blocking collectives  20.8 us (21%)
  waiting for transfers between devices  11 us (11%)
    pallas_call x3, Pallas kernels, local(): pl.pallas_call(functools.partial(local_kernel, first), in_specs=(hbm(2) i...  23.2 us
    all_to_all x1, blocking collectives, exchange(): lax.all_to_all(chunks, ('zt', 'xy'), 0, 0, axis_index_groups=groups(), ti...  20.8 us
    pallas_call x3, Pallas kernels, remote(): pl.pallas_call(functools.partial(remote_kernel, last), in_specs=vmem(7),...  16.4 us
    ppermute x12, starting transfers between devices, pairs(): return lax.ppermute(plane, axis, swaps)  13.6 us
    all_to_all x1, waiting for transfers between devices, exchange(): lax.all_to_all(chunks, ('zt', 'xy'), 0, 0, axis_index_groups=groups(), ti...  10.7 us
    all_to_all x1, starting transfers between devices, exchange(): lax.all_to_all(chunks, ('zt', 'xy'), 0, 0, axis_index_groups=groups(), ti...  10.4 us
  transfers between devices with their start and end apart: 13, of which 2 were waited for; matrix products, arithmetic and copies ran while one was open for 0% of the time, Pallas kernels for 25%

profile of v6, /device:TPU:1, one launch (start us, length us, event | category | flops | bytes accessed | tf_op | source)
XLA Modules:
  0.0 101.1 jit_solution(13874772247317727245)
XLA Ops:
  0.0 0.9 copy-done
  1.0 1.1 %split.1 = bf16[2,2,8,16,512]{4,3,2,1,0:T(8,128)(2,1)} custom-call(bf16[512,256]{1,0:T(8,128)(2,1)S(1)} %bitcast.12), custom_call_target="tpu_custom_call" | custom-call | tf_op jit(solution)/shard_map/split/pallas_call | solution.py:127
  2.0 10.4 %all-to-all-start = ((bf16[32,16,512]{2,1,0:T(8,128)(2,1)}), bf16[32,16,512]{2,1,0:T(8,128)(2,1)S(1)}, u32[]{:S(2)}, u32[]{:S(2)}) async-start(bf16[32,16,512]{2,1,0:T(8,128)(2,1)} %bitcast.3), calls=%async_computation | async-start | bytes 1048576 | tf_op jit(solution)/shard_map/all_to_all | solution.py:372
  12.4 1.8 %prepare.1 = (bf16[64,64,256]{2,1,0:T(8,128)(2,1)S(1)}, f32[64,256]{1,0:T(8,128)S(1)}) custom-call(bf16[9,64,64,256]{3,2,1,0:T(8,128)(2,1)} %bitcast.13), custom_call_target="tpu_custom_call" | custom-call | flops 10000000 | bytes 4194304 | tf_op jit(solution)/shard_map/prepare/pallas_call | solution.py:92
  14.2 10.7 %all-to-all-done = bf16[32,16,512]{2,1,0:T(8,128)(2,1)S(1)} async-done(((bf16[32,16,512]{2,1,0:T(8,128)(2,1)}), bf16[32,16,512]{2,1,0:T(8,128)(2,1)S(1)}, u32[]{:S(2)}, u32[]{:S(2)}) %all-to-all-start) | async-done | bytes 524320 | tf_op jit(solution)/shard_map/all_to_all | solution.py:372
  24.9 0.4 start.1
  25.3 0.6 collective-permute-start
  25.9 2.7 %collective-permute-start.1 = (bf16[8,64,256]{2,1,0:T(8,128)(2,1)S(1)}, bf16[8,64,256]{2,1,0:T(8,128)(2,1)S(1)}, u32[]{:S(2)}, u32[]{:S(2)}) collective-permute-start(bf16[8,64,256]{2,1,0:T(8,128)(2,1)S(1)} %get-tuple-element.21.refs_4_), channel_id=1, source_target_pairs={{16,32},{32,16},{48,64},{64,48},{80,96},{96,80},{112,0},{0,112},{1... | collective-permute-start | bytes 786440 | tf_op jit(solution)/shard_map/ppermute | solution.py:363
  28.6 0.8 collective-permute-start.2
  29.4 0.2 collective-permute-start.3
  29.6 8.6 %local.3 = (f32[8,64,256]{2,1,0:T(8,128)S(1)}, bf16[5,64,64,256]{3,2,1,0:T(8,128)(2,1)S(1)}, bf16[4,64,64,256]{3,2,1,0:T(8,128)(2,1)S(1)}) custom-call(bf16[1,64,64,256]{3,2,1,0:T(8,128)(2,1)S(1)} %bitcast.11, bf16[9,64,64,256]{3,2,1,0:T(8,128)(2,1)} %bitcast.14, bf16[8,64,256]{2,1,0:T(8,128)(2,1)S(1)} %get-tuple-element.19.refs_2_.refs_1_, ...), custom_call_target="tpu_custom_call" | custom-call | flops 1000000000 | bytes 12582912 | tf_op jit(solution)/shard_map/local/pallas_call | solution.py:303
  38.2 5.5 %remote.3 = (f32[8,64,256]{2,1,0:T(8,128)S(1)}, bf16[8,64,256]{2,1,0:T(8,128)(2,1)S(1)}) custom-call(bf16[4,64,64,256]{3,2,1,0:T(8,128)(2,1)S(1)} %get-tuple-element.22.refs_0_, bf16[8,64,256]{2,1,0:T(8,128)(2,1)S(1)} %collective-permute-done.refs_1_, bf16[8,64,256]{2,1,0:T(8,128)(2,1)S(1)} %collective-permute-done.1.refs_2_, ...), custom_call_target="tpu_custom_call" | custom-call | flops 1000000000 | bytes 12582912 | tf_op jit(solution)/shard_map/remote/pallas_call | solution.py:345
  43.8 2.4 %collective-permute-start.5 = (bf16[8,64,256]{2,1,0:T(8,128)(2,1)S(1)}, bf16[8,64,256]{2,1,0:T(8,128)(2,1)S(1)}, u32[]{:S(2)}, u32[]{:S(2)}) collective-permute-start(bf16[8,64,256]{2,1,0:T(8,128)(2,1)S(1)} %get-tuple-element.24.refs_3_), channel_id=1, source_target_pairs={{16,32},{32,16},{48,64},{64,48},{80,96},{96,80},{112,0},{0,112},{1... | collective-permute-start | bytes 786440 | tf_op jit(solution)/shard_map/ppermute | solution.py:363
  46.2 2.0 %collective-permute-start.6 = (bf16[8,64,256]{2,1,0:T(8,128)(2,1)S(1)}, bf16[8,64,256]{2,1,0:T(8,128)(2,1)S(1)}, u32[]{:S(2)}, u32[]{:S(2)}) collective-permute-start(bf16[8,64,256]{2,1,0:T(8,128)(2,1)S(1)} %get-tuple-element.24.refs_3_), channel_id=1, source_target_pairs={{0,1},{1,0},{2,3},{3,2},{4,5},{5,4},{6,7},{7,6},{8,9},{9,8},{10,11... | collective-permute-start | bytes 786440 | tf_op jit(solution)/shard_map/ppermute | solution.py:363
  48.1 7.3 %local.4.refs_5_ = f32[8,64,256]{2,1,0:T(8,128)S(1)} custom-call(bf16[5,64,64,256]{3,2,1,0:T(8,128)(2,1)S(1)} %get-tuple-element.25.refs_0_, bf16[8,64,256]{2,1,0:T(8,128)(2,1)S(1)} %get-tuple-element.19.refs_2_.refs_1_, f32[8,64,256]{2,1,0:T(8,128)S(1)} %get-tuple-element.26.refs_2_, bf16[8,64,256]{2,1,0:T(8,128)(2,1)S(1)} %get-tuple-element.24.refs_3_, ...), custom_call_target="tpu_custom_call" | custom-call | flops 1000000000 | bytes 12582912 | tf_op jit(solution)/shard_map/local/pallas_call | solution.py:303
  55.5 5.5 %remote.4 = (f32[8,64,256]{2,1,0:T(8,128)S(1)}, bf16[8,64,256]{2,1,0:T(8,128)(2,1)S(1)}) custom-call(bf16[4,64,64,256]{3,2,1,0:T(8,128)(2,1)S(1)} %get-tuple-element.22.refs_0_, bf16[8,64,256]{2,1,0:T(8,128)(2,1)S(1)} %collective-permute-done.4.refs_1_, bf16[8,64,256]{2,1,0:T(8,128)(2,1)S(1)} %collective-permute-done.5.refs_2_, ...), custom_call_target="tpu_custom_call" | custom-call | flops 1000000000 | bytes 12582912 | tf_op jit(solution)/shard_map/remote/pallas_call | solution.py:345
  61.0 3.0 %collective-permute-start.10 = (bf16[8,64,256]{2,1,0:T(8,128)(2,1)S(1)}, bf16[8,64,256]{2,1,0:T(8,128)(2,1)S(1)}, u32[]{:S(2)}, u32[]{:S(2)}) collective-permute-start(bf16[8,64,256]{2,1,0:T(8,128)(2,1)S(1)} %get-tuple-element.27.refs_3_), channel_id=1, source_target_pairs={{0,1},{1,0},{2,3},{3,2},{4,5},{5,4},{6,7},{7,6},{8,9},{9,8},{10,11... | collective-permute-start | bytes 786440 | tf_op jit(solution)/shard_map/ppermute | solution.py:363
  63.9 1.9 %collective-permute-start.9 = (bf16[8,64,256]{2,1,0:T(8,128)(2,1)S(1)}, bf16[8,64,256]{2,1,0:T(8,128)(2,1)S(1)}, u32[]{:S(2)}, u32[]{:S(2)}) collective-permute-start(bf16[8,64,256]{2,1,0:T(8,128)(2,1)S(1)} %get-tuple-element.27.refs_3_), channel_id=1, source_target_pairs={{16,32},{32,16},{48,64},{64,48},{80,96},{96,80},{112,0},{0,112},{1... | collective-permute-start | bytes 786440 | tf_op jit(solution)/shard_map/ppermute | solution.py:363
  65.9 7.3 %local.5.refs_5_ = f32[8,64,256]{2,1,0:T(8,128)S(1)} custom-call(bf16[5,64,64,256]{3,2,1,0:T(8,128)(2,1)S(1)} %get-tuple-element.25.refs_0_, bf16[8,64,256]{2,1,0:T(8,128)(2,1)S(1)} %get-tuple-element.19.refs_2_.refs_1_, f32[8,64,256]{2,1,0:T(8,128)S(1)} %get-tuple-element.28.refs_2_, bf16[8,64,256]{2,1,0:T(8,128)(2,1)S(1)} %get-tuple-element.27.refs_3_, ...), custom_call_target="tpu_custom_call" | custom-call | flops 1000000000 | bytes 12582912 | tf_op jit(solution)/shard_map/local/pallas_call | solution.py:303
  73.2 0.3 collective-permute-done.9.refs_2_
  73.5 5.4 %remote.5.rounded_ref = bf16[8,64,256]{2,1,0:T(8,128)(2,1)S(1)} custom-call(bf16[4,64,64,256]{3,2,1,0:T(8,128)(2,1)S(1)} %get-tuple-element.22.refs_0_, bf16[8,64,256]{2,1,0:T(8,128)(2,1)S(1)} %collective-permute-done.8.refs_1_, bf16[8,64,256]{2,1,0:T(8,128)(2,1)S(1)} %collective-permute-done.9.refs_2_, ...), custom_call_target="tpu_custom_call" | custom-call | flops 1000000000 | bytes 12582912 | tf_op jit(solution)/shard_map/remote/pallas_call | solution.py:345
  78.9 0.3 leave.1
  79.3 20.8 %all_to_all.10 = bf16[32,16,512]{2,1,0:T(8,128)(2,1)S(1)} all-to-all(bf16[32,16,512]{2,1,0:T(8,128)(2,1)S(1)} %bitcast.9), channel_id=1, replica_groups={{0,1,2,3,4,5,6,7,8,9,10,11,12,13,14,15,16,17,18,19,20,21,22,23,24,25,26..., dimensions={0} | all-to-all | bytes 1048576 | tf_op jit(solution)/shard_map/all_to_all | solution.py:372
  100.1 1.1 %join.1 = f32[512,256]{1,0:T(8,128)} custom-call(bf16[2,2,128,512]{3,2,1,0:T(8,128)(2,1)S(1)} %bitcast.10), custom_call_target="tpu_custom_call" | custom-call | tf_op jit(solution)/shard_map/join/pallas_call | solution.py:207
  (16 shorter events, 0.1 us)
Async XLA Ops:
  0.0 0.9 copy-start
  2.0 22.9 %all-to-all-start = ((bf16[32,16,512]{2,1,0:T(8,128)(2,1)}), bf16[32,16,512]{2,1,0:T(8,128)(2,1)S(1)}, u32[]{:S(2)}, u32[]{:S(2)}) async-start(bf16[32,16,512]{2,1,0:T(8,128)(2,1)} %bitcast.3), calls=%async_computation | async-start | bytes 1048576 | tf_op jit(solution)/shard_map/all_to_all | solution.py:372
  25.3 12.9 %collective-permute-start = (bf16[8,64,256]{2,1,0:T(8,128)(2,1)S(1)}, bf16[8,64,256]{2,1,0:T(8,128)(2,1)S(1)}, u32[]{:S(2)}, u32[]{:S(2)}) collective-permute-start(bf16[8,64,256]{2,1,0:T(8,128)(2,1)S(1)} %get-tuple-element.21.refs_4_), channel_id=1, source_target_pairs={{0,16},{16,0},{32,48},{48,32},{64,80},{80,64},{96,112},{112,96},{1... | collective-permute-start | bytes 786440 | tf_op jit(solution)/shard_map/ppermute | solution.py:363
  25.9 12.3 %collective-permute-start.1 = (bf16[8,64,256]{2,1,0:T(8,128)(2,1)S(1)}, bf16[8,64,256]{2,1,0:T(8,128)(2,1)S(1)}, u32[]{:S(2)}, u32[]{:S(2)}) collective-permute-start(bf16[8,64,256]{2,1,0:T(8,128)(2,1)S(1)} %get-tuple-element.21.refs_4_), channel_id=1, source_target_pairs={{16,32},{32,16},{48,64},{64,48},{80,96},{96,80},{112,0},{0,112},{1... | collective-permute-start | bytes 786440 | tf_op jit(solution)/shard_map/ppermute | solution.py:363
  28.6 9.6 %collective-permute-start.2 = (bf16[8,64,256]{2,1,0:T(8,128)(2,1)S(1)}, bf16[8,64,256]{2,1,0:T(8,128)(2,1)S(1)}, u32[]{:S(2)}, u32[]{:S(2)}) collective-permute-start(bf16[8,64,256]{2,1,0:T(8,128)(2,1)S(1)} %get-tuple-element.21.refs_4_), channel_id=1, source_target_pairs={{0,1},{1,0},{2,3},{3,2},{4,5},{5,4},{6,7},{7,6},{8,9},{9,8},{10,11... | collective-permute-start | bytes 786440 | tf_op jit(solution)/shard_map/ppermute | solution.py:363
  29.4 8.8 %collective-permute-start.3 = (bf16[8,64,256]{2,1,0:T(8,128)(2,1)S(1)}, bf16[8,64,256]{2,1,0:T(8,128)(2,1)S(1)}, u32[]{:S(2)}, u32[]{:S(2)}) collective-permute-start(bf16[8,64,256]{2,1,0:T(8,128)(2,1)S(1)} %get-tuple-element.21.refs_4_), channel_id=1, source_target_pairs={{1,2},{2,1},{3,4},{4,3},{5,6},{6,5},{7,8},{8,7},{9,10},{10,9},{11,... | collective-permute-start | bytes 786440 | tf_op jit(solution)/shard_map/ppermute | solution.py:363
  43.7 11.8 %collective-permute-start.4 = (bf16[8,64,256]{2,1,0:T(8,128)(2,1)S(1)}, bf16[8,64,256]{2,1,0:T(8,128)(2,1)S(1)}, u32[]{:S(2)}, u32[]{:S(2)}) collective-permute-start(bf16[8,64,256]{2,1,0:T(8,128)(2,1)S(1)} %get-tuple-element.24.refs_3_), channel_id=1, source_target_pairs={{0,16},{16,0},{32,48},{48,32},{64,80},{80,64},{96,112},{112,96},{1... | collective-permute-start | bytes 786440 | tf_op jit(solution)/shard_map/ppermute | solution.py:363
  43.8 11.7 %collective-permute-start.5 = (bf16[8,64,256]{2,1,0:T(8,128)(2,1)S(1)}, bf16[8,64,256]{2,1,0:T(8,128)(2,1)S(1)}, u32[]{:S(2)}, u32[]{:S(2)}) collective-permute-start(bf16[8,64,256]{2,1,0:T(8,128)(2,1)S(1)} %get-tuple-element.24.refs_3_), channel_id=1, source_target_pairs={{16,32},{32,16},{48,64},{64,48},{80,96},{96,80},{112,0},{0,112},{1... | collective-permute-start | bytes 786440 | tf_op jit(solution)/shard_map/ppermute | solution.py:363
  46.2 9.3 %collective-permute-start.6 = (bf16[8,64,256]{2,1,0:T(8,128)(2,1)S(1)}, bf16[8,64,256]{2,1,0:T(8,128)(2,1)S(1)}, u32[]{:S(2)}, u32[]{:S(2)}) collective-permute-start(bf16[8,64,256]{2,1,0:T(8,128)(2,1)S(1)} %get-tuple-element.24.refs_3_), channel_id=1, source_target_pairs={{0,1},{1,0},{2,3},{3,2},{4,5},{5,4},{6,7},{7,6},{8,9},{9,8},{10,11... | collective-permute-start | bytes 786440 | tf_op jit(solution)/shard_map/ppermute | solution.py:363
  48.1 7.4 %collective-permute-start.7 = (bf16[8,64,256]{2,1,0:T(8,128)(2,1)S(1)}, bf16[8,64,256]{2,1,0:T(8,128)(2,1)S(1)}, u32[]{:S(2)}, u32[]{:S(2)}) collective-permute-start(bf16[8,64,256]{2,1,0:T(8,128)(2,1)S(1)} %get-tuple-element.24.refs_3_), channel_id=1, source_target_pairs={{1,2},{2,1},{3,4},{4,3},{5,6},{6,5},{7,8},{8,7},{9,10},{10,9},{11,... | collective-permute-start | bytes 786440 | tf_op jit(solution)/shard_map/ppermute | solution.py:363
  61.0 12.2 %collective-permute-start.10 = (bf16[8,64,256]{2,1,0:T(8,128)(2,1)S(1)}, bf16[8,64,256]{2,1,0:T(8,128)(2,1)S(1)}, u32[]{:S(2)}, u32[]{:S(2)}) collective-permute-start(bf16[8,64,256]{2,1,0:T(8,128)(2,1)S(1)} %get-tuple-element.27.refs_3_), channel_id=1, source_target_pairs={{0,1},{1,0},{2,3},{3,2},{4,5},{5,4},{6,7},{7,6},{8,9},{9,8},{10,11... | collective-permute-start | bytes 786440 | tf_op jit(solution)/shard_map/ppermute | solution.py:363
  63.9 9.3 %collective-permute-start.11 = (bf16[8,64,256]{2,1,0:T(8,128)(2,1)S(1)}, bf16[8,64,256]{2,1,0:T(8,128)(2,1)S(1)}, u32[]{:S(2)}, u32[]{:S(2)}) collective-permute-start(bf16[8,64,256]{2,1,0:T(8,128)(2,1)S(1)} %get-tuple-element.27.refs_3_), channel_id=1, source_target_pairs={{1,2},{2,1},{3,4},{4,3},{5,6},{6,5},{7,8},{8,7},{9,10},{10,9},{11,... | collective-permute-start | bytes 786440 | tf_op jit(solution)/shard_map/ppermute | solution.py:363
  63.9 9.3 %collective-permute-start.8 = (bf16[8,64,256]{2,1,0:T(8,128)(2,1)S(1)}, bf16[8,64,256]{2,1,0:T(8,128)(2,1)S(1)}, u32[]{:S(2)}, u32[]{:S(2)}) collective-permute-start(bf16[8,64,256]{2,1,0:T(8,128)(2,1)S(1)} %get-tuple-element.27.refs_3_), channel_id=1, source_target_pairs={{0,16},{16,0},{32,48},{48,32},{64,80},{80,64},{96,112},{112,96},{1... | collective-permute-start | bytes 786440 | tf_op jit(solution)/shard_map/ppermute | solution.py:363
  63.9 9.6 %collective-permute-start.9 = (bf16[8,64,256]{2,1,0:T(8,128)(2,1)S(1)}, bf16[8,64,256]{2,1,0:T(8,128)(2,1)S(1)}, u32[]{:S(2)}, u32[]{:S(2)}) collective-permute-start(bf16[8,64,256]{2,1,0:T(8,128)(2,1)S(1)} %get-tuple-element.27.refs_3_), channel_id=1, source_target_pairs={{16,32},{32,16},{48,64},{64,48},{80,96},{96,80},{112,0},{0,112},{1... | collective-permute-start | bytes 786440 | tf_op jit(solution)/shard_map/ppermute | solution.py:363

commit v7 on v6

--- a/solution.py
+++ b/solution.py
@@ -37,7 +37,7 @@
         if arrive is not None:
             arrive(step)
 
-        @pl.loop(0, ROWS // PAIR, unroll=4)
+        @pl.loop(0, ROWS // PAIR, unroll=8)
         def _(pair):
             row = start + pair * PAIR
             for first in range(0, count, GROUP):

time: 101 us -> 101 us (level)
  no operation moved by 1% of the time
where the time goes in v7:
time: 101 us
  Pallas kernels  43.8 us (43%)
  starting transfers between devices  23.9 us (24%)
  blocking collectives  20.8 us (21%)
  waiting for transfers between devices  11.2 us (11%)
    pallas_call x3, Pallas kernels, local(): pl.pallas_call(functools.partial(local_kernel, first), in_specs=(hbm(2) i...  23 us
    all_to_all x1, blocking collectives, exchange(): lax.all_to_all(chunks, ('zt', 'xy'), 0, 0, axis_index_groups=groups(), ti...  20.8 us
    pallas_call x3, Pallas kernels, remote(): pl.pallas_call(functools.partial(remote_kernel, last), in_specs=vmem(7),...  16.2 us
    ppermute x12, starting transfers between devices, pairs(): return lax.ppermute(plane, axis, swaps)  13.6 us
    all_to_all x1, waiting for transfers between devices, exchange(): lax.all_to_all(chunks, ('zt', 'xy'), 0, 0, axis_index_groups=groups(), ti...  10.7 us
    all_to_all x1, starting transfers between devices, exchange(): lax.all_to_all(chunks, ('zt', 'xy'), 0, 0, axis_index_groups=groups(), ti...  10.4 us
  transfers between devices with their start and end apart: 13, of which 2 were waited for; matrix products, arithmetic and copies ran while one was open for 0% of the time, Pallas kernels for 25%

profile of v7, /device:TPU:1, one launch (start us, length us, event | category | flops | bytes accessed | tf_op | source)
XLA Modules:
  0.0 100.8 jit_solution(8302382933500012052)
XLA Ops:
  0.0 0.9 copy-done
  1.0 1.1 %split.1 = bf16[2,2,8,16,512]{4,3,2,1,0:T(8,128)(2,1)} custom-call(bf16[512,256]{1,0:T(8,128)(2,1)S(1)} %bitcast.12), custom_call_target="tpu_custom_call" | custom-call | tf_op jit(solution)/shard_map/split/pallas_call | solution.py:127
  2.0 10.4 %all-to-all-start = ((bf16[32,16,512]{2,1,0:T(8,128)(2,1)}), bf16[32,16,512]{2,1,0:T(8,128)(2,1)S(1)}, u32[]{:S(2)}, u32[]{:S(2)}) async-start(bf16[32,16,512]{2,1,0:T(8,128)(2,1)} %bitcast.3), calls=%async_computation | async-start | bytes 1048576 | tf_op jit(solution)/shard_map/all_to_all | solution.py:372
  12.4 1.8 %prepare.1 = (bf16[64,64,256]{2,1,0:T(8,128)(2,1)S(1)}, f32[64,256]{1,0:T(8,128)S(1)}) custom-call(bf16[9,64,64,256]{3,2,1,0:T(8,128)(2,1)} %bitcast.13), custom_call_target="tpu_custom_call" | custom-call | flops 10000000 | bytes 4194304 | tf_op jit(solution)/shard_map/prepare/pallas_call | solution.py:92
  14.2 10.7 %all-to-all-done = bf16[32,16,512]{2,1,0:T(8,128)(2,1)S(1)} async-done(((bf16[32,16,512]{2,1,0:T(8,128)(2,1)}), bf16[32,16,512]{2,1,0:T(8,128)(2,1)S(1)}, u32[]{:S(2)}, u32[]{:S(2)}) %all-to-all-start) | async-done | bytes 524320 | tf_op jit(solution)/shard_map/all_to_all | solution.py:372
  24.9 0.4 start.1
  25.3 0.6 collective-permute-start
  25.9 2.7 %collective-permute-start.1 = (bf16[8,64,256]{2,1,0:T(8,128)(2,1)S(1)}, bf16[8,64,256]{2,1,0:T(8,128)(2,1)S(1)}, u32[]{:S(2)}, u32[]{:S(2)}) collective-permute-start(bf16[8,64,256]{2,1,0:T(8,128)(2,1)S(1)} %get-tuple-element.21.refs_4_), channel_id=1, source_target_pairs={{16,32},{32,16},{48,64},{64,48},{80,96},{96,80},{112,0},{0,112},{1... | collective-permute-start | bytes 786440 | tf_op jit(solution)/shard_map/ppermute | solution.py:363
  28.6 0.8 collective-permute-start.2
  29.4 0.2 collective-permute-start.3
  29.6 8.5 %local.3 = (f32[8,64,256]{2,1,0:T(8,128)S(1)}, bf16[5,64,64,256]{3,2,1,0:T(8,128)(2,1)S(1)}, bf16[4,64,64,256]{3,2,1,0:T(8,128)(2,1)S(1)}) custom-call(bf16[1,64,64,256]{3,2,1,0:T(8,128)(2,1)S(1)} %bitcast.11, bf16[9,64,64,256]{3,2,1,0:T(8,128)(2,1)} %bitcast.14, bf16[8,64,256]{2,1,0:T(8,128)(2,1)S(1)} %get-tuple-element.19.refs_2_.refs_1_, ...), custom_call_target="tpu_custom_call" | custom-call | flops 1000000000 | bytes 12582912 | tf_op jit(solution)/shard_map/local/pallas_call | solution.py:303
  38.1 5.4 %remote.3 = (f32[8,64,256]{2,1,0:T(8,128)S(1)}, bf16[8,64,256]{2,1,0:T(8,128)(2,1)S(1)}) custom-call(bf16[4,64,64,256]{3,2,1,0:T(8,128)(2,1)S(1)} %get-tuple-element.22.refs_0_, bf16[8,64,256]{2,1,0:T(8,128)(2,1)S(1)} %collective-permute-done.refs_1_, bf16[8,64,256]{2,1,0:T(8,128)(2,1)S(1)} %collective-permute-done.1.refs_2_, ...), custom_call_target="tpu_custom_call" | custom-call | flops 1000000000 | bytes 12582912 | tf_op jit(solution)/shard_map/remote/pallas_call | solution.py:345
  43.6 2.5 %collective-permute-start.5 = (bf16[8,64,256]{2,1,0:T(8,128)(2,1)S(1)}, bf16[8,64,256]{2,1,0:T(8,128)(2,1)S(1)}, u32[]{:S(2)}, u32[]{:S(2)}) collective-permute-start(bf16[8,64,256]{2,1,0:T(8,128)(2,1)S(1)} %get-tuple-element.24.refs_3_), channel_id=1, source_target_pairs={{16,32},{32,16},{48,64},{64,48},{80,96},{96,80},{112,0},{0,112},{1... | collective-permute-start | bytes 786440 | tf_op jit(solution)/shard_map/ppermute | solution.py:363
  46.1 2.0 %collective-permute-start.6 = (bf16[8,64,256]{2,1,0:T(8,128)(2,1)S(1)}, bf16[8,64,256]{2,1,0:T(8,128)(2,1)S(1)}, u32[]{:S(2)}, u32[]{:S(2)}) collective-permute-start(bf16[8,64,256]{2,1,0:T(8,128)(2,1)S(1)} %get-tuple-element.24.refs_3_), channel_id=1, source_target_pairs={{0,1},{1,0},{2,3},{3,2},{4,5},{5,4},{6,7},{7,6},{8,9},{9,8},{10,11... | collective-permute-start | bytes 786440 | tf_op jit(solution)/shard_map/ppermute | solution.py:363
  48.1 7.2 %local.4.refs_5_ = f32[8,64,256]{2,1,0:T(8,128)S(1)} custom-call(bf16[5,64,64,256]{3,2,1,0:T(8,128)(2,1)S(1)} %get-tuple-element.25.refs_0_, bf16[8,64,256]{2,1,0:T(8,128)(2,1)S(1)} %get-tuple-element.19.refs_2_.refs_1_, f32[8,64,256]{2,1,0:T(8,128)S(1)} %get-tuple-element.26.refs_2_, bf16[8,64,256]{2,1,0:T(8,128)(2,1)S(1)} %get-tuple-element.24.refs_3_, ...), custom_call_target="tpu_custom_call" | custom-call | flops 1000000000 | bytes 12582912 | tf_op jit(solution)/shard_map/local/pallas_call | solution.py:303
  55.3 5.4 %remote.4 = (f32[8,64,256]{2,1,0:T(8,128)S(1)}, bf16[8,64,256]{2,1,0:T(8,128)(2,1)S(1)}) custom-call(bf16[4,64,64,256]{3,2,1,0:T(8,128)(2,1)S(1)} %get-tuple-element.22.refs_0_, bf16[8,64,256]{2,1,0:T(8,128)(2,1)S(1)} %collective-permute-done.4.refs_1_, bf16[8,64,256]{2,1,0:T(8,128)(2,1)S(1)} %collective-permute-done.5.refs_2_, ...), custom_call_target="tpu_custom_call" | custom-call | flops 1000000000 | bytes 12582912 | tf_op jit(solution)/shard_map/remote/pallas_call | solution.py:345
  60.7 3.0 %collective-permute-start.10 = (bf16[8,64,256]{2,1,0:T(8,128)(2,1)S(1)}, bf16[8,64,256]{2,1,0:T(8,128)(2,1)S(1)}, u32[]{:S(2)}, u32[]{:S(2)}) collective-permute-start(bf16[8,64,256]{2,1,0:T(8,128)(2,1)S(1)} %get-tuple-element.27.refs_3_), channel_id=1, source_target_pairs={{0,1},{1,0},{2,3},{3,2},{4,5},{5,4},{6,7},{7,6},{8,9},{9,8},{10,11... | collective-permute-start | bytes 786440 | tf_op jit(solution)/shard_map/ppermute | solution.py:363
  63.7 1.8 %collective-permute-start.9 = (bf16[8,64,256]{2,1,0:T(8,128)(2,1)S(1)}, bf16[8,64,256]{2,1,0:T(8,128)(2,1)S(1)}, u32[]{:S(2)}, u32[]{:S(2)}) collective-permute-start(bf16[8,64,256]{2,1,0:T(8,128)(2,1)S(1)} %get-tuple-element.27.refs_3_), channel_id=1, source_target_pairs={{16,32},{32,16},{48,64},{64,48},{80,96},{96,80},{112,0},{0,112},{1... | collective-permute-start | bytes 786440 | tf_op jit(solution)/shard_map/ppermute | solution.py:363
  65.6 7.2 %local.5.refs_5_ = f32[8,64,256]{2,1,0:T(8,128)S(1)} custom-call(bf16[5,64,64,256]{3,2,1,0:T(8,128)(2,1)S(1)} %get-tuple-element.25.refs_0_, bf16[8,64,256]{2,1,0:T(8,128)(2,1)S(1)} %get-tuple-element.19.refs_2_.refs_1_, f32[8,64,256]{2,1,0:T(8,128)S(1)} %get-tuple-element.28.refs_2_, bf16[8,64,256]{2,1,0:T(8,128)(2,1)S(1)} %get-tuple-element.27.refs_3_, ...), custom_call_target="tpu_custom_call" | custom-call | flops 1000000000 | bytes 12582912 | tf_op jit(solution)/shard_map/local/pallas_call | solution.py:303
  72.8 0.4 collective-permute-done.9.refs_2_
  73.3 5.3 %remote.5.rounded_ref = bf16[8,64,256]{2,1,0:T(8,128)(2,1)S(1)} custom-call(bf16[4,64,64,256]{3,2,1,0:T(8,128)(2,1)S(1)} %get-tuple-element.22.refs_0_, bf16[8,64,256]{2,1,0:T(8,128)(2,1)S(1)} %collective-permute-done.8.refs_1_, bf16[8,64,256]{2,1,0:T(8,128)(2,1)S(1)} %collective-permute-done.9.refs_2_, ...), custom_call_target="tpu_custom_call" | custom-call | flops 1000000000 | bytes 12582912 | tf_op jit(solution)/shard_map/remote/pallas_call | solution.py:345
  78.6 0.3 leave.1
  79.0 20.8 %all_to_all.10 = bf16[32,16,512]{2,1,0:T(8,128)(2,1)S(1)} all-to-all(bf16[32,16,512]{2,1,0:T(8,128)(2,1)S(1)} %bitcast.9), channel_id=1, replica_groups={{0,1,2,3,4,5,6,7,8,9,10,11,12,13,14,15,16,17,18,19,20,21,22,23,24,25,26..., dimensions={0} | all-to-all | bytes 1048576 | tf_op jit(solution)/shard_map/all_to_all | solution.py:372
  99.8 1.1 %join.1 = f32[512,256]{1,0:T(8,128)} custom-call(bf16[2,2,128,512]{3,2,1,0:T(8,128)(2,1)S(1)} %bitcast.10), custom_call_target="tpu_custom_call" | custom-call | tf_op jit(solution)/shard_map/join/pallas_call | solution.py:207
  (16 shorter events, 0.1 us)
Async XLA Ops:
  0.0 0.9 copy-start
  2.0 22.9 %all-to-all-start = ((bf16[32,16,512]{2,1,0:T(8,128)(2,1)}), bf16[32,16,512]{2,1,0:T(8,128)(2,1)S(1)}, u32[]{:S(2)}, u32[]{:S(2)}) async-start(bf16[32,16,512]{2,1,0:T(8,128)(2,1)} %bitcast.3), calls=%async_computation | async-start | bytes 1048576 | tf_op jit(solution)/shard_map/all_to_all | solution.py:372
  25.3 12.8 %collective-permute-start = (bf16[8,64,256]{2,1,0:T(8,128)(2,1)S(1)}, bf16[8,64,256]{2,1,0:T(8,128)(2,1)S(1)}, u32[]{:S(2)}, u32[]{:S(2)}) collective-permute-start(bf16[8,64,256]{2,1,0:T(8,128)(2,1)S(1)} %get-tuple-element.21.refs_4_), channel_id=1, source_target_pairs={{0,16},{16,0},{32,48},{48,32},{64,80},{80,64},{96,112},{112,96},{1... | collective-permute-start | bytes 786440 | tf_op jit(solution)/shard_map/ppermute | solution.py:363
  25.9 12.2 %collective-permute-start.1 = (bf16[8,64,256]{2,1,0:T(8,128)(2,1)S(1)}, bf16[8,64,256]{2,1,0:T(8,128)(2,1)S(1)}, u32[]{:S(2)}, u32[]{:S(2)}) collective-permute-start(bf16[8,64,256]{2,1,0:T(8,128)(2,1)S(1)} %get-tuple-element.21.refs_4_), channel_id=1, source_target_pairs={{16,32},{32,16},{48,64},{64,48},{80,96},{96,80},{112,0},{0,112},{1... | collective-permute-start | bytes 786440 | tf_op jit(solution)/shard_map/ppermute | solution.py:363
  28.6 9.5 %collective-permute-start.2 = (bf16[8,64,256]{2,1,0:T(8,128)(2,1)S(1)}, bf16[8,64,256]{2,1,0:T(8,128)(2,1)S(1)}, u32[]{:S(2)}, u32[]{:S(2)}) collective-permute-start(bf16[8,64,256]{2,1,0:T(8,128)(2,1)S(1)} %get-tuple-element.21.refs_4_), channel_id=1, source_target_pairs={{0,1},{1,0},{2,3},{3,2},{4,5},{5,4},{6,7},{7,6},{8,9},{9,8},{10,11... | collective-permute-start | bytes 786440 | tf_op jit(solution)/shard_map/ppermute | solution.py:363
  29.4 8.7 %collective-permute-start.3 = (bf16[8,64,256]{2,1,0:T(8,128)(2,1)S(1)}, bf16[8,64,256]{2,1,0:T(8,128)(2,1)S(1)}, u32[]{:S(2)}, u32[]{:S(2)}) collective-permute-start(bf16[8,64,256]{2,1,0:T(8,128)(2,1)S(1)} %get-tuple-element.21.refs_4_), channel_id=1, source_target_pairs={{1,2},{2,1},{3,4},{4,3},{5,6},{6,5},{7,8},{8,7},{9,10},{10,9},{11,... | collective-permute-start | bytes 786440 | tf_op jit(solution)/shard_map/ppermute | solution.py:363
  43.5 11.8 %collective-permute-start.4 = (bf16[8,64,256]{2,1,0:T(8,128)(2,1)S(1)}, bf16[8,64,256]{2,1,0:T(8,128)(2,1)S(1)}, u32[]{:S(2)}, u32[]{:S(2)}) collective-permute-start(bf16[8,64,256]{2,1,0:T(8,128)(2,1)S(1)} %get-tuple-element.24.refs_3_), channel_id=1, source_target_pairs={{0,16},{16,0},{32,48},{48,32},{64,80},{80,64},{96,112},{112,96},{1... | collective-permute-start | bytes 786440 | tf_op jit(solution)/shard_map/ppermute | solution.py:363
  43.6 11.7 %collective-permute-start.5 = (bf16[8,64,256]{2,1,0:T(8,128)(2,1)S(1)}, bf16[8,64,256]{2,1,0:T(8,128)(2,1)S(1)}, u32[]{:S(2)}, u32[]{:S(2)}) collective-permute-start(bf16[8,64,256]{2,1,0:T(8,128)(2,1)S(1)} %get-tuple-element.24.refs_3_), channel_id=1, source_target_pairs={{16,32},{32,16},{48,64},{64,48},{80,96},{96,80},{112,0},{0,112},{1... | collective-permute-start | bytes 786440 | tf_op jit(solution)/shard_map/ppermute | solution.py:363
  46.1 9.2 %collective-permute-start.6 = (bf16[8,64,256]{2,1,0:T(8,128)(2,1)S(1)}, bf16[8,64,256]{2,1,0:T(8,128)(2,1)S(1)}, u32[]{:S(2)}, u32[]{:S(2)}) collective-permute-start(bf16[8,64,256]{2,1,0:T(8,128)(2,1)S(1)} %get-tuple-element.24.refs_3_), channel_id=1, source_target_pairs={{0,1},{1,0},{2,3},{3,2},{4,5},{5,4},{6,7},{7,6},{8,9},{9,8},{10,11... | collective-permute-start | bytes 786440 | tf_op jit(solution)/shard_map/ppermute | solution.py:363
  48.1 7.3 %collective-permute-start.7 = (bf16[8,64,256]{2,1,0:T(8,128)(2,1)S(1)}, bf16[8,64,256]{2,1,0:T(8,128)(2,1)S(1)}, u32[]{:S(2)}, u32[]{:S(2)}) collective-permute-start(bf16[8,64,256]{2,1,0:T(8,128)(2,1)S(1)} %get-tuple-element.24.refs_3_), channel_id=1, source_target_pairs={{1,2},{2,1},{3,4},{4,3},{5,6},{6,5},{7,8},{8,7},{9,10},{10,9},{11,... | collective-permute-start | bytes 786440 | tf_op jit(solution)/shard_map/ppermute | solution.py:363
  60.7 12.1 %collective-permute-start.10 = (bf16[8,64,256]{2,1,0:T(8,128)(2,1)S(1)}, bf16[8,64,256]{2,1,0:T(8,128)(2,1)S(1)}, u32[]{:S(2)}, u32[]{:S(2)}) collective-permute-start(bf16[8,64,256]{2,1,0:T(8,128)(2,1)S(1)} %get-tuple-element.27.refs_3_), channel_id=1, source_target_pairs={{0,1},{1,0},{2,3},{3,2},{4,5},{5,4},{6,7},{7,6},{8,9},{9,8},{10,11... | collective-permute-start | bytes 786440 | tf_op jit(solution)/shard_map/ppermute | solution.py:363
  63.7 9.1 %collective-permute-start.11 = (bf16[8,64,256]{2,1,0:T(8,128)(2,1)S(1)}, bf16[8,64,256]{2,1,0:T(8,128)(2,1)S(1)}, u32[]{:S(2)}, u32[]{:S(2)}) collective-permute-start(bf16[8,64,256]{2,1,0:T(8,128)(2,1)S(1)} %get-tuple-element.27.refs_3_), channel_id=1, source_target_pairs={{1,2},{2,1},{3,4},{4,3},{5,6},{6,5},{7,8},{8,7},{9,10},{10,9},{11,... | collective-permute-start | bytes 786440 | tf_op jit(solution)/shard_map/ppermute | solution.py:363
  63.7 9.1 %collective-permute-start.8 = (bf16[8,64,256]{2,1,0:T(8,128)(2,1)S(1)}, bf16[8,64,256]{2,1,0:T(8,128)(2,1)S(1)}, u32[]{:S(2)}, u32[]{:S(2)}) collective-permute-start(bf16[8,64,256]{2,1,0:T(8,128)(2,1)S(1)} %get-tuple-element.27.refs_3_), channel_id=1, source_target_pairs={{0,16},{16,0},{32,48},{48,32},{64,80},{80,64},{96,112},{112,96},{1... | collective-permute-start | bytes 786440 | tf_op jit(solution)/shard_map/ppermute | solution.py:363
  63.7 9.6 %collective-permute-start.9 = (bf16[8,64,256]{2,1,0:T(8,128)(2,1)S(1)}, bf16[8,64,256]{2,1,0:T(8,128)(2,1)S(1)}, u32[]{:S(2)}, u32[]{:S(2)}) collective-permute-start(bf16[8,64,256]{2,1,0:T(8,128)(2,1)S(1)} %get-tuple-element.27.refs_3_), channel_id=1, source_target_pairs={{16,32},{32,16},{48,64},{64,48},{80,96},{96,80},{112,0},{0,112},{1... | collective-permute-start | bytes 786440 | tf_op jit(solution)/shard_map/ppermute | solution.py:363
